TPU v7x, 128 devices: a whole 4x4x4 slice. The times are simulated.
128 devices in a mesh: blk: 32 (over x_lo, z, y), chan: 4 (over x_hi, core).
Axes of the slice: x: 4 (x_hi: 2, x_lo: 2; x = x_hi * 2 + x_lo), y: 4, z: 4, core: 2. Of those that a mesh axis runs over, the one named last changes fastest.
Arguments:
- pair_rep: bfloat16 [512, 512, 128], P('blk'), may hold values from -6 to 6
- proj_weight: bfloat16 [2, 4, 128, 128], P(None, None, None, 'chan'), may hold values from -0.5 to 0.5
- gate_weight: bfloat16 [2, 128, 128], replicated, may hold values from -0.5 to 0.5
- out_weight: bfloat16 [2, 128, 128], P(None, 'chan'), may hold values from -0.5 to 0.5
- in_gain: float32 [2, 128], replicated, may hold values from 0.1 to 1.9
- out_gain: float32 [2, 128], P(None, 'chan'), may hold values from 0.1 to 1.9
Outputs:
- pair_out: bfloat16 [512, 512, 128], P('blk', 'chan')
All inputs are finite; a program needn't handle non-finite values.
Results may differ from a plain program's by a relative error of at most 0.02.
Values may be sent and summed in bfloat16 or wider, within the bound.
No kernel may reach another device: no remote copies, remote signals or barrier semaphores. Data moves between devices by JAX's collectives and lax.ppermute only.
A program may use at most 128 MiB of HBM per device.

v0:
```python
import jax
import jax.numpy as jnp
from jax import lax
from jax.sharding import PartitionSpec as P

HIDDEN_SIZE = 128


epsilon = 1e-05


def cell_norm(values, gain):
    mean = jnp.mean(values, -1, keepdims=True)
    square = jnp.mean(values * values, -1, keepdims=True)
    return (values - mean) * lax.rsqrt(square - mean * mean + epsilon) * gain


def halves(normed, weights):
    parts = jnp.einsum("ikz,qzc->qcik", normed, weights, preferred_element_type=jnp.float32)
    left_part = (parts[0] * jax.nn.sigmoid(parts[1])).astype(jnp.bfloat16)
    right_part = (parts[2] * jax.nn.sigmoid(parts[3])).astype(jnp.bfloat16)
    return (left_part, right_part)


def gates(normed, weights):
    return jax.nn.sigmoid(
        jnp.einsum("ijz,zy->ijy", normed, weights, preferred_element_type=jnp.float32)
    )


def hidden_norm(product, out_gain):
    total_sum, total_square = (
        lax.psum(jnp.sum(product, 0).astype(jnp.bfloat16), "chan").astype(jnp.float32),
        lax.psum(jnp.sum(product * product, 0).astype(jnp.bfloat16), "chan").astype(jnp.float32),
    )
    mean = total_sum / HIDDEN_SIZE
    square = total_square / HIDDEN_SIZE
    scale_inv = lax.rsqrt(square - mean * mean + epsilon)
    return ((product - mean) * scale_inv * out_gain[:, None, None]).astype(jnp.bfloat16)


def project_out(hidden_n, weights):
    return jnp.einsum("cij,cz->ijz", hidden_n, weights, preferred_element_type=jnp.float32)


def block_product(left_turned, block_rows):
    return jnp.einsum("cki,ckj->cij", left_turned, block_rows, preferred_element_type=jnp.float32)


def on_device(pair_rep, proj_weight, gate_weight, out_weight, in_gain, out_gain):
    col_count = pair_rep.shape[1] // lax.axis_size("chan")
    col_start = lax.axis_index("chan") * col_count
    normed = cell_norm(pair_rep.astype(jnp.float32), in_gain[0]).astype(jnp.bfloat16)
    left_out, right_out = halves(normed, proj_weight[0])
    gating = gates(normed, gate_weight[0])
    product = jnp.einsum(
        "cik,cjk->cij",
        left_out,
        lax.all_gather(right_out, "blk", axis=1, tiled=True),
        preferred_element_type=jnp.float32,
    )
    hidden_out = hidden_norm(product, out_gain[0])
    update = lax.psum(project_out(hidden_out, out_weight[0]).astype(jnp.bfloat16), "chan").astype(
        jnp.float32
    )
    middle = (pair_rep.astype(jnp.float32) + gating * update).astype(jnp.bfloat16)
    normed_mid = cell_norm(middle.astype(jnp.float32), in_gain[1]).astype(jnp.bfloat16)
    gating_mid = gates(normed_mid, gate_weight[1])
    turned = lax.all_to_all(middle, "blk", split_axis=1, concat_axis=0, tiled=True)
    normed_turn = cell_norm(turned.astype(jnp.float32), in_gain[1]).astype(jnp.bfloat16)
    left_turned, right_turned = halves(normed_turn, proj_weight[1])
    product_in = block_product(left_turned, lax.all_gather(right_turned, "blk", axis=2, tiled=True))
    hidden_in = hidden_norm(product_in, out_gain[1])
    share_last = lax.psum_scatter(
        project_out(hidden_in, out_weight[1]).astype(jnp.bfloat16),
        "chan",
        scatter_dimension=1,
        tiled=True,
    ).astype(jnp.float32)
    own_mid = lax.dynamic_slice_in_dim(middle, col_start, col_count, 1).astype(jnp.float32)
    own_gate_mid = lax.dynamic_slice_in_dim(gating_mid, col_start, col_count, 1)
    return (own_mid + own_gate_mid * share_last).astype(jnp.bfloat16)


def solution(mesh):
    placed = (
        P("blk", None, None),
        P(None, None, None, "chan"),
        P(),
        P(None, "chan", None),
        P(),
        P(None, "chan"),
    )
    return jax.shard_map(
        on_device, mesh=mesh, in_specs=placed, out_specs=P("blk", "chan", None), check_vma=False
    )
```

profile of v0, /device:TPU:1, one launch (start us, length us, event | category | flops | bytes accessed | tf_op | source)
XLA Modules:
  0.0 643.3 jit_solution(3746611839745580955)
XLA Ops:
  6.5 0.0 copy-start.1
  6.5 0.0 all-gather.5.cloned.1.call-start
  6.5 0.8 slice_bitcast_fusion.3
  7.3 2.9 copy.57
  10.2 0.6 convert_reduce_fusion
  10.8 0.0 copy-done.1
  10.8 0.9 convolution_bitcast_fusion.1
  11.8 0.0 copy-start.4
  11.8 1.6 fusion.61
  13.4 0.0 all-gather.5.cloned.1.call-update
  13.4 0.0 all-reduce.4.cloned.1.call-start
  13.4 0.0 copy-done.4
  13.4 190.9 %all-gather.5.cloned.1.call-done = bf16[1,32,512,512]{3,1,0,2:T(8,128)(2,1)} async-done(((bf16[1,32,16,512]{3,1,0,2:T(8,128)(2,1)}), bf16[1,32,512,512]{3,1,0,2:T(8,128)(2,1)}) %all-gather.5.cloned.1.call-update) | async-done | bytes 16777232 | tf_op jit(solution)/shard_map/all_gather | solution.py:59
  204.4 0.0 copy-start.3
  204.4 17.6 %fusion.75 = (bf16[16,512]{1,0:T(8,128)(2,1)S(1)}, bf16[16,512]{1,0:T(8,128)(2,1)S(1)}, f32[32,16,512]{2,1,0:T(8,128)S(1)}) fusion(bf16[1,32,512,512]{3,1,0,2:T(8,128)(2,1)} %all-gather.5.cloned.1.call-done, bf16[32,16,512]{2,0,1:T(8,128)(2,1)} %get-tuple-element.21), kind=kOutput, calls=%fused_computation.108 | convolution fusion | flops 269205504 | bytes 18382848 | tf_op jit(solution)/shard_map/cik,cjk->cij/dot_general | solution.py:56
  222.0 0.0 copy-start.2
  222.0 19.0 %all-reduce.1 = (bf16[16,512]{1,0:T(8,128)(2,1)S(1)}, bf16[16,512]{1,0:T(8,128)(2,1)S(1)}) all-reduce(bf16[16,512]{1,0:T(8,128)(2,1)S(1)} %get-tuple-element.14, bf16[16,512]{1,0:T(8,128)(2,1)S(1)} %get-tuple-element.13), channel_id=1, replica_groups=mesh['blk'=32,'chan'=4] {'chan'}, use_global_device_ids=true, to_apply=%region_5.0 | all-reduce | flops 16384 | bytes 65536 | tf_op jit(solution)/shard_map/psum | solution.py:34
  241.0 0.1 multiply_convert_fusion.1
  241.1 0.0 copy-done.3
  241.1 2.1 convolution_convert_fusion.1
  243.2 0.0 all-reduce.4.cloned.1.call-update
  243.2 0.2 all-gather.7.cloned.1.call-start
  243.5 57.7 %all-reduce.4.cloned.1.call-done = bf16[16,512,128]{1,2,0:T(8,128)(2,1)} async-done(((bf16[16,512,128]{1,2,0:T(8,128)(2,1)}), bf16[16,512,128]{1,2,0:T(8,128)(2,1)}) %all-reduce.4.cloned.1.call-update) | async-done | bytes 2097168 | tf_op jit(solution)/shard_map/psum | solution.py:63
  301.1 0.0 copy-done.2
  301.1 4.8 convert_reduce_fusion.1
  306.0 3.4 copy.67
  309.4 33.2 %all_to_all.4 = bf16[16,512,128]{2,0,1:T(8,128)(2,1)S(1)} all-to-all(bf16[16,512,128]{2,0,1:T(8,128)(2,1)S(1)} %copy.67), channel_id=1, replica_groups=mesh['blk'=32,'chan'=4] {'blk'}, dimensions={1} | all-to-all | bytes 4194304 | tf_op jit(solution)/shard_map/all_to_all | solution.py:69
  342.6 0.5 copy.68
  343.2 2.2 fusion.16
  345.4 0.1 broadcast_multiply_fusion
  345.5 2.5 fusion.19
  348.0 0.6 copy.69
  348.6 1.0 convolution_bitcast_fusion
  349.6 1.4 fusion.60
  351.0 0.0 all-gather.7.cloned.1.call-update
  351.0 0.0 reduce-scatter.4.cloned.1.call-start
  351.1 186.7 %all-gather.7.cloned.1.call-done = bf16[1,32,512,512]{2,1,0,3:T(8,128)(2,1)} async-done(((bf16[1,32,512,16]{2,1,0,3:T(8,128)(2,1)}), bf16[1,32,512,512]{2,1,0,3:T(8,128)(2,1)}) %all-gather.7.cloned.1.call-update) | async-done | bytes 16777232 | tf_op jit(solution)/shard_map/all_gather | solution.py:72
  537.8 26.4 %copy.71 = bf16[1,32,512,512]{3,2,1,0:T(8,128)(2,1)} copy(bf16[1,32,512,512]{2,1,0,3:T(8,128)(2,1)} %all-gather.7.cloned.1.call-done) | data formatting | bytes 33554432 | tf_op jit(solution)/shard_map/all_gather | solution.py:72
  564.2 8.3 %fusion.74 = (bf16[16,512]{1,0:T(8,128)(2,1)S(1)}, bf16[16,512]{1,0:T(8,128)(2,1)S(1)}, f32[32,16,512]{2,1,0:T(8,128)S(1)}) fusion(bf16[1,32,512,512]{3,2,1,0:T(8,128)(2,1)} %copy.71, bf16[32,512,16]{1,0,2:T(8,128)(2,1)S(1)} %get-tuple-element.19), kind=kOutput, calls=%fused_computation.107 | convolution fusion | flops 269205504 | bytes 18382848 | tf_op jit(solution)/shard_map/cki,ckj->cij/dot_general | solution.py:47
  572.5 19.5 %all-reduce = (bf16[16,512]{1,0:T(8,128)(2,1)S(1)}, bf16[16,512]{1,0:T(8,128)(2,1)S(1)}) all-reduce(bf16[16,512]{1,0:T(8,128)(2,1)S(1)} %get-tuple-element.12, bf16[16,512]{1,0:T(8,128)(2,1)S(1)} %get-tuple-element.11), channel_id=1, replica_groups=mesh['blk'=32,'chan'=4] {'chan'}, use_global_device_ids=true, to_apply=%region_14.0 | all-reduce | flops 16384 | bytes 65536 | tf_op jit(solution)/shard_map/psum | solution.py:34
  592.0 0.1 multiply_convert_fusion
  592.1 0.8 convolution_convert_fusion
  592.9 1.4 copy.86
  594.3 0.0 copy-start
  594.3 1.9 copy.114
  596.2 0.0 reduce-scatter.4.cloned.1.call-update
  596.2 0.0 copy-done
  596.2 2.9 fusion.21
  599.1 33.5 %reduce-scatter.4.cloned.1.call-done = bf16[128,2048]{1,0:T(8,128)(2,1)} async-done(((bf16[512,2048]{1,0:T(8,128)(2,1)}), bf16[128,2048]{1,0:T(8,128)(2,1)}) %reduce-scatter.4.cloned.1.call-update) | async-done | bytes 524304
  632.6 1.1 copy.91
  633.8 0.5 copy.87
  634.2 1.6 fusion.53
  635.8 1.0 copy.75
  (5 shorter events, 0.1 us)
Async XLA Ops:
  6.5 4.3 copy-start.1
  6.5 197.8 %all-gather.5.cloned.1.call-start = ((), (), s32[]{:S(2)}) async-start(), calls=%async_computation.3 | async-start | bytes 17301504 | tf_op jit(solution)/shard_map/all_gather | solution.py:59
  11.8 1.7 copy-start.4
  13.4 287.8 %all-reduce.4.cloned.1.call-start = ((), (), s32[]{:S(2)}) async-start(), calls=%async_computation.2 | async-start | bytes 4194304 | tf_op jit(solution)/shard_map/psum | solution.py:63
  204.4 36.8 %copy-start.3 = (bf16[2,32,128]{2,1,0:T(8,128)(2,1)S(1)}, bf16[2,32,128]{2,1,0:T(8,128)(2,1)}, u32[]{:S(2)}) copy-start(bf16[2,32,128]{2,1,0:T(8,128)(2,1)} %param.9) | copy-start | bytes 49156
  222.0 79.2 %copy-start.2 = (bf16[2,128,128]{2,1,0:T(8,128)(2,1)S(1)}, bf16[2,128,128]{2,1,0:T(8,128)(2,1)}, u32[]{:S(2)}) copy-start(bf16[2,128,128]{2,1,0:T(8,128)(2,1)} %param.8) | copy-start | bytes 196612
  243.2 294.6 %all-gather.7.cloned.1.call-start = ((), (), s32[]{:S(2)}) async-start(), calls=%async_computation.4 | async-start | bytes 17301504 | tf_op jit(solution)/shard_map/all_gather | solution.py:72
  351.0 281.6 %reduce-scatter.4.cloned.1.call-start = ((), (), s32[]{:S(2)}) async-start(), calls=%async_computation.5 | async-start | bytes 2621440
  594.3 1.9 copy-start
Sparse Core Ops, SparseCore 0:
  13.5 190.8 all-gather.4
  243.4 57.7 all-reduce.3
  351.1 186.6 all-gather.6
  596.3 36.2 reduce-scatter.3
where the time goes:
time: 645 us; the launch traced here: 643 us
  waiting for transfers between devices  469 us (73%)
  blocking collectives  71.7 us (11%)
  local copies, waits for them, and re-layouts  40.4 us (6%)
  matrix products  38.4 us (6%)
  between operations  13.3 us (2%)
  other arithmetic  10.4 us (2%)
    all_gather x1, waiting for transfers between devices, on_device(): lax.all_gather(right_out, 'blk', axis=1, tiled=True)  191 us
    all_gather x1, waiting for transfers between devices, on_device(): lax.all_gather(right_turned, 'blk', axis=2, tiled=True)  187 us
    psum x1, waiting for transfers between devices, on_device(): lax.psum(project_out(hidden_out, out_weight[0]).astype(jnp.bfloat16), 'ch...  57.7 us
    psum x2, blocking collectives, hidden_norm(): lax.psum(jnp.sum(product * product, 0).astype(jnp.bfloat16), 'chan')  38.4 us
    unnamed x5, waiting for transfers between devices  33.6 us
    all_to_all x1, blocking collectives, on_device(): lax.all_to_all(middle, 'blk', split_axis=1, concat_axis=0, tiled=True)  33.2 us
    all_gather x1, local copies, waits for them, and re-layouts, on_device(): lax.all_gather(right_turned, 'blk', axis=2, tiled=True)  26.4 us
    dot_general x1, matrix products, on_device(): jnp.einsum('cik,cjk->cij', left_out, lax.all_gather(right_out, 'blk', axi...  17.6 us
  transfers between devices with their start and end apart: 4, of which 4 were waited for; matrix products, arithmetic and copies ran while one was open for 0% of the time, Pallas kernels for 0%

commit v1 on v0

v1 whole, which is shorter than its diff:
```python
import functools

import jax
import jax.numpy as jnp
from jax import lax
from jax.experimental import pallas as pl
from jax.experimental.pallas import tpu as pltpu
from jax.sharding import PartitionSpec as P

epsilon = 1e-05
F32 = jnp.float32
BF16 = jnp.bfloat16
VMEM_LIMIT = 48 * 1024 * 1024


def params():
    return pltpu.CompilerParams(vmem_limit_bytes=VMEM_LIMIT)


def cost(flops, moved):
    return pl.CostEstimate(flops=flops, bytes_accessed=moved, transcendentals=0)


def sig(x):
    return 0.5 + 0.5 * jnp.tanh(0.5 * x)


def dot(a, b, ca, cb):
    return lax.dot_general(a, b, (((ca,), (cb,)), ((), ())), preferred_element_type=F32)


def centering(n):
    eye = lax.broadcasted_iota(jnp.int32, (n, n), 0) == lax.broadcasted_iota(jnp.int32, (n, n), 1)
    return (jnp.where(eye, 1.0, 0.0) - 1.0 / n).astype(BF16)


def norm_last(x, gain):
    n = x.shape[-1]
    d = dot(x, centering(n), 1, 0)
    var = dot((d * d).astype(BF16), jnp.full((n, n), 1.0 / n, BF16), 1, 0)
    return (d * lax.rsqrt(var + epsilon) * gain).astype(BF16)


def project_kernel(x_ref, w_ref, gain_ref, out_ref, tmp):
    rows, cols, ch = x_ref.shape
    share = out_ref.shape[0]
    gain = gain_ref[...]
    for i in range(rows):
        normed = norm_last(x_ref[i], gain)
        parts = dot(w_ref[...], normed, 1, 1)
        left = parts[:share] * sig(parts[share : 2 * share])
        right = parts[2 * share : 3 * share] * sig(parts[3 * share :])
        tmp[0, pl.ds(i, share, stride=rows), :] = left
        tmp[1, pl.ds(i, share, stride=rows), :] = right
    for s in range(2):
        out_ref[:, s] = tmp[s].reshape(share, rows, cols).astype(BF16)


def project(x, w, gain, share):
    rows, width, ch = x.shape
    cols = 128
    return pl.pallas_call(
        project_kernel,
        grid=(width // cols,),
        in_specs=[
            pl.BlockSpec((rows, cols, ch), lambda t: (0, t, 0)),
            pl.BlockSpec(w.shape, lambda t: (0, 0)),
            pl.BlockSpec(gain.shape, lambda t: (0, 0)),
        ],
        out_specs=pl.BlockSpec((share, 2, rows, cols), lambda t: (0, 0, 0, t)),
        out_shape=jax.ShapeDtypeStruct((share, 2, rows, width), BF16),
        scratch_shapes=[pltpu.VMEM((2, share * rows, cols), F32)],
        compiler_params=params(),
        name="project_rows",
    )(x, w, gain)


def gate_kernel(x_ref, w_ref, gain_ref, out_ref):
    rows, cols, ch = x_ref.shape
    normed = norm_last(x_ref[...].reshape(rows * cols, ch), gain_ref[...])
    out_ref[...] = sig(dot(normed, w_ref[...], 1, 0)).reshape(rows, cols, ch)


def gates(x, w, gain):
    rows, cols, ch = x.shape
    return pl.pallas_call(
        gate_kernel,
        out_shape=jax.ShapeDtypeStruct(x.shape, F32),
        compiler_params=params(),
        cost_estimate=cost(6 * rows * cols * ch * ch, 6 * rows * cols * ch),
        name="gate_rows",
    )(x, w, gain)


def outgoing_kernel(x_ref, out_ref):
    blocks, _, rows, n = x_ref.shape
    tiles, cols = out_ref.shape[1], out_ref.shape[3]
    left = x_ref[:, 0].reshape(blocks * rows, n)
    per = cols // rows
    for q in range(tiles):
        right = x_ref[q * per : (q + 1) * per, 1].reshape(cols, n)
        out_ref[:, q] = dot(left, right, 1, 1).reshape(blocks, rows, cols).astype(BF16)


def outgoing(x, tiles):
    blocks, _, rows, n = x.shape
    return pl.pallas_call(
        outgoing_kernel,
        out_shape=jax.ShapeDtypeStruct((blocks, tiles, rows, n // tiles), BF16),
        compiler_params=params(),
        name="outgoing_product",
    )(x)


def incoming_kernel(x_ref, out_ref):
    blocks, tiles, _, rows, cols = x_ref.shape
    per = cols // rows
    rights = [x_ref[:, q, 1].reshape(blocks * rows, cols) for q in range(tiles)]
    right = jnp.concatenate(rights, axis=1)
    for p in range(tiles):
        left = x_ref[:, p, 0].reshape(blocks * rows, cols)
        product = dot(left, right, 0, 0).astype(BF16)
        for q in range(tiles):
            out_ref[p * per : (p + 1) * per, q] = product[:, q * cols : (q + 1) * cols].reshape(per, rows, cols)


def incoming(x):
    blocks, tiles, _, rows, cols = x.shape
    return pl.pallas_call(
        incoming_kernel,
        out_shape=jax.ShapeDtypeStruct((blocks, tiles, rows, cols), BF16),
        compiler_params=params(),
        name="incoming_product",
    )(x)


def normalized_products(p_ref, tmp):
    ch, rows, cols = p_ref.shape
    p = p_ref[...].astype(F32)
    d = p - jnp.sum(p, 0, keepdims=True) * (1.0 / ch)
    var = jnp.sum(d * d, 0, keepdims=True) * (1.0 / ch)
    tmp[...] = (d * lax.rsqrt(var + epsilon)).reshape(ch * rows, cols)


def middle_kernel(p_ref, pair_ref, gate_ref, ow_ref, w_ref, gain_ref, mid_ref, out_ref, tmp, tmp2):
    ch, rows, cols = p_ref.shape
    normalized_products(p_ref, tmp)
    gain = gain_ref[...]
    for i in range(rows):
        hidden = tmp[pl.ds(i, ch, stride=rows), :].astype(BF16)
        update = dot(hidden, ow_ref[...], 0, 0)
        mid = (pair_ref[i].astype(F32) + gate_ref[i] * update).astype(BF16)
        mid_ref[i] = mid
        parts = dot(w_ref[...], norm_last(mid, gain), 1, 1)
        tmp2[0, pl.ds(i, ch, stride=rows), :] = parts[:ch] * sig(parts[ch : 2 * ch])
        tmp2[1, pl.ds(i, ch, stride=rows), :] = parts[2 * ch : 3 * ch] * sig(parts[3 * ch :])
    for s in range(2):
        out_ref[:, s] = tmp2[s].reshape(ch, rows, cols).astype(BF16)


def middle_step(p, pair, gate, ow, w, gain):
    ch, rows, cols = p.shape
    return pl.pallas_call(
        middle_kernel,
        out_shape=(
            jax.ShapeDtypeStruct(pair.shape, BF16),
            jax.ShapeDtypeStruct((ch, 2, rows, cols), BF16),
        ),
        scratch_shapes=[pltpu.VMEM((ch * rows, cols), F32), pltpu.VMEM((2, ch * rows, cols), F32)],
        compiler_params=params(),
        name="middle_step",
    )(p, pair, gate, ow, w, gain)


def last_kernel(p_ref, mid_ref, gate_ref, ow_ref, out_ref, tmp):
    ch, rows, cols = p_ref.shape
    normalized_products(p_ref, tmp)
    for i in range(rows):
        hidden = tmp[pl.ds(i, ch, stride=rows), :].astype(BF16)
        update = dot(hidden, ow_ref[...], 0, 0)
        out_ref[i] = (mid_ref[i].astype(F32) + gate_ref[i] * update).astype(BF16)


def last_step(p, mid, gate, ow):
    ch, rows, cols = p.shape
    return pl.pallas_call(
        last_kernel,
        out_shape=jax.ShapeDtypeStruct(mid.shape, BF16),
        scratch_shapes=[pltpu.VMEM((ch * rows, cols), F32)],
        compiler_params=params(),
        name="last_step",
    )(p, mid, gate, ow)


def on_device(pair_rep, proj_weight, gate_weight, out_weight, in_gain, out_gain):
    rows, width, ch = pair_rep.shape
    tiles = lax.axis_size("chan")
    blocks = lax.axis_size("blk")
    share = proj_weight.shape[3]
    cols = width // tiles
    everywhere = ("blk", "chan")

    turned = jnp.transpose(proj_weight, (0, 1, 3, 2))
    mine = turned[0].reshape(4 * share, ch)
    scaled = (out_weight.astype(F32) * out_gain[:, :, None]).astype(BF16)
    packed = jnp.concatenate([turned[1].reshape(4 * share, ch), scaled.reshape(2 * share, ch)], 0)
    whole = lax.all_gather(packed, "chan", axis=0, tiled=False)

    def by_device(v):
        return jnp.moveaxis(v, 0, -2).reshape(v.shape[1:-2] + (share * tiles, ch))

    weights_in = by_device(whole[:, : 4 * share].reshape(tiles, 4, share, ch)).reshape(4 * share * tiles, ch)
    weights_out = by_device(whole[:, 4 * share :].reshape(tiles, 2, share, ch))

    halves = project(pair_rep, mine, in_gain[0:1], share)
    halves = lax.all_to_all(halves, "blk", 0, 0, tiled=True)
    own = lax.dynamic_slice_in_dim(pair_rep, lax.axis_index("chan") * cols, cols, 1)
    gate = gates(own, gate_weight[0], in_gain[0:1])

    product = outgoing(halves, tiles).reshape(blocks * tiles, rows, cols)
    product = lax.all_to_all(product, everywhere, 0, 0, tiled=True)
    mid, halves = middle_step(product, own, gate, weights_out[0], weights_in, in_gain[1:2])
    halves = lax.all_to_all(halves, everywhere, 0, 0, tiled=True)
    gate = gates(mid, gate_weight[1], in_gain[1:2])

    product = incoming(halves.reshape(blocks, tiles, 2, rows, cols)).reshape(blocks * tiles, rows, cols)
    product = lax.all_to_all(product, everywhere, 0, 0, tiled=True)
    return last_step(product, mid, gate, weights_out[1])


def solution(mesh):
    placed = (
        P("blk", None, None),
        P(None, None, None, "chan"),
        P(),
        P(None, "chan", None),
        P(),
        P(None, "chan"),
    )
    return jax.shard_map(
        on_device, mesh=mesh, in_specs=placed, out_specs=P("blk", "chan", None), check_vma=False
    )
```

time: 645 us -> 114 us (0.18)
  waiting for transfers between devices: 469 us -> 28.7 us
  matrix products: 38.4 us -> 0 us
  local copies, waits for them, and re-layouts: 40.4 us -> 4.47 us
  blocking collectives: 71.7 us -> 35.9 us
  Pallas kernels: 0 us -> 22.5 us
  starting transfers between devices: 0.31 us -> 22.2 us
  between operations: 13.3 us -> 0.13 us
  other arithmetic: 10.4 us -> 0.08 us
    all_gather x2 -> x0, waiting for transfers between devices: 378 us -> none  [the longest x1 191 us: on_device(): lax.all_gather(right_out, 'blk', axis=1, tiled=True)]
    psum x1 -> x0, waiting for transfers between devices: 57.7 us -> none  [on_device(): lax.psum(project_out(hidden_out, out_weight[0]).astype(jnp.bfloat16), 'ch...]
    psum x2 -> x0, blocking collectives: 38.4 us -> none  [hidden_norm(): lax.psum(jnp.sum(product * product, 0).astype(jnp.bfloat16), 'chan')]
    dot_general x8 -> x0, matrix products: 38.4 us -> none  [the longest x1 17.6 us: on_device(): jnp.einsum('cik,cjk->cij', left_out, lax.all_gather(right_out, 'blk', axi...]
    unnamed x5 -> x0, waiting for transfers between devices: 33.6 us -> none
    all_to_all x0 -> x3, waiting for transfers between devices: none -> 28.7 us  [the longest x2 15.1 us: on_device(): product = lax.all_to_all(product, everywhere, 0, 0, tiled=True)]
    all_gather x1 -> x0, local copies, waits for them, and re-layouts: 26.4 us -> none  [on_device(): lax.all_gather(right_turned, 'blk', axis=2, tiled=True)]
    pallas_call x0 -> x7, Pallas kernels: none -> 22.5 us  [the longest x1 11.3 us: project(): pl.pallas_call(project_kernel, grid=(width // cols,), in_specs=[pl.BlockS...]
  transfers between devices with their start and end apart: 4 -> 3, of which waited for: 4 -> 3; matrix products, arithmetic and copies ran while one was open for 0% -> 1% of each run, Pallas kernels for 0% -> 1%
where the time goes in v1:
time: 114 us
  blocking collectives  35.9 us (31%)
  waiting for transfers between devices  28.7 us (25%)
  Pallas kernels  22.5 us (20%)
  starting transfers between devices  22.2 us (19%)
  local copies, waits for them, and re-layouts  4.47 us (4%)
    all_to_all x1, blocking collectives, on_device(): halves = lax.all_to_all(halves, everywhere, 0, 0, tiled=True)  24.7 us
    all_to_all x2, waiting for transfers between devices, on_device(): product = lax.all_to_all(product, everywhere, 0, 0, tiled=True)  15.1 us
    all_to_all x1, waiting for transfers between devices, on_device(): halves = lax.all_to_all(halves, 'blk', 0, 0, tiled=True)  13.6 us
    all_to_all x2, starting transfers between devices, on_device(): product = lax.all_to_all(product, everywhere, 0, 0, tiled=True)  12.4 us
    pallas_call x1, Pallas kernels, project(): pl.pallas_call(project_kernel, grid=(width // cols,), in_specs=[pl.BlockS...  11.3 us
    all_gather x1, blocking collectives, on_device(): whole = lax.all_gather(packed, 'chan', axis=0, tiled=False)  11.2 us
    all_to_all x1, starting transfers between devices, on_device(): halves = lax.all_to_all(halves, 'blk', 0, 0, tiled=True)  9.8 us
    pallas_call x1, Pallas kernels, middle_step(): pl.pallas_call(middle_kernel, out_shape=(jax.ShapeDtypeStruct(pair.shape,...  5.33 us
  transfers between devices with their start and end apart: 3, of which 3 were waited for; matrix products, arithmetic and copies ran while one was open for 1% of the time, Pallas kernels for 1%

profile of v1, /device:TPU:1, one launch (start us, length us, event | category | flops | bytes accessed | tf_op | source)
XLA Modules:
  0.0 114.0 jit_solution(4766366134353893102)
XLA Ops:
  0.0 0.8 fusion.2
  0.8 0.8 fusion.1
  1.5 0.0 copy-start
  1.5 1.6 %copy-done = bf16[16,512,128]{2,1,0:T(8,128)(2,1)S(1)} copy-done((bf16[16,512,128]{2,1,0:T(8,128)(2,1)S(1)}, bf16[16,512,128]{2,1,0:T(8,128)(2,1)}, u32[]{:S(2)}) %copy-start) | copy-done | bytes 2097176
  3.1 0.0 copy-start.2
  3.1 0.0 copy-start.3
  3.1 11.3 %project_rows.1 = bf16[32,2,16,512]{3,2,1,0:T(8,128)(2,1)} custom-call(bf16[16,512,128]{2,1,0:T(8,128)(2,1)S(1)} %copy-done, bf16[128,128]{1,0:T(8,128)(2,1)S(1)} %bitcast.25, f32[1,128]{1,0:T(1,128)S(1)} %get-tuple-element.16.gain_ref), custom_call_target="tpu_custom_call" | custom-call | tf_op jit(solution)/shard_map/project_rows/pallas_call | solution.py:62
  14.5 9.8 %all-to-all-start = ((bf16[32,2,16,512]{3,2,1,0:T(8,128)(2,1)}), bf16[32,2,16,512]{3,2,1,0:T(8,128)(2,1)S(1)}, u32[]{:S(2)}, u32[]{:S(2)}) async-start(bf16[32,2,16,512]{3,2,1,0:T(8,128)(2,1)} %project_rows.1), calls=%async_computation | async-start | bytes 2097152 | tf_op jit(solution)/shard_map/all_to_all | solution.py:216
  24.3 0.0 copy-done.2
  24.3 0.0 copy-done.3
  24.3 0.1 multiply_convert_fusion
  24.4 0.0 copy-start.1
  24.4 1.1 constant_dynamic-slice_fusion.x_ref.pair_ref
  25.5 13.6 %all-to-all-done.x_ref = bf16[32,2,16,512]{3,2,1,0:T(8,128)(2,1)S(1)} async-done(((bf16[32,2,16,512]{3,2,1,0:T(8,128)(2,1)}), bf16[32,2,16,512]{3,2,1,0:T(8,128)(2,1)S(1)}, u32[]{:S(2)}, u32[]{:S(2)}) %all-to-all-start) | async-done | bytes 1048608 | tf_op jit(solution)/shard_map/all_to_all | solution.py:216
  39.1 1.5 %outgoing_product.1 = bf16[32,4,16,128]{3,2,1,0:T(8,128)(2,1)} custom-call(bf16[32,2,16,512]{3,2,1,0:T(8,128)(2,1)S(1)} %all-to-all-done.x_ref), custom_call_target="tpu_custom_call" | custom-call | tf_op jit(solution)/shard_map/outgoing_product/pallas_call | solution.py:107
  40.6 8.3 %all-to-all-start.1 = ((bf16[128,16,128]{2,1,0:T(8,128)(2,1)}), bf16[128,16,128]{2,1,0:T(8,128)(2,1)S(1)}, u32[]{:S(2)}, u32[]{:S(2)}) async-start(bf16[128,16,128]{2,1,0:T(8,128)(2,1)} %bitcast.2), calls=%async_computation.1 | async-start | bytes 1048576 | tf_op jit(solution)/shard_map/all_to_all | solution.py:221
  48.9 11.2 %all-gather = bf16[768,128]{1,0:T(8,128)(2,1)S(1)} all-gather(bf16[192,128]{1,0:T(8,128)(2,1)S(1)} %pad_maximum_fusion), channel_id=2, replica_groups=mesh['blk'=32,'chan'=4] {'chan'}, dimensions={0}, use_global_device_ids=true | all-gather | bytes 245760 | tf_op jit(solution)/shard_map/all_gather | solution.py:207
  60.1 0.1 copy.9
  60.2 0.1 copy.10
  60.3 0.0 copy-done.1
  60.3 0.7 gate_rows.2.gate_ref
  61.1 1.9 %all-to-all-done.1.p_ref = bf16[128,16,128]{2,1,0:T(8,128)(2,1)S(1)} async-done(((bf16[128,16,128]{2,1,0:T(8,128)(2,1)}), bf16[128,16,128]{2,1,0:T(8,128)(2,1)S(1)}, u32[]{:S(2)}, u32[]{:S(2)}) %all-to-all-start.1) | async-done | bytes 524320 | tf_op jit(solution)/shard_map/all_to_all | solution.py:221
  63.0 5.3 %middle_step.1 = (bf16[16,128,128]{2,1,0:T(8,128)(2,1)S(1)}, bf16[128,2,16,128]{3,2,1,0:T(8,128)(2,1)S(1)}) custom-call(bf16[128,16,128]{2,1,0:T(8,128)(2,1)S(1)} %all-to-all-done.1.p_ref, bf16[16,128,128]{2,1,0:T(8,128)(2,1)S(1)} %constant_dynamic-slice_fusion.x_ref.pair_ref, f32[16,128,128]{2,1,0:T(8,128)S(1)} %gate_rows.2.gate_ref, ...), custom_call_target="tpu_custom_call" | custom-call | tf_op jit(solution)/shard_map/middle_step/pallas_call | solution.py:163
  68.4 24.7 %all_to_all.20 = bf16[128,2,16,128]{3,2,1,0:T(8,128)(2,1)S(1)} all-to-all(bf16[128,2,16,128]{3,2,1,0:T(8,128)(2,1)S(1)} %get-tuple-element.7), channel_id=1, replica_groups=mesh['blk'=32,'chan'=4] {'blk','chan'}, dimensions={0} | all-to-all | bytes 2097152 | tf_op jit(solution)/shard_map/all_to_all | solution.py:223
  93.1 1.3 %incoming_product.1 = bf16[32,4,16,128]{3,2,1,0:T(8,128)(2,1)} custom-call(bf16[32,4,2,16,128]{4,3,2,1,0:T(8,128)(2,1)S(1)} %bitcast.22), custom_call_target="tpu_custom_call" | custom-call | tf_op jit(solution)/shard_map/incoming_product/pallas_call | solution.py:129
  94.4 4.1 %all-to-all-start.3 = ((bf16[128,16,128]{2,1,0:T(8,128)(2,1)}), bf16[128,16,128]{2,1,0:T(8,128)(2,1)S(1)}, u32[]{:S(2)}, u32[]{:S(2)}) async-start(bf16[128,16,128]{2,1,0:T(8,128)(2,1)} %bitcast.14), calls=%async_computation.3 | async-start | bytes 1048576 | tf_op jit(solution)/shard_map/all_to_all | solution.py:227
  98.4 0.7 gate_rows.3.gate_ref
  99.2 13.1 %all-to-all-done.3.p_ref = bf16[128,16,128]{2,1,0:T(8,128)(2,1)S(1)} async-done(((bf16[128,16,128]{2,1,0:T(8,128)(2,1)}), bf16[128,16,128]{2,1,0:T(8,128)(2,1)S(1)}, u32[]{:S(2)}, u32[]{:S(2)}) %all-to-all-start.3) | async-done | bytes 524320 | tf_op jit(solution)/shard_map/all_to_all | solution.py:227
  112.3 1.7 %last_step.1 = bf16[16,128,128]{2,1,0:T(8,128)(2,1)} custom-call(bf16[128,16,128]{2,1,0:T(8,128)(2,1)S(1)} %all-to-all-done.3.p_ref, bf16[16,128,128]{2,1,0:T(8,128)(2,1)S(1)} %get-tuple-element.8.x_ref.mid_ref, f32[16,128,128]{2,1,0:T(8,128)S(1)} %gate_rows.3.gate_ref, bf16[128,128]{1,0:T(8,128)(2,1)S(1)} %bitcast.26), custom_call_target="tpu_custom_call" | custom-call | tf_op jit(solution)/shard_map/last_step/pallas_call | solution.py:186
  (5 shorter events, 0.1 us)
Async XLA Ops:
  1.5 1.6 %copy-start = (bf16[16,512,128]{2,1,0:T(8,128)(2,1)S(1)}, bf16[16,512,128]{2,1,0:T(8,128)(2,1)}, u32[]{:S(2)}) copy-start(bf16[16,512,128]{2,1,0:T(8,128)(2,1)} %x_ref.1) | copy-start | bytes 6291460
  3.1 21.1 %copy-start.2 = (bf16[2,32,128]{2,1,0:T(8,128)(2,1)S(1)}, bf16[2,32,128]{2,1,0:T(8,128)(2,1)}, u32[]{:S(2)}) copy-start(bf16[2,32,128]{2,1,0:T(8,128)(2,1)} %param.9) | copy-start | bytes 49156
  3.1 21.1 %copy-start.3 = (f32[2,32]{1,0:T(2,128)S(1)}, f32[2,32]{1,0:T(2,128)}, u32[]{:S(2)}) copy-start(f32[2,32]{1,0:T(2,128)} %param.11) | copy-start | bytes 772
  14.5 24.6 %all-to-all-start = ((bf16[32,2,16,512]{3,2,1,0:T(8,128)(2,1)}), bf16[32,2,16,512]{3,2,1,0:T(8,128)(2,1)S(1)}, u32[]{:S(2)}, u32[]{:S(2)}) async-start(bf16[32,2,16,512]{3,2,1,0:T(8,128)(2,1)} %project_rows.1), calls=%async_computation | async-start | bytes 2097152 | tf_op jit(solution)/shard_map/all_to_all | solution.py:216
  24.4 35.9 %copy-start.1 = (bf16[2,128,128]{2,1,0:T(8,128)(2,1)S(1)}, bf16[2,128,128]{2,1,0:T(8,128)(2,1)}, u32[]{:S(2)}) copy-start(bf16[2,128,128]{2,1,0:T(8,128)(2,1)} %param.8) | copy-start | bytes 196612
  40.6 22.4 %all-to-all-start.1 = ((bf16[128,16,128]{2,1,0:T(8,128)(2,1)}), bf16[128,16,128]{2,1,0:T(8,128)(2,1)S(1)}, u32[]{:S(2)}, u32[]{:S(2)}) async-start(bf16[128,16,128]{2,1,0:T(8,128)(2,1)} %bitcast.2), calls=%async_computation.1 | async-start | bytes 1048576 | tf_op jit(solution)/shard_map/all_to_all | solution.py:221
  94.4 17.9 %all-to-all-start.3 = ((bf16[128,16,128]{2,1,0:T(8,128)(2,1)}), bf16[128,16,128]{2,1,0:T(8,128)(2,1)S(1)}, u32[]{:S(2)}, u32[]{:S(2)}) async-start(bf16[128,16,128]{2,1,0:T(8,128)(2,1)} %bitcast.14), calls=%async_computation.3 | async-start | bytes 1048576 | tf_op jit(solution)/shard_map/all_to_all | solution.py:227

commit v2 on v1

v2 whole, which is shorter than its diff:
```python
import jax
import jax.numpy as jnp
from jax import lax
from jax.experimental import pallas as pl
from jax.experimental.pallas import tpu as pltpu
from jax.sharding import PartitionSpec as P

epsilon = 1e-05
F32 = jnp.float32
BF16 = jnp.bfloat16
WHOLE = pl.BlockSpec(memory_space=pltpu.VMEM)


def params(mib):
    return pltpu.CompilerParams(vmem_limit_bytes=mib * 1024 * 1024)


def cost(flops, moved):
    return pl.CostEstimate(flops=flops, bytes_accessed=moved, transcendentals=0)


def dot(a, b, ca, cb):
    return lax.dot_general(a, b, (((ca,), (cb,)), ((), ())), preferred_element_type=F32)


def project_kernel(x_ref, w_ref, gain_ref, out_ref, tmp):
    rows, cols, ch = x_ref.shape
    share = out_ref.shape[0]
    weights = (w_ref[0].reshape(4 * share, ch).astype(F32) * gain_ref[0:1]).astype(BF16)
    x = jnp.concatenate([x_ref[i].T for i in range(rows)], 1).astype(F32)
    centered = x - jnp.sum(x, 0, keepdims=True) * (1.0 / ch)
    var = jnp.sum(centered * centered, 0, keepdims=True) * (1.0 / ch)
    scale = jnp.broadcast_to(0.5 * lax.rsqrt(var + epsilon), (share, rows * cols))
    parts = dot(weights, centered.astype(BF16), 1, 0)
    for i in range(rows):
        lanes = slice(i * cols, (i + 1) * cols)
        for s in range(2):
            value = parts[2 * s * share : (2 * s + 1) * share, lanes] * scale[:, lanes]
            gate = jnp.tanh(parts[(2 * s + 1) * share : (2 * s + 2) * share, lanes] * scale[:, lanes])
            tmp[s, pl.ds(i, share, stride=rows), :] = value + value * gate
    for s in range(2):
        out_ref[:, s] = tmp[s].reshape(share, rows, cols).astype(BF16)


def project(x, w, gain, cols):
    rows, width, ch = x.shape
    share = w.shape[2]
    return pl.pallas_call(
        project_kernel,
        grid=(width // cols,),
        in_specs=[pl.BlockSpec((rows, cols, ch), lambda t: (0, t, 0)), WHOLE, WHOLE],
        out_specs=pl.BlockSpec((share, 2, rows, cols), lambda t: (0, 0, 0, t)),
        out_shape=jax.ShapeDtypeStruct((share, 2, rows, width), BF16),
        scratch_shapes=[pltpu.VMEM((2, share * rows, cols), F32)],
        compiler_params=params(60),
        name="project_rows",
    )(x, w, gain)


def norm_down(x, gain):
    ch = x.shape[0]
    centered = x - jnp.sum(x, 0, keepdims=True) * (1.0 / ch)
    var = jnp.sum(centered * centered, 0, keepdims=True) * (1.0 / ch)
    out = centered * lax.rsqrt(var + epsilon)
    return (out if gain is None else out * gain).astype(BF16)


def gate_of(x, w_ref, gain_ref, s):
    w = (w_ref[s].astype(F32).T * gain_ref[s : s + 1]).astype(BF16)
    return 0.5 + 0.5 * jnp.tanh(0.5 * dot(w, norm_down(x, None), 1, 0))


def first_gate_kernel(x_ref, w_ref, gain_ref, turned_ref, gate_ref):
    rows, cols, ch = x_ref.shape
    turned = jnp.concatenate([x_ref[i].astype(F32).T for i in range(rows)], 1)
    turned_ref[...] = turned.astype(BF16)
    gate_ref[...] = gate_of(turned, w_ref, gain_ref, 0)


def first_gate(x, w, gain):
    rows, cols, ch = x.shape
    return pl.pallas_call(
        first_gate_kernel,
        out_shape=(
            jax.ShapeDtypeStruct((ch, rows * cols), BF16),
            jax.ShapeDtypeStruct((ch, rows * cols), F32),
        ),
        compiler_params=params(32),
        cost_estimate=cost(2 * rows * cols * ch * ch, 8 * rows * cols * ch),
        name="first_gate",
    )(x, w, gain)


def second_gate_kernel(x_ref, w_ref, gain_ref, gate_ref):
    gate_ref[...] = gate_of(x_ref[...].astype(F32), w_ref, gain_ref, 1)


def second_gate(x, w, gain):
    return pl.pallas_call(
        second_gate_kernel,
        out_shape=jax.ShapeDtypeStruct(x.shape, F32),
        compiler_params=params(32),
        cost_estimate=cost(2 * x.size * x.shape[0], 6 * x.size),
        name="second_gate",
    )(x, w, gain)


def outgoing_kernel(x_ref, out_ref):
    blocks, _, rows, n = x_ref.shape
    tiles, cols = out_ref.shape[1], out_ref.shape[3]
    left = x_ref[:, 0].reshape(blocks * rows, n)
    per = cols // rows
    for q in range(tiles):
        right = x_ref[q * per : (q + 1) * per, 1].reshape(cols, n)
        out_ref[:, q] = dot(left, right, 1, 1).reshape(blocks, rows, cols).astype(BF16)


def outgoing(x, tiles):
    blocks, _, rows, n = x.shape
    return pl.pallas_call(
        outgoing_kernel,
        out_shape=jax.ShapeDtypeStruct((blocks, tiles, rows, n // tiles), BF16),
        compiler_params=params(32),
        name="outgoing_product",
    )(x)


def incoming_kernel(x_ref, out_ref):
    blocks, tiles, _, rows, cols = x_ref.shape
    per = cols // rows
    rights = [x_ref[:, q, 1].reshape(blocks * rows, cols) for q in range(tiles)]
    right = jnp.concatenate(rights, axis=1)
    for p in range(tiles):
        left = x_ref[:, p, 0].reshape(blocks * rows, cols)
        product = dot(left, right, 0, 0).astype(BF16)
        for q in range(tiles):
            out_ref[p * per : (p + 1) * per, q] = product[:, q * cols : (q + 1) * cols].reshape(per, rows, cols)


def incoming(x):
    blocks, tiles, _, rows, cols = x.shape
    return pl.pallas_call(
        incoming_kernel,
        out_shape=jax.ShapeDtypeStruct((blocks, tiles, rows, cols), BF16),
        compiler_params=params(32),
        name="incoming_product",
    )(x)


def update_of(p_ref, whole_ref, s, tmp):
    ch, rows, cols = p_ref.shape
    tiles = whole_ref.shape[0]
    share = ch // tiles
    p = p_ref[...].astype(F32)
    tmp[...] = p.reshape(ch * rows, cols)
    mean = jnp.sum(p, 0) * (1.0 / ch)
    square = jnp.sum(p * p, 0) * (1.0 / ch)
    scale = lax.rsqrt(square - mean * mean + epsilon)
    weights = jnp.concatenate(
        [whole_ref[q, (4 + s) * share : (5 + s) * share] for q in range(tiles)], 0
    )
    columns = dot(weights, jnp.ones((ch, cols), BF16), 0, 0)
    row = [
        jnp.concatenate(
            [tmp[pl.ds(q * rows + i, share, stride=tiles * rows), :] for q in range(tiles)], 0
        ).astype(BF16)
        for i in range(rows)
    ]
    summed = dot(weights, jnp.concatenate(row, 1), 0, 0)
    return [
        (summed[:, i * cols : (i + 1) * cols] - columns * mean[i : i + 1]) * scale[i : i + 1]
        for i in range(rows)
    ]


def middle_kernel(p_ref, pair_ref, gate_ref, whole_ref, mid_ref, out_ref, tmp, tmp2):
    ch, rows, cols = p_ref.shape
    tiles = whole_ref.shape[0]
    share = ch // tiles
    updates = update_of(p_ref, whole_ref, 0, tmp)
    normed = []
    for i in range(rows):
        lanes = slice(i * cols, (i + 1) * cols)
        mid = (pair_ref[:, lanes].astype(F32) + gate_ref[:, lanes] * updates[i]).astype(BF16)
        mid_ref[:, lanes] = mid
        normed.append(norm_down(mid.astype(F32), None))
    weights = jnp.concatenate(
        [whole_ref[q, a * share : (a + 1) * share] for a in range(4) for q in range(tiles)], 0
    )
    parts = dot(weights, jnp.concatenate(normed, 1), 1, 0)
    for i in range(rows):
        lanes = slice(i * cols, (i + 1) * cols)
        for s in range(2):
            value = parts[2 * s * ch : (2 * s + 1) * ch, lanes]
            both = value + value * jnp.tanh(parts[(2 * s + 1) * ch : (2 * s + 2) * ch, lanes])
            for q in range(tiles):
                tmp2[s, pl.ds(q * rows + i, share, stride=tiles * rows), :] = both[q * share : (q + 1) * share]
    for s in range(2):
        out_ref[:, s] = tmp2[s].reshape(ch, rows, cols).astype(BF16)


def middle_step(p, pair, gate, whole):
    ch, rows, cols = p.shape
    return pl.pallas_call(
        middle_kernel,
        out_shape=(
            jax.ShapeDtypeStruct(pair.shape, BF16),
            jax.ShapeDtypeStruct((ch, 2, rows, cols), BF16),
        ),
        scratch_shapes=[pltpu.VMEM((ch * rows, cols), F32), pltpu.VMEM((2, ch * rows, cols), F32)],
        compiler_params=params(32),
        name="middle_step",
    )(p, pair, gate, whole)


def last_kernel(p_ref, mid_ref, gate_ref, whole_ref, out_ref, tmp):
    ch, rows, cols = p_ref.shape
    updates = update_of(p_ref, whole_ref, 1, tmp)
    for i in range(rows):
        lanes = slice(i * cols, (i + 1) * cols)
        out = mid_ref[:, lanes].astype(F32) + gate_ref[:, lanes] * updates[i]
        out_ref[i] = out.T.astype(BF16)


def last_step(p, mid, gate, whole):
    ch, rows, cols = p.shape
    return pl.pallas_call(
        last_kernel,
        out_shape=jax.ShapeDtypeStruct((rows, cols, mid.shape[0]), BF16),
        scratch_shapes=[pltpu.VMEM((ch * rows, cols), F32)],
        compiler_params=params(32),
        name="last_step",
    )(p, mid, gate, whole)


def on_device(pair_rep, proj_weight, gate_weight, out_weight, in_gain, out_gain):
    rows, width, ch = pair_rep.shape
    tiles = lax.axis_size("chan")
    blocks = lax.axis_size("blk")
    share = proj_weight.shape[3]
    cols = width // tiles
    everywhere = ("blk", "chan")

    turned = jnp.transpose(proj_weight, (0, 1, 3, 2))
    halves = project(pair_rep, turned, in_gain, cols)

    turned, out_weight, out_gain, gain, halves = lax.optimization_barrier(
        (turned, out_weight, out_gain, in_gain, halves)
    )
    later = (turned[1].astype(F32) * (0.5 * gain[1])).astype(BF16).reshape(4 * share, ch)
    scaled = (out_weight.astype(F32) * out_gain[:, :, None]).astype(BF16).reshape(2 * share, ch)
    packed = jnp.concatenate([later, scaled], 0)
    whole = lax.all_gather(packed, "chan", axis=0, tiled=False)
    own = lax.dynamic_slice_in_dim(pair_rep, lax.axis_index("chan") * cols, cols, 1)
    own, gate = first_gate(own, gate_weight, in_gain)

    halves = lax.all_to_all(halves, "blk", 0, 0, tiled=True)
    halves, whole, own, gate = lax.optimization_barrier((halves, whole, own, gate))
    product = outgoing(halves, tiles).reshape(blocks * tiles, rows, cols)
    product = lax.all_to_all(product, everywhere, 0, 0, tiled=True)
    mid, halves = middle_step(product, own, gate, whole)
    gate = second_gate(mid, gate_weight, in_gain)
    halves = lax.all_to_all(halves, everywhere, 0, 0, tiled=True)

    product = incoming(halves.reshape(blocks, tiles, 2, rows, cols)).reshape(blocks * tiles, rows, cols)
    product = lax.all_to_all(product, everywhere, 0, 0, tiled=True)
    return last_step(product, mid, gate, whole)


def solution(mesh):
    placed = (
        P("blk", None, None),
        P(None, None, None, "chan"),
        P(),
        P(None, "chan", None),
        P(),
        P(None, "chan"),
    )
    return jax.shard_map(
        on_device, mesh=mesh, in_specs=placed, out_specs=P("blk", "chan", None), check_vma=False
    )
```

time: 114 us -> 101 us (0.89)
  blocking collectives: 35.9 us -> 59.3 us
  waiting for transfers between devices: 28.7 us -> 13.3 us
  Pallas kernels: 22.5 us -> 13.1 us
  starting transfers between devices: 22.2 us -> 14 us
  local copies, waits for them, and re-layouts: 4.47 us -> 1.12 us
    all_to_all x0 -> x1, blocking collectives: none -> 21.1 us  [on_device(): product = lax.all_to_all(product, everywhere, 0, 0, tiled=True)]
    all_to_all x1, waiting for transfers between devices: 13.6 us -> 0.01 us  [on_device(): halves = lax.all_to_all(halves, 'blk', 0, 0, tiled=True)]
    all_to_all x2 -> x1, starting transfers between devices: 12.4 us -> 4.07 us  [on_device(): product = lax.all_to_all(product, everywhere, 0, 0, tiled=True)]
    pallas_call x1, Pallas kernels: 11.3 us -> 4.91 us  [project(): pl.pallas_call(project_kernel, grid=(width // cols,), in_specs=[pl.BlockS...]
    all_gather x1, blocking collectives: 11.2 us -> 15 us  [on_device(): whole = lax.all_gather(packed, 'chan', axis=0, tiled=False)]
    pallas_call x1, Pallas kernels: 5.33 us -> 3.1 us  [middle_step(): pl.pallas_call(middle_kernel, out_shape=(jax.ShapeDtypeStruct(pair.shape,...]
    all_to_all x2 -> x1, waiting for transfers between devices: 15.1 us -> 13.3 us  [on_device(): product = lax.all_to_all(product, everywhere, 0, 0, tiled=True)]
    unnamed x10, local copies, waits for them, and re-layouts: 1.76 us -> 0.02 us
  transfers between devices with their start and end apart: 3 -> 2, of which waited for: 3 -> 1; matrix products, arithmetic and copies ran while one was open for 1% -> 1% of each run, Pallas kernels for 1% -> 1%
where the time goes in v2:
time: 101 us
  blocking collectives  59.3 us (59%)
  starting transfers between devices  14 us (14%)
  waiting for transfers between devices  13.3 us (13%)
  Pallas kernels  13.1 us (13%)
  local copies, waits for them, and re-layouts  1.12 us (1%)
    all_to_all x1, blocking collectives, on_device(): halves = lax.all_to_all(halves, everywhere, 0, 0, tiled=True)  23.1 us
    all_to_all x1, blocking collectives, on_device(): product = lax.all_to_all(product, everywhere, 0, 0, tiled=True)  21.1 us
    all_gather x1, blocking collectives, on_device(): whole = lax.all_gather(packed, 'chan', axis=0, tiled=False)  15 us
    all_to_all x1, waiting for transfers between devices, on_device(): product = lax.all_to_all(product, everywhere, 0, 0, tiled=True)  13.3 us
    all_to_all x1, starting transfers between devices, on_device(): halves = lax.all_to_all(halves, 'blk', 0, 0, tiled=True)  9.95 us
    pallas_call x1, Pallas kernels, project(): pl.pallas_call(project_kernel, grid=(width // cols,), in_specs=[pl.BlockS...  4.91 us
    all_to_all x1, starting transfers between devices, on_device(): product = lax.all_to_all(product, everywhere, 0, 0, tiled=True)  4.07 us
    pallas_call x1, Pallas kernels, middle_step(): pl.pallas_call(middle_kernel, out_shape=(jax.ShapeDtypeStruct(pair.shape,...  3.1 us
  transfers between devices with their start and end apart: 2, of which 1 were waited for; matrix products, arithmetic and copies ran while one was open for 1% of the time, Pallas kernels for 1%

profile of v2, /device:TPU:1, one launch (start us, length us, event | category | flops | bytes accessed | tf_op | source)
XLA Modules:
  0.0 101.0 jit_solution(17029315172442391821)
XLA Ops:
  0.0 0.0 copy-start.2
  0.0 4.9 %project_rows.1 = bf16[32,2,16,512]{3,2,1,0:T(8,128)(2,1)} custom-call(bf16[16,512,128]{2,1,0:T(8,128)(2,1)} %x_ref.1, bf16[2,4,32,128]{3,2,1,0:T(8,128)(2,1)} %bitcast.15, f32[2,128]{1,0:T(2,128)} %gain_ref.5), custom_call_target="tpu_custom_call" | custom-call | tf_op jit(solution)/shard_map/project_rows/pallas_call | solution.py:48
  4.9 0.0 copy-start
  4.9 0.0 copy-start.1
  4.9 0.0 copy-start.3
  4.9 0.0 copy-start.4
  4.9 10.0 %all-to-all-start = ((bf16[32,2,16,512]{3,2,1,0:T(8,128)(2,1)}), bf16[32,2,16,512]{3,2,1,0:T(8,128)(2,1)S(1)}, u32[]{:S(2)}, u32[]{:S(2)}) async-start(bf16[32,2,16,512]{3,2,1,0:T(8,128)(2,1)} %project_rows.1), calls=%async_computation | async-start | bytes 2097152 | tf_op jit(solution)/shard_map/all_to_all | solution.py:257
  14.9 0.0 copy-done.2
  14.9 1.1 %constant_dynamic-slice_fusion.x_ref = bf16[16,128,128]{2,1,0:T(8,128)(2,1)S(1)} fusion(bf16[16,512,128]{2,1,0:T(8,128)(2,1)} %x_ref.1, s32[]{:T(128)S(6)} %select_n.3), kind=kLoop, calls=%fused_computation.5 | loop fusion | bytes 1048580 | tf_op jit(solution)/shard_map/dynamic_slice | solution.py:254
  16.0 0.0 copy-done
  16.0 0.0 copy-done.1
  16.0 0.7 first_gate.1
  16.7 0.0 copy-done.3
  16.7 0.0 copy-done.4
  16.8 0.1 multiply_convert_fusion
  16.9 15.0 %all-gather = bf16[768,128]{1,0:T(8,128)(2,1)S(1)} all-gather(bf16[192,128]{1,0:T(8,128)(2,1)S(1)} %pad_maximum_fusion), channel_id=2, replica_groups=mesh['blk'=32,'chan'=4] {'chan'}, dimensions={0}, use_global_device_ids=true | all-gather | bytes 245760 | tf_op jit(solution)/shard_map/all_gather | solution.py:253
  31.9 0.0 all-to-all-done.x_ref
  31.9 0.7 outgoing_product.1
  32.6 21.1 %all_to_all.20.p_ref = bf16[128,16,128]{2,1,0:T(8,128)(2,1)S(1)} all-to-all(bf16[128,16,128]{2,1,0:T(8,128)(2,1)S(1)} %bitcast.12), channel_id=1, replica_groups=mesh['blk'=32,'chan'=4] {'blk','chan'}, dimensions={0} | all-to-all | bytes 1048576 | tf_op jit(solution)/shard_map/all_to_all | solution.py:260
  53.8 3.1 %middle_step.1 = (bf16[128,2048]{1,0:T(8,128)(2,1)S(1)}, bf16[128,2,16,128]{3,2,1,0:T(8,128)(2,1)S(1)}) custom-call(bf16[128,16,128]{2,1,0:T(8,128)(2,1)S(1)} %all_to_all.20.p_ref, bf16[128,2048]{1,0:T(8,128)(2,1)S(1)} %get-tuple-element.26.pair_ref, f32[128,2048]{1,0:T(8,128)S(1)} %get-tuple-element.27.gate_ref, bf16[4,192,128]{2,1,0:T(8,128)(2,1)S(1)} %bitcast.13), custom_call_target="tpu_custom_call" | custom-call | tf_op jit(solution)/shard_map/middle_step/pallas_call | solution.py:204
  56.9 23.1 %all_to_all.21 = bf16[128,2,16,128]{3,2,1,0:T(8,128)(2,1)S(1)} all-to-all(bf16[128,2,16,128]{3,2,1,0:T(8,128)(2,1)S(1)} %get-tuple-element.29), channel_id=1, replica_groups=mesh['blk'=32,'chan'=4] {'blk','chan'}, dimensions={0} | all-to-all | bytes 2097152 | tf_op jit(solution)/shard_map/all_to_all | solution.py:263
  79.9 1.3 %incoming_product.1 = bf16[32,4,16,128]{3,2,1,0:T(8,128)(2,1)} custom-call(bf16[32,4,2,16,128]{4,3,2,1,0:T(8,128)(2,1)S(1)} %bitcast.11), custom_call_target="tpu_custom_call" | custom-call | tf_op jit(solution)/shard_map/incoming_product/pallas_call | solution.py:142
  81.2 4.1 %all-to-all-start.3 = ((bf16[128,16,128]{2,1,0:T(8,128)(2,1)}), bf16[128,16,128]{2,1,0:T(8,128)(2,1)S(1)}, u32[]{:S(2)}, u32[]{:S(2)}) async-start(bf16[128,16,128]{2,1,0:T(8,128)(2,1)} %bitcast.7), calls=%async_computation.3 | async-start | bytes 1048576 | tf_op jit(solution)/shard_map/all_to_all | solution.py:266
  85.3 0.5 second_gate.1.gate_ref
  85.8 13.3 %all-to-all-done.3.p_ref = bf16[128,16,128]{2,1,0:T(8,128)(2,1)S(1)} async-done(((bf16[128,16,128]{2,1,0:T(8,128)(2,1)}), bf16[128,16,128]{2,1,0:T(8,128)(2,1)S(1)}, u32[]{:S(2)}, u32[]{:S(2)}) %all-to-all-start.3) | async-done | bytes 524320 | tf_op jit(solution)/shard_map/all_to_all | solution.py:266
  99.1 1.9 %last_step.1 = bf16[16,128,128]{2,1,0:T(8,128)(2,1)} custom-call(bf16[128,16,128]{2,1,0:T(8,128)(2,1)S(1)} %all-to-all-done.3.p_ref, bf16[128,2048]{1,0:T(8,128)(2,1)S(1)} %get-tuple-element.30.x_ref.mid_ref, f32[128,2048]{1,0:T(8,128)S(1)} %second_gate.1.gate_ref, bf16[4,192,128]{2,1,0:T(8,128)(2,1)S(1)} %bitcast.14), custom_call_target="tpu_custom_call" | custom-call | tf_op jit(solution)/shard_map/last_step/pallas_call | solution.py:227
  (4 shorter events, 0.0 us)
Async XLA Ops:
  0.0 14.9 %copy-start.2 = (bf16[2,4,128,32]{2,3,1,0:T(8,128)(2,1)S(1)}, bf16[2,4,128,32]{2,3,1,0:T(8,128)(2,1)}, u32[]{:S(2)}) copy-start(bf16[2,4,128,32]{2,3,1,0:T(8,128)(2,1)} %param.7) | copy-start | bytes 196612
  4.9 11.1 %copy-start = (bf16[2,128,128]{2,1,0:T(8,128)(2,1)S(1)}, bf16[2,128,128]{2,1,0:T(8,128)(2,1)}, u32[]{:S(2)}) copy-start(bf16[2,128,128]{2,1,0:T(8,128)(2,1)} %w_ref.3) | copy-start | bytes 196612
  4.9 11.1 %copy-start.1 = (f32[2,128]{1,0:T(2,128)S(1)}, f32[2,128]{1,0:T(2,128)}, u32[]{:S(2)}) copy-start(f32[2,128]{1,0:T(2,128)} %gain_ref.5) | copy-start | bytes 3076
  4.9 11.8 %copy-start.3 = (bf16[2,32,128]{2,1,0:T(8,128)(2,1)S(1)}, bf16[2,32,128]{2,1,0:T(8,128)(2,1)}, u32[]{:S(2)}) copy-start(bf16[2,32,128]{2,1,0:T(8,128)(2,1)} %param.9) | copy-start | bytes 49156
  4.9 11.8 %copy-start.4 = (f32[2,32]{1,0:T(2,128)S(1)}, f32[2,32]{1,0:T(2,128)}, u32[]{:S(2)}) copy-start(f32[2,32]{1,0:T(2,128)} %param.11) | copy-start | bytes 772
  4.9 27.0 %all-to-all-start = ((bf16[32,2,16,512]{3,2,1,0:T(8,128)(2,1)}), bf16[32,2,16,512]{3,2,1,0:T(8,128)(2,1)S(1)}, u32[]{:S(2)}, u32[]{:S(2)}) async-start(bf16[32,2,16,512]{3,2,1,0:T(8,128)(2,1)} %project_rows.1), calls=%async_computation | async-start | bytes 2097152 | tf_op jit(solution)/shard_map/all_to_all | solution.py:257
  81.2 17.9 %all-to-all-start.3 = ((bf16[128,16,128]{2,1,0:T(8,128)(2,1)}), bf16[128,16,128]{2,1,0:T(8,128)(2,1)S(1)}, u32[]{:S(2)}, u32[]{:S(2)}) async-start(bf16[128,16,128]{2,1,0:T(8,128)(2,1)} %bitcast.7), calls=%async_computation.3 | async-start | bytes 1048576 | tf_op jit(solution)/shard_map/all_to_all | solution.py:266

commit v3 on v2

--- a/solution.py
+++ b/solution.py
@@ -57,24 +57,23 @@
     )(x, w, gain)
 
 
-def norm_down(x, gain):
+def norm_down(x):
     ch = x.shape[0]
     centered = x - jnp.sum(x, 0, keepdims=True) * (1.0 / ch)
     var = jnp.sum(centered * centered, 0, keepdims=True) * (1.0 / ch)
-    out = centered * lax.rsqrt(var + epsilon)
-    return (out if gain is None else out * gain).astype(BF16)
-
-
-def gate_of(x, w_ref, gain_ref, s):
-    w = (w_ref[s].astype(F32).T * gain_ref[s : s + 1]).astype(BF16)
-    return 0.5 + 0.5 * jnp.tanh(0.5 * dot(w, norm_down(x, None), 1, 0))
+    return (centered * lax.rsqrt(var + epsilon)).astype(BF16)
+
+
+def gate_of(normed, w_ref, gain_ref, s):
+    w = (w_ref[s].astype(F32).T * (0.5 * gain_ref[s : s + 1])).astype(BF16)
+    return 0.5 + 0.5 * jnp.tanh(dot(w, normed, 1, 0))
 
 
 def first_gate_kernel(x_ref, w_ref, gain_ref, turned_ref, gate_ref):
     rows, cols, ch = x_ref.shape
     turned = jnp.concatenate([x_ref[i].astype(F32).T for i in range(rows)], 1)
     turned_ref[...] = turned.astype(BF16)
-    gate_ref[...] = gate_of(turned, w_ref, gain_ref, 0)
+    gate_ref[...] = gate_of(norm_down(turned), w_ref, gain_ref, 0)
 
 
 def first_gate(x, w, gain):
@@ -88,20 +87,6 @@
         compiler_params=params(32),
         cost_estimate=cost(2 * rows * cols * ch * ch, 8 * rows * cols * ch),
         name="first_gate",
-    )(x, w, gain)
-
-
-def second_gate_kernel(x_ref, w_ref, gain_ref, gate_ref):
-    gate_ref[...] = gate_of(x_ref[...].astype(F32), w_ref, gain_ref, 1)
-
-
-def second_gate(x, w, gain):
-    return pl.pallas_call(
-        second_gate_kernel,
-        out_shape=jax.ShapeDtypeStruct(x.shape, F32),
-        compiler_params=params(32),
-        cost_estimate=cost(2 * x.size * x.shape[0], 6 * x.size),
-        name="second_gate",
     )(x, w, gain)
 
 
@@ -173,7 +158,7 @@
     ]
 
 
-def middle_kernel(p_ref, pair_ref, gate_ref, whole_ref, mid_ref, out_ref, tmp, tmp2):
+def middle_kernel(p_ref, pair_ref, gate_ref, whole_ref, gw_ref, gain_ref, mid_ref, gate2_ref, out_ref, tmp, tmp2):
     ch, rows, cols = p_ref.shape
     tiles = whole_ref.shape[0]
     share = ch // tiles
@@ -183,11 +168,12 @@
         lanes = slice(i * cols, (i + 1) * cols)
         mid = (pair_ref[:, lanes].astype(F32) + gate_ref[:, lanes] * updates[i]).astype(BF16)
         mid_ref[:, lanes] = mid
-        normed.append(norm_down(mid.astype(F32), None))
+        normed.append(norm_down(mid.astype(F32)))
     weights = jnp.concatenate(
         [whole_ref[q, a * share : (a + 1) * share] for a in range(4) for q in range(tiles)], 0
     )
-    parts = dot(weights, jnp.concatenate(normed, 1), 1, 0)
+    normed = jnp.concatenate(normed, 1)
+    parts = dot(weights, normed, 1, 0)
     for i in range(rows):
         lanes = slice(i * cols, (i + 1) * cols)
         for s in range(2):
@@ -197,20 +183,22 @@
                 tmp2[s, pl.ds(q * rows + i, share, stride=tiles * rows), :] = both[q * share : (q + 1) * share]
     for s in range(2):
         out_ref[:, s] = tmp2[s].reshape(ch, rows, cols).astype(BF16)
-
-
-def middle_step(p, pair, gate, whole):
+    gate2_ref[...] = gate_of(normed, gw_ref, gain_ref, 1)
+
+
+def middle_step(p, pair, gate, whole, gate_weight, in_gain):
     ch, rows, cols = p.shape
     return pl.pallas_call(
         middle_kernel,
         out_shape=(
             jax.ShapeDtypeStruct(pair.shape, BF16),
+            jax.ShapeDtypeStruct(pair.shape, F32),
             jax.ShapeDtypeStruct((ch, 2, rows, cols), BF16),
         ),
         scratch_shapes=[pltpu.VMEM((ch * rows, cols), F32), pltpu.VMEM((2, ch * rows, cols), F32)],
         compiler_params=params(32),
         name="middle_step",
-    )(p, pair, gate, whole)
+    )(p, pair, gate, whole, gate_weight, in_gain)
 
 
 def last_kernel(p_ref, mid_ref, gate_ref, whole_ref, out_ref, tmp):
@@ -231,6 +219,18 @@
         compiler_params=params(32),
         name="last_step",
     )(p, mid, gate, whole)
+
+
+def gather_small(x, axis):
+    n = lax.axis_size(axis)
+    me = lax.axis_index(axis)
+    parts = [x] + [lax.ppermute(x, axis, [(i, i ^ k) for i in range(n)]) for k in range(1, n)]
+    bit = 1
+    while bit < n:
+        swap = (me & bit) != 0
+        parts = [jnp.where(swap, parts[k ^ bit], parts[k]) for k in range(n)]
+        bit *= 2
+    return jnp.stack(parts)
 
 
 def on_device(pair_rep, proj_weight, gate_weight, out_weight, in_gain, out_gain):
@@ -250,7 +250,7 @@
     later = (turned[1].astype(F32) * (0.5 * gain[1])).astype(BF16).reshape(4 * share, ch)
     scaled = (out_weight.astype(F32) * out_gain[:, :, None]).astype(BF16).reshape(2 * share, ch)
     packed = jnp.concatenate([later, scaled], 0)
-    whole = lax.all_gather(packed, "chan", axis=0, tiled=False)
+    whole = gather_small(packed, "chan")
     own = lax.dynamic_slice_in_dim(pair_rep, lax.axis_index("chan") * cols, cols, 1)
     own, gate = first_gate(own, gate_weight, in_gain)
 
@@ -258,8 +258,7 @@
     halves, whole, own, gate = lax.optimization_barrier((halves, whole, own, gate))
     product = outgoing(halves, tiles).reshape(blocks * tiles, rows, cols)
     product = lax.all_to_all(product, everywhere, 0, 0, tiled=True)
-    mid, halves = middle_step(product, own, gate, whole)
-    gate = second_gate(mid, gate_weight, in_gain)
+    mid, gate, halves = middle_step(product, own, gate, whole, gate_weight, in_gain)
     halves = lax.all_to_all(halves, everywhere, 0, 0, tiled=True)
 
     product = incoming(halves.reshape(blocks, tiles, 2, rows, cols)).reshape(blocks * tiles, rows, cols)

time: 101 us -> 100 us (0.990)
  waiting for transfers between devices: 13.3 us -> 10.8 us
  blocking collectives: 59.3 us -> 61.6 us
  Pallas kernels: 13.1 us -> 12 us
    all_to_all x1 -> x2, blocking collectives: 21.1 us -> 38.6 us  [on_device(): product = lax.all_to_all(product, everywhere, 0, 0, tiled=True)]
    all_gather x1 -> x0, blocking collectives: 15 us -> none  [on_device(): whole = lax.all_gather(packed, 'chan', axis=0, tiled=False)]
    all_to_all x1 -> x0, waiting for transfers between devices: 13.3 us -> none  [on_device(): product = lax.all_to_all(product, everywhere, 0, 0, tiled=True)]
    ppermute x0 -> x3, waiting for transfers between devices: none -> 10.8 us  [gather_small(): lax.ppermute(x, axis, [(i, i ^ k) for i in range(n)])]
    ppermute x0 -> x3, starting transfers between devices: none -> 4.26 us  [gather_small(): lax.ppermute(x, axis, [(i, i ^ k) for i in range(n)])]
    all_to_all x1 -> x0, starting transfers between devices: 4.07 us -> none  [on_device(): product = lax.all_to_all(product, everywhere, 0, 0, tiled=True)]
  transfers between devices with their start and end apart: 2 -> 4, of which waited for: 1 -> 2; matrix products, arithmetic and copies ran while one was open for 1% -> 1% of each run, Pallas kernels for 1% -> 1%
where the time goes in v3:
time: 100 us
  blocking collectives  61.6 us (62%)
  starting transfers between devices  14.2 us (14%)
  Pallas kernels  12 us (12%)
  waiting for transfers between devices  10.8 us (11%)
  local copies, waits for them, and re-layouts  1.1 us (1%)
    all_to_all x2, blocking collectives, on_device(): product = lax.all_to_all(product, everywhere, 0, 0, tiled=True)  38.6 us
    all_to_all x1, blocking collectives, on_device(): halves = lax.all_to_all(halves, everywhere, 0, 0, tiled=True)  23.1 us
    ppermute x3, waiting for transfers between devices, gather_small(): lax.ppermute(x, axis, [(i, i ^ k) for i in range(n)])  10.8 us
    all_to_all x1, starting transfers between devices, on_device(): halves = lax.all_to_all(halves, 'blk', 0, 0, tiled=True)  9.94 us
    pallas_call x1, Pallas kernels, project(): pl.pallas_call(project_kernel, grid=(width // cols,), in_specs=[pl.BlockS...  4.94 us
    ppermute x3, starting transfers between devices, gather_small(): lax.ppermute(x, axis, [(i, i ^ k) for i in range(n)])  4.26 us
    pallas_call x1, Pallas kernels, middle_step(): pl.pallas_call(middle_kernel, out_shape=(jax.ShapeDtypeStruct(pair.shape,...  3.31 us
  transfers between devices with their start and end apart: 4, of which 2 were waited for; matrix products, arithmetic and copies ran while one was open for 1% of the time, Pallas kernels for 1%

profile of v3, /device:TPU:1, one launch (start us, length us, event | category | flops | bytes accessed | tf_op | source)
XLA Modules:
  0.0 100.0 jit_solution(12561313342658179495)
XLA Ops:
  0.0 0.0 copy-start.2
  0.0 0.0 copy-start.3
  0.0 0.0 copy-start.4
  0.0 0.0 copy-start.1
  0.0 4.9 %project_rows.1 = bf16[32,2,16,512]{3,2,1,0:T(8,128)(2,1)} custom-call(bf16[16,512,128]{2,1,0:T(8,128)(2,1)} %x_ref.1, bf16[2,4,32,128]{3,2,1,0:T(8,128)(2,1)} %bitcast.21, f32[2,128]{1,0:T(2,128)} %gain_ref.5), custom_call_target="tpu_custom_call" | custom-call | tf_op jit(solution)/shard_map/project_rows/pallas_call | solution.py:48
  5.0 0.0 copy-start
  5.0 9.9 %all-to-all-start = ((bf16[32,2,16,512]{3,2,1,0:T(8,128)(2,1)}), bf16[32,2,16,512]{3,2,1,0:T(8,128)(2,1)S(1)}, u32[]{:S(2)}, u32[]{:S(2)}) async-start(bf16[32,2,16,512]{3,2,1,0:T(8,128)(2,1)} %project_rows.1), calls=%async_computation | async-start | bytes 2097152 | tf_op jit(solution)/shard_map/all_to_all | solution.py:257
  14.9 0.0 copy-done.2
  14.9 0.0 copy-done.3
  14.9 0.0 copy-done.4
  15.0 0.1 multiply_convert_fusion
  15.0 0.0 copy-done.1
  15.1 1.0 %collective-permute-start.2 = (bf16[192,128]{1,0:T(8,128)(2,1)S(1)}, bf16[192,128]{1,0:T(8,128)(2,1)S(1)}, u32[]{:S(2)}, u32[]{:S(2)}) collective-permute-start(bf16[192,128]{1,0:T(8,128)(2,1)S(1)} %pad_maximum_fusion.1), channel_id=1, source_target_pairs={{0,1},{1,0},{2,3},{3,2},{4,5},{5,4},{6,7},{7,6},{8,9},{9,8},{10,11... | collective-permute-start | bytes 147464 | tf_op jit(solution)/shard_map/ppermute | solution.py:227
  16.1 2.5 %collective-permute-start.1 = (bf16[192,128]{1,0:T(8,128)(2,1)S(1)}, bf16[192,128]{1,0:T(8,128)(2,1)S(1)}, u32[]{:S(2)}, u32[]{:S(2)}) collective-permute-start(bf16[192,128]{1,0:T(8,128)(2,1)S(1)} %pad_maximum_fusion.1), channel_id=1, source_target_pairs={{0,2},{1,3},{2,0},{3,1},{4,6},{5,7},{6,4},{7,5},{8,10},{9,11},{10,... | collective-permute-start | bytes 147464 | tf_op jit(solution)/shard_map/ppermute | solution.py:227
  18.6 0.8 collective-permute-start
  19.3 1.1 %constant_dynamic-slice_fusion.x_ref = bf16[16,128,128]{2,1,0:T(8,128)(2,1)S(1)} fusion(bf16[16,512,128]{2,1,0:T(8,128)(2,1)} %x_ref.1, s32[]{:T(128)S(6)} %select_n.51), kind=kLoop, calls=%fused_computation.14 | loop fusion | bytes 1048580 | tf_op jit(solution)/shard_map/dynamic_slice | solution.py:254
  20.4 0.0 copy-done
  20.4 0.7 first_gate.1
  21.1 0.0 collective-permute-done.2
  21.1 8.6 %collective-permute-done.1 = bf16[192,128]{1,0:T(8,128)(2,1)S(1)} collective-permute-done((bf16[192,128]{1,0:T(8,128)(2,1)S(1)}, bf16[192,128]{1,0:T(8,128)(2,1)S(1)}, u32[]{:S(2)}, u32[]{:S(2)}) %collective-permute-start.1) | collective-permute-done | bytes 49184 | tf_op jit(solution)/shard_map/ppermute | solution.py:227
  29.7 2.2 %collective-permute-done = bf16[192,128]{1,0:T(8,128)(2,1)S(1)} collective-permute-done((bf16[192,128]{1,0:T(8,128)(2,1)S(1)}, bf16[192,128]{1,0:T(8,128)(2,1)S(1)}, u32[]{:S(2)}, u32[]{:S(2)}) %collective-permute-start) | collective-permute-done | bytes 49184 | tf_op jit(solution)/shard_map/ppermute | solution.py:227
  31.9 0.1 select_bitcast_fusion.3
  32.0 0.0 all-to-all-done.x_ref
  32.0 0.7 outgoing_product.1
  32.7 20.8 %all_to_all.20.p_ref = bf16[128,16,128]{2,1,0:T(8,128)(2,1)S(1)} all-to-all(bf16[128,16,128]{2,1,0:T(8,128)(2,1)S(1)} %bitcast.19), channel_id=1, replica_groups=mesh['blk'=32,'chan'=4] {'blk','chan'}, dimensions={0} | all-to-all | bytes 1048576 | tf_op jit(solution)/shard_map/all_to_all | solution.py:260
  53.6 3.3 %middle_step.1 = (bf16[128,2048]{1,0:T(8,128)(2,1)S(1)}, f32[128,2048]{1,0:T(8,128)S(1)}, bf16[128,2,16,128]{3,2,1,0:T(8,128)(2,1)S(1)}) custom-call(bf16[128,16,128]{2,1,0:T(8,128)(2,1)S(1)} %all_to_all.20.p_ref, bf16[128,2048]{1,0:T(8,128)(2,1)S(1)} %get-tuple-element.27.pair_ref, f32[128,2048]{1,0:T(8,128)S(1)} %get-tuple-element.28.gate_ref, ...), custom_call_target="tpu_custom_call" | custom-call | tf_op jit(solution)/shard_map/middle_step/pallas_call | solution.py:191
  56.9 23.1 %all_to_all.21 = bf16[128,2,16,128]{3,2,1,0:T(8,128)(2,1)S(1)} all-to-all(bf16[128,2,16,128]{3,2,1,0:T(8,128)(2,1)S(1)} %get-tuple-element.30), channel_id=1, replica_groups=mesh['blk'=32,'chan'=4] {'blk','chan'}, dimensions={0} | all-to-all | bytes 2097152 | tf_op jit(solution)/shard_map/all_to_all | solution.py:262
  80.0 0.5 incoming_product.1
  80.5 17.7 %all_to_all.22.p_ref = bf16[128,16,128]{2,1,0:T(8,128)(2,1)S(1)} all-to-all(bf16[128,16,128]{2,1,0:T(8,128)(2,1)S(1)} %bitcast.20), channel_id=1, replica_groups=mesh['blk'=32,'chan'=4] {'blk','chan'}, dimensions={0} | all-to-all | bytes 1048576 | tf_op jit(solution)/shard_map/all_to_all | solution.py:265
  98.2 1.9 %last_step.1 = bf16[16,128,128]{2,1,0:T(8,128)(2,1)} custom-call(bf16[128,16,128]{2,1,0:T(8,128)(2,1)S(1)} %all_to_all.22.p_ref, bf16[128,2048]{1,0:T(8,128)(2,1)S(1)} %get-tuple-element.31.mid_ref, f32[128,2048]{1,0:T(8,128)S(1)} %get-tuple-element.32.gate_ref, bf16[4,192,128]{2,1,0:T(8,128)(2,1)S(1)} %pad_maximum_fusion.whole_ref), custom_call_target="tpu_custom_call" | custom-call | tf_op jit(solution)/shard_map/last_step/pallas_call | solution.py:215
  (5 shorter events, 0.1 us)
Async XLA Ops:
  0.0 14.9 %copy-start.2 = (bf16[2,4,128,32]{2,3,1,0:T(8,128)(2,1)S(1)}, bf16[2,4,128,32]{2,3,1,0:T(8,128)(2,1)}, u32[]{:S(2)}) copy-start(bf16[2,4,128,32]{2,3,1,0:T(8,128)(2,1)} %param.7) | copy-start | bytes 196612
  0.0 14.9 %copy-start.3 = (bf16[2,32,128]{2,1,0:T(8,128)(2,1)S(1)}, bf16[2,32,128]{2,1,0:T(8,128)(2,1)}, u32[]{:S(2)}) copy-start(bf16[2,32,128]{2,1,0:T(8,128)(2,1)} %param.9) | copy-start | bytes 49156
  0.0 14.9 %copy-start.4 = (f32[2,32]{1,0:T(2,128)S(1)}, f32[2,32]{1,0:T(2,128)}, u32[]{:S(2)}) copy-start(f32[2,32]{1,0:T(2,128)} %param.11) | copy-start | bytes 772
  0.0 15.0 %copy-start.1 = (f32[2,128]{1,0:T(2,128)S(1)}, f32[2,128]{1,0:T(2,128)}, u32[]{:S(2)}) copy-start(f32[2,128]{1,0:T(2,128)} %gain_ref.5) | copy-start | bytes 3076
  5.0 15.5 %copy-start = (bf16[2,128,128]{2,1,0:T(8,128)(2,1)S(1)}, bf16[2,128,128]{2,1,0:T(8,128)(2,1)}, u32[]{:S(2)}) copy-start(bf16[2,128,128]{2,1,0:T(8,128)(2,1)} %gw_ref.1) | copy-start | bytes 196612
  5.0 27.0 %all-to-all-start = ((bf16[32,2,16,512]{3,2,1,0:T(8,128)(2,1)}), bf16[32,2,16,512]{3,2,1,0:T(8,128)(2,1)S(1)}, u32[]{:S(2)}, u32[]{:S(2)}) async-start(bf16[32,2,16,512]{3,2,1,0:T(8,128)(2,1)} %project_rows.1), calls=%async_computation | async-start | bytes 2097152 | tf_op jit(solution)/shard_map/all_to_all | solution.py:257
  15.1 6.0 %collective-permute-start.2 = (bf16[192,128]{1,0:T(8,128)(2,1)S(1)}, bf16[192,128]{1,0:T(8,128)(2,1)S(1)}, u32[]{:S(2)}, u32[]{:S(2)}) collective-permute-start(bf16[192,128]{1,0:T(8,128)(2,1)S(1)} %pad_maximum_fusion.1), channel_id=1, source_target_pairs={{0,1},{1,0},{2,3},{3,2},{4,5},{5,4},{6,7},{7,6},{8,9},{9,8},{10,11... | collective-permute-start | bytes 147464 | tf_op jit(solution)/shard_map/ppermute | solution.py:227
  16.1 13.6 %collective-permute-start.1 = (bf16[192,128]{1,0:T(8,128)(2,1)S(1)}, bf16[192,128]{1,0:T(8,128)(2,1)S(1)}, u32[]{:S(2)}, u32[]{:S(2)}) collective-permute-start(bf16[192,128]{1,0:T(8,128)(2,1)S(1)} %pad_maximum_fusion.1), channel_id=1, source_target_pairs={{0,2},{1,3},{2,0},{3,1},{4,6},{5,7},{6,4},{7,5},{8,10},{9,11},{10,... | collective-permute-start | bytes 147464 | tf_op jit(solution)/shard_map/ppermute | solution.py:227
  18.6 13.3 %collective-permute-start = (bf16[192,128]{1,0:T(8,128)(2,1)S(1)}, bf16[192,128]{1,0:T(8,128)(2,1)S(1)}, u32[]{:S(2)}, u32[]{:S(2)}) collective-permute-start(bf16[192,128]{1,0:T(8,128)(2,1)S(1)} %pad_maximum_fusion.1), channel_id=1, source_target_pairs={{0,3},{1,2},{2,1},{3,0},{4,7},{5,6},{6,5},{7,4},{8,11},{9,10},{10,... | collective-permute-start | bytes 147464 | tf_op jit(solution)/shard_map/ppermute | solution.py:227

commit v4 on v3

--- a/solution.py
+++ b/solution.py
@@ -23,7 +23,12 @@
     return lax.dot_general(a, b, (((ca,), (cb,)), ((), ())), preferred_element_type=F32)
 
 
-def project_kernel(x_ref, w_ref, gain_ref, out_ref, tmp):
+def stacked(x, rows):
+    cols = x.shape[1] // rows
+    return jnp.swapaxes(jnp.stack([x[:, i * cols : (i + 1) * cols] for i in range(rows)], 0), 0, 1)
+
+
+def project_kernel(x_ref, w_ref, gain_ref, out_ref):
     rows, cols, ch = x_ref.shape
     share = out_ref.shape[0]
     weights = (w_ref[0].reshape(4 * share, ch).astype(F32) * gain_ref[0:1]).astype(BF16)
@@ -32,26 +37,22 @@
     var = jnp.sum(centered * centered, 0, keepdims=True) * (1.0 / ch)
     scale = jnp.broadcast_to(0.5 * lax.rsqrt(var + epsilon), (share, rows * cols))
     parts = dot(weights, centered.astype(BF16), 1, 0)
-    for i in range(rows):
-        lanes = slice(i * cols, (i + 1) * cols)
-        for s in range(2):
-            value = parts[2 * s * share : (2 * s + 1) * share, lanes] * scale[:, lanes]
-            gate = jnp.tanh(parts[(2 * s + 1) * share : (2 * s + 2) * share, lanes] * scale[:, lanes])
-            tmp[s, pl.ds(i, share, stride=rows), :] = value + value * gate
     for s in range(2):
-        out_ref[:, s] = tmp[s].reshape(share, rows, cols).astype(BF16)
-
-
-def project(x, w, gain, cols):
+        value = parts[2 * s * share : (2 * s + 1) * share] * scale
+        gate = jnp.tanh(parts[(2 * s + 1) * share : (2 * s + 2) * share] * scale)
+        out_ref[:, s] = stacked((value + value * gate).astype(BF16), rows)
+
+
+def project(x, w, gain):
     rows, width, ch = x.shape
     share = w.shape[2]
+    cols = width // 2
     return pl.pallas_call(
         project_kernel,
         grid=(width // cols,),
         in_specs=[pl.BlockSpec((rows, cols, ch), lambda t: (0, t, 0)), WHOLE, WHOLE],
         out_specs=pl.BlockSpec((share, 2, rows, cols), lambda t: (0, 0, 0, t)),
         out_shape=jax.ShapeDtypeStruct((share, 2, rows, width), BF16),
-        scratch_shapes=[pltpu.VMEM((2, share * rows, cols), F32)],
         compiler_params=params(60),
         name="project_rows",
     )(x, w, gain)
@@ -132,57 +133,36 @@
     )(x)
 
 
-def update_of(p_ref, whole_ref, s, tmp):
+def update_of(p_ref, weights):
     ch, rows, cols = p_ref.shape
-    tiles = whole_ref.shape[0]
-    share = ch // tiles
     p = p_ref[...].astype(F32)
-    tmp[...] = p.reshape(ch * rows, cols)
     mean = jnp.sum(p, 0) * (1.0 / ch)
     square = jnp.sum(p * p, 0) * (1.0 / ch)
     scale = lax.rsqrt(square - mean * mean + epsilon)
-    weights = jnp.concatenate(
-        [whole_ref[q, (4 + s) * share : (5 + s) * share] for q in range(tiles)], 0
-    )
     columns = dot(weights, jnp.ones((ch, cols), BF16), 0, 0)
-    row = [
-        jnp.concatenate(
-            [tmp[pl.ds(q * rows + i, share, stride=tiles * rows), :] for q in range(tiles)], 0
-        ).astype(BF16)
-        for i in range(rows)
-    ]
-    summed = dot(weights, jnp.concatenate(row, 1), 0, 0)
+    by_row = jnp.swapaxes(p_ref[...], 0, 1)
+    summed = dot(weights, jnp.concatenate([by_row[i] for i in range(rows)], 1), 0, 0)
     return [
         (summed[:, i * cols : (i + 1) * cols] - columns * mean[i : i + 1]) * scale[i : i + 1]
         for i in range(rows)
     ]
 
 
-def middle_kernel(p_ref, pair_ref, gate_ref, whole_ref, gw_ref, gain_ref, mid_ref, gate2_ref, out_ref, tmp, tmp2):
+def middle_kernel(p_ref, pair_ref, gate_ref, whole_ref, gw_ref, gain_ref, mid_ref, gate2_ref, out_ref):
     ch, rows, cols = p_ref.shape
-    tiles = whole_ref.shape[0]
-    share = ch // tiles
-    updates = update_of(p_ref, whole_ref, 0, tmp)
+    updates = update_of(p_ref, whole_ref[4])
     normed = []
     for i in range(rows):
         lanes = slice(i * cols, (i + 1) * cols)
         mid = (pair_ref[:, lanes].astype(F32) + gate_ref[:, lanes] * updates[i]).astype(BF16)
         mid_ref[:, lanes] = mid
         normed.append(norm_down(mid.astype(F32)))
-    weights = jnp.concatenate(
-        [whole_ref[q, a * share : (a + 1) * share] for a in range(4) for q in range(tiles)], 0
-    )
     normed = jnp.concatenate(normed, 1)
-    parts = dot(weights, normed, 1, 0)
-    for i in range(rows):
-        lanes = slice(i * cols, (i + 1) * cols)
-        for s in range(2):
-            value = parts[2 * s * ch : (2 * s + 1) * ch, lanes]
-            both = value + value * jnp.tanh(parts[(2 * s + 1) * ch : (2 * s + 2) * ch, lanes])
-            for q in range(tiles):
-                tmp2[s, pl.ds(q * rows + i, share, stride=tiles * rows), :] = both[q * share : (q + 1) * share]
+    parts = dot(whole_ref[:4].reshape(4 * ch, ch), normed, 1, 0)
     for s in range(2):
-        out_ref[:, s] = tmp2[s].reshape(ch, rows, cols).astype(BF16)
+        value = parts[2 * s * ch : (2 * s + 1) * ch]
+        gate = jnp.tanh(parts[(2 * s + 1) * ch : (2 * s + 2) * ch])
+        out_ref[:, s] = stacked((value + value * gate).astype(BF16), rows)
     gate2_ref[...] = gate_of(normed, gw_ref, gain_ref, 1)
 
 
@@ -195,19 +175,18 @@
             jax.ShapeDtypeStruct(pair.shape, F32),
             jax.ShapeDtypeStruct((ch, 2, rows, cols), BF16),
         ),
-        scratch_shapes=[pltpu.VMEM((ch * rows, cols), F32), pltpu.VMEM((2, ch * rows, cols), F32)],
         compiler_params=params(32),
         name="middle_step",
     )(p, pair, gate, whole, gate_weight, in_gain)
 
 
-def last_kernel(p_ref, mid_ref, gate_ref, whole_ref, out_ref, tmp):
+def last_kernel(p_ref, mid_ref, gate_ref, whole_ref, out_ref):
     ch, rows, cols = p_ref.shape
-    updates = update_of(p_ref, whole_ref, 1, tmp)
+    updates = update_of(p_ref, whole_ref[5])
     for i in range(rows):
         lanes = slice(i * cols, (i + 1) * cols)
         out = mid_ref[:, lanes].astype(F32) + gate_ref[:, lanes] * updates[i]
-        out_ref[i] = out.T.astype(BF16)
+        out_ref[i] = out.astype(BF16).T
 
 
 def last_step(p, mid, gate, whole):
@@ -215,7 +194,6 @@
     return pl.pallas_call(
         last_kernel,
         out_shape=jax.ShapeDtypeStruct((rows, cols, mid.shape[0]), BF16),
-        scratch_shapes=[pltpu.VMEM((ch * rows, cols), F32)],
         compiler_params=params(32),
         name="last_step",
     )(p, mid, gate, whole)
@@ -230,7 +208,7 @@
         swap = (me & bit) != 0
         parts = [jnp.where(swap, parts[k ^ bit], parts[k]) for k in range(n)]
         bit *= 2
-    return jnp.stack(parts)
+    return jnp.stack(parts, -2)
 
 
 def on_device(pair_rep, proj_weight, gate_weight, out_weight, in_gain, out_gain):
@@ -242,15 +220,15 @@
     everywhere = ("blk", "chan")
 
     turned = jnp.transpose(proj_weight, (0, 1, 3, 2))
-    halves = project(pair_rep, turned, in_gain, cols)
+    halves = project(pair_rep, turned, in_gain)
 
     turned, out_weight, out_gain, gain, halves = lax.optimization_barrier(
         (turned, out_weight, out_gain, in_gain, halves)
     )
-    later = (turned[1].astype(F32) * (0.5 * gain[1])).astype(BF16).reshape(4 * share, ch)
-    scaled = (out_weight.astype(F32) * out_gain[:, :, None]).astype(BF16).reshape(2 * share, ch)
-    packed = jnp.concatenate([later, scaled], 0)
-    whole = gather_small(packed, "chan")
+    later = (turned[1].astype(F32) * (0.5 * gain[1])).astype(BF16)
+    scaled = (out_weight.astype(F32) * out_gain[:, :, None]).astype(BF16)
+    whole = gather_small(jnp.concatenate([later, scaled], 0), "chan")
+    whole = whole.reshape(6, share * tiles, ch)
     own = lax.dynamic_slice_in_dim(pair_rep, lax.axis_index("chan") * cols, cols, 1)
     own, gate = first_gate(own, gate_weight, in_gain)
 

time: 100 us -> 97.9 us (0.979)
  Pallas kernels: 12 us -> 9.37 us
    pallas_call x1, Pallas kernels: 3.31 us -> 1.68 us  [middle_step(): pl.pallas_call(middle_kernel, out_shape=(jax.ShapeDtypeStruct(pair.shape,...]
where the time goes in v4:
time: 97.9 us; the launch traced here: 97.6 us
  blocking collectives  61.6 us (63%)
  starting transfers between devices  14.2 us (15%)
  waiting for transfers between devices  10.8 us (11%)
  Pallas kernels  9.37 us (10%)
  local copies, waits for them, and re-layouts  1.25 us (1%)
    all_to_all x2, blocking collectives, on_device(): product = lax.all_to_all(product, everywhere, 0, 0, tiled=True)  38.6 us
    all_to_all x1, blocking collectives, on_device(): halves = lax.all_to_all(halves, everywhere, 0, 0, tiled=True)  23.1 us
    ppermute x3, waiting for transfers between devices, gather_small(): lax.ppermute(x, axis, [(i, i ^ k) for i in range(n)])  10.8 us
    all_to_all x1, starting transfers between devices, on_device(): halves = lax.all_to_all(halves, 'blk', 0, 0, tiled=True)  9.94 us
    pallas_call x1, Pallas kernels, project(): pl.pallas_call(project_kernel, grid=(width // cols,), in_specs=[pl.BlockS...  4.52 us
    ppermute x3, starting transfers between devices, gather_small(): lax.ppermute(x, axis, [(i, i ^ k) for i in range(n)])  4.26 us
  transfers between devices with their start and end apart: 4, of which 2 were waited for; matrix products, arithmetic and copies ran while one was open for 1% of the time, Pallas kernels for 1%

profile of v4, /device:TPU:1, one launch (start us, length us, event | category | flops | bytes accessed | tf_op | source)
XLA Modules:
  0.0 97.6 jit_solution(17711299155782595852)
XLA Ops:
  0.0 0.0 copy-start.3
  0.0 0.0 copy-start.4
  0.0 0.0 copy-start.1
  0.0 0.0 copy-start.2
  0.0 4.5 %project_rows.1 = bf16[32,2,16,512]{3,2,1,0:T(8,128)(2,1)} custom-call(bf16[16,512,128]{2,1,0:T(8,128)(2,1)} %x_ref.1, bf16[2,4,32,128]{3,2,1,0:T(8,128)(2,1)} %bitcast.23, f32[2,128]{1,0:T(2,128)} %gain_ref.5), custom_call_target="tpu_custom_call" | custom-call | tf_op jit(solution)/shard_map/project_rows/pallas_call | solution.py:50
  4.5 0.0 copy-start
  4.5 9.9 %all-to-all-start = ((bf16[32,2,16,512]{3,2,1,0:T(8,128)(2,1)}), bf16[32,2,16,512]{3,2,1,0:T(8,128)(2,1)S(1)}, u32[]{:S(2)}, u32[]{:S(2)}) async-start(bf16[32,2,16,512]{3,2,1,0:T(8,128)(2,1)} %project_rows.1), calls=%async_computation | async-start | bytes 2097152 | tf_op jit(solution)/shard_map/all_to_all | solution.py:235
  14.5 0.0 copy-done.3
  14.5 0.0 copy-done.4
  14.5 0.1 multiply_convert_fusion
  14.6 0.0 copy-done.1
  14.6 0.0 copy-done.2
  14.6 1.0 %collective-permute-start.2 = (bf16[6,32,128]{2,1,0:T(8,128)(2,1)S(1)}, bf16[6,32,128]{2,1,0:T(8,128)(2,1)S(1)}, u32[]{:S(2)}, u32[]{:S(2)}) collective-permute-start(bf16[6,32,128]{2,1,0:T(8,128)(2,1)S(1)} %pad_maximum_fusion.1), channel_id=1, source_target_pairs={{0,1},{1,0},{2,3},{3,2},{4,5},{5,4},{6,7},{7,6},{8,9},{9,8},{10,11... | collective-permute-start | bytes 147464 | tf_op jit(solution)/shard_map/ppermute | solution.py:205
  15.7 2.5 %collective-permute-start.1 = (bf16[6,32,128]{2,1,0:T(8,128)(2,1)S(1)}, bf16[6,32,128]{2,1,0:T(8,128)(2,1)S(1)}, u32[]{:S(2)}, u32[]{:S(2)}) collective-permute-start(bf16[6,32,128]{2,1,0:T(8,128)(2,1)S(1)} %pad_maximum_fusion.1), channel_id=1, source_target_pairs={{0,2},{1,3},{2,0},{3,1},{4,6},{5,7},{6,4},{7,5},{8,10},{9,11},{10,... | collective-permute-start | bytes 147464 | tf_op jit(solution)/shard_map/ppermute | solution.py:205
  18.1 0.8 collective-permute-start
  18.9 1.1 %constant_dynamic-slice_fusion.x_ref = bf16[16,128,128]{2,1,0:T(8,128)(2,1)S(1)} fusion(bf16[16,512,128]{2,1,0:T(8,128)(2,1)} %x_ref.1, s32[]{:T(128)S(6)} %select_n.51), kind=kLoop, calls=%fused_computation.14 | loop fusion | bytes 1048580 | tf_op jit(solution)/shard_map/dynamic_slice | solution.py:232
  20.0 0.0 copy-done
  20.0 0.7 first_gate.1
  20.7 0.0 collective-permute-done.2
  20.7 8.6 %collective-permute-done.1 = bf16[6,32,128]{2,1,0:T(8,128)(2,1)S(1)} collective-permute-done((bf16[6,32,128]{2,1,0:T(8,128)(2,1)S(1)}, bf16[6,32,128]{2,1,0:T(8,128)(2,1)S(1)}, u32[]{:S(2)}, u32[]{:S(2)}) %collective-permute-start.1) | collective-permute-done | bytes 49184 | tf_op jit(solution)/shard_map/ppermute | solution.py:205
  29.3 2.2 %collective-permute-done = bf16[6,32,128]{2,1,0:T(8,128)(2,1)S(1)} collective-permute-done((bf16[6,32,128]{2,1,0:T(8,128)(2,1)S(1)}, bf16[6,32,128]{2,1,0:T(8,128)(2,1)S(1)}, u32[]{:S(2)}, u32[]{:S(2)}) %collective-permute-start) | collective-permute-done | bytes 49184 | tf_op jit(solution)/shard_map/ppermute | solution.py:205
  31.5 0.2 copy.7
  31.7 0.0 all-to-all-done.x_ref
  31.7 0.7 outgoing_product.1
  32.4 20.9 %all_to_all.20.p_ref = bf16[128,16,128]{2,1,0:T(8,128)(2,1)S(1)} all-to-all(bf16[128,16,128]{2,1,0:T(8,128)(2,1)S(1)} %bitcast.19), channel_id=1, replica_groups=mesh['blk'=32,'chan'=4] {'blk','chan'}, dimensions={0} | all-to-all | bytes 1048576 | tf_op jit(solution)/shard_map/all_to_all | solution.py:238
  53.3 1.7 %middle_step.1 = (bf16[128,2048]{1,0:T(8,128)(2,1)S(1)}, f32[128,2048]{1,0:T(8,128)S(1)}, bf16[128,2,16,128]{3,2,1,0:T(8,128)(2,1)S(1)}) custom-call(bf16[128,16,128]{2,1,0:T(8,128)(2,1)S(1)} %all_to_all.20.p_ref, bf16[128,2048]{1,0:T(8,128)(2,1)S(1)} %get-tuple-element.27.pair_ref, f32[128,2048]{1,0:T(8,128)S(1)} %get-tuple-element.28.gate_ref, ...), custom_call_target="tpu_custom_call" | custom-call | tf_op jit(solution)/shard_map/middle_step/pallas_call | solution.py:171
  55.0 23.1 %all_to_all.21 = bf16[128,2,16,128]{3,2,1,0:T(8,128)(2,1)S(1)} all-to-all(bf16[128,2,16,128]{3,2,1,0:T(8,128)(2,1)S(1)} %get-tuple-element.30), channel_id=1, replica_groups=mesh['blk'=32,'chan'=4] {'blk','chan'}, dimensions={0} | all-to-all | bytes 2097152 | tf_op jit(solution)/shard_map/all_to_all | solution.py:240
  78.0 0.5 incoming_product.1
  78.5 17.7 %all_to_all.22.p_ref = bf16[128,16,128]{2,1,0:T(8,128)(2,1)S(1)} all-to-all(bf16[128,16,128]{2,1,0:T(8,128)(2,1)S(1)} %bitcast.20), channel_id=1, replica_groups=mesh['blk'=32,'chan'=4] {'blk','chan'}, dimensions={0} | all-to-all | bytes 1048576 | tf_op jit(solution)/shard_map/all_to_all | solution.py:243
  96.2 1.3 %last_step.1 = bf16[16,128,128]{2,1,0:T(8,128)(2,1)} custom-call(bf16[128,16,128]{2,1,0:T(8,128)(2,1)S(1)} %all_to_all.22.p_ref, bf16[128,2048]{1,0:T(8,128)(2,1)S(1)} %get-tuple-element.31.mid_ref, f32[128,2048]{1,0:T(8,128)S(1)} %get-tuple-element.32.gate_ref, bf16[6,128,128]{2,1,0:T(8,128)(2,1)S(1)} %bitcast.22), custom_call_target="tpu_custom_call" | custom-call | tf_op jit(solution)/shard_map/last_step/pallas_call | solution.py:194
  (5 shorter events, 0.1 us)
Async XLA Ops:
  0.0 14.5 %copy-start.3 = (bf16[2,32,128]{2,1,0:T(8,128)(2,1)S(1)}, bf16[2,32,128]{2,1,0:T(8,128)(2,1)}, u32[]{:S(2)}) copy-start(bf16[2,32,128]{2,1,0:T(8,128)(2,1)} %param.9) | copy-start | bytes 49156
  0.0 14.5 %copy-start.4 = (f32[2,32]{1,0:T(2,128)S(1)}, f32[2,32]{1,0:T(2,128)}, u32[]{:S(2)}) copy-start(f32[2,32]{1,0:T(2,128)} %param.11) | copy-start | bytes 772
  0.0 14.6 %copy-start.1 = (f32[2,128]{1,0:T(2,128)S(1)}, f32[2,128]{1,0:T(2,128)}, u32[]{:S(2)}) copy-start(f32[2,128]{1,0:T(2,128)} %gain_ref.5) | copy-start | bytes 3076
  0.0 14.6 %copy-start.2 = (bf16[2,4,128,32]{2,3,1,0:T(8,128)(2,1)S(1)}, bf16[2,4,128,32]{2,3,1,0:T(8,128)(2,1)}, u32[]{:S(2)}) copy-start(bf16[2,4,128,32]{2,3,1,0:T(8,128)(2,1)} %param.7) | copy-start | bytes 196612
  4.5 15.5 %copy-start = (bf16[2,128,128]{2,1,0:T(8,128)(2,1)S(1)}, bf16[2,128,128]{2,1,0:T(8,128)(2,1)}, u32[]{:S(2)}) copy-start(bf16[2,128,128]{2,1,0:T(8,128)(2,1)} %gw_ref.1) | copy-start | bytes 196612
  4.5 27.2 %all-to-all-start = ((bf16[32,2,16,512]{3,2,1,0:T(8,128)(2,1)}), bf16[32,2,16,512]{3,2,1,0:T(8,128)(2,1)S(1)}, u32[]{:S(2)}, u32[]{:S(2)}) async-start(bf16[32,2,16,512]{3,2,1,0:T(8,128)(2,1)} %project_rows.1), calls=%async_computation | async-start | bytes 2097152 | tf_op jit(solution)/shard_map/all_to_all | solution.py:235
  14.6 6.0 %collective-permute-start.2 = (bf16[6,32,128]{2,1,0:T(8,128)(2,1)S(1)}, bf16[6,32,128]{2,1,0:T(8,128)(2,1)S(1)}, u32[]{:S(2)}, u32[]{:S(2)}) collective-permute-start(bf16[6,32,128]{2,1,0:T(8,128)(2,1)S(1)} %pad_maximum_fusion.1), channel_id=1, source_target_pairs={{0,1},{1,0},{2,3},{3,2},{4,5},{5,4},{6,7},{7,6},{8,9},{9,8},{10,11... | collective-permute-start | bytes 147464 | tf_op jit(solution)/shard_map/ppermute | solution.py:205
  15.7 13.6 %collective-permute-start.1 = (bf16[6,32,128]{2,1,0:T(8,128)(2,1)S(1)}, bf16[6,32,128]{2,1,0:T(8,128)(2,1)S(1)}, u32[]{:S(2)}, u32[]{:S(2)}) collective-permute-start(bf16[6,32,128]{2,1,0:T(8,128)(2,1)S(1)} %pad_maximum_fusion.1), channel_id=1, source_target_pairs={{0,2},{1,3},{2,0},{3,1},{4,6},{5,7},{6,4},{7,5},{8,10},{9,11},{10,... | collective-permute-start | bytes 147464 | tf_op jit(solution)/shard_map/ppermute | solution.py:205
  18.1 13.3 %collective-permute-start = (bf16[6,32,128]{2,1,0:T(8,128)(2,1)S(1)}, bf16[6,32,128]{2,1,0:T(8,128)(2,1)S(1)}, u32[]{:S(2)}, u32[]{:S(2)}) collective-permute-start(bf16[6,32,128]{2,1,0:T(8,128)(2,1)S(1)} %pad_maximum_fusion.1), channel_id=1, source_target_pairs={{0,3},{1,2},{2,1},{3,0},{4,7},{5,6},{6,5},{7,4},{8,11},{9,10},{10,... | collective-permute-start | bytes 147464 | tf_op jit(solution)/shard_map/ppermute | solution.py:205

commit v5 on v4

--- a/solution.py
+++ b/solution.py
@@ -199,10 +199,15 @@
     )(p, mid, gate, whole)
 
 
-def gather_small(x, axis):
-    n = lax.axis_size(axis)
-    me = lax.axis_index(axis)
-    parts = [x] + [lax.ppermute(x, axis, [(i, i ^ k) for i in range(n)]) for k in range(1, n)]
+def gather_chan(x):
+    n = lax.axis_size("chan")
+    me = lax.axis_index("chan")
+    far = n * lax.axis_size("blk") // 2
+    parts = [x]
+    for k in range(1, n):
+        step = k ^ far if k & 2 else k
+        pairs = [(i, i ^ step) for i in range(2 * far)]
+        parts.append(lax.ppermute(x, ("blk", "chan"), pairs))
     bit = 1
     while bit < n:
         swap = (me & bit) != 0
@@ -227,7 +232,7 @@
     )
     later = (turned[1].astype(F32) * (0.5 * gain[1])).astype(BF16)
     scaled = (out_weight.astype(F32) * out_gain[:, :, None]).astype(BF16)
-    whole = gather_small(jnp.concatenate([later, scaled], 0), "chan")
+    whole = gather_chan(jnp.concatenate([later, scaled], 0))
     whole = whole.reshape(6, share * tiles, ch)
     own = lax.dynamic_slice_in_dim(pair_rep, lax.axis_index("chan") * cols, cols, 1)
     own, gate = first_gate(own, gate_weight, in_gain)

time: 97.9 us -> 96.6 us (0.987)
  waiting for transfers between devices: 10.8 us -> 8.74 us
  blocking collectives: 61.6 us -> 62.7 us
    ppermute x3, waiting for transfers between devices: 10.8 us -> 3.3 us  [gather_chan(): parts.append(lax.ppermute(x, ('blk', 'chan'), pairs))]
    all_to_all x1, waiting for transfers between devices: 0.01 us -> 5.43 us  [on_device(): halves = lax.all_to_all(halves, 'blk', 0, 0, tiled=True)]
    all_to_all x2, blocking collectives: 38.6 us -> 39.6 us  [on_device(): product = lax.all_to_all(product, everywhere, 0, 0, tiled=True)]
where the time goes in v5:
time: 96.6 us; the launch traced here: 96.3 us
  blocking collectives  62.7 us (65%)
  starting transfers between devices  13.9 us (14%)
  Pallas kernels  9.36 us (10%)
  waiting for transfers between devices  8.74 us (9%)
  local copies, waits for them, and re-layouts  1.25 us (1%)
    all_to_all x2, blocking collectives, on_device(): product = lax.all_to_all(product, everywhere, 0, 0, tiled=True)  39.6 us
    all_to_all x1, blocking collectives, on_device(): halves = lax.all_to_all(halves, everywhere, 0, 0, tiled=True)  23.1 us
    all_to_all x1, starting transfers between devices, on_device(): halves = lax.all_to_all(halves, 'blk', 0, 0, tiled=True)  9.94 us
    all_to_all x1, waiting for transfers between devices, on_device(): halves = lax.all_to_all(halves, 'blk', 0, 0, tiled=True)  5.43 us
    pallas_call x1, Pallas kernels, project(): pl.pallas_call(project_kernel, grid=(width // cols,), in_specs=[pl.BlockS...  4.52 us
    ppermute x3, starting transfers between devices, gather_chan(): parts.append(lax.ppermute(x, ('blk', 'chan'), pairs))  3.97 us
    ppermute x3, waiting for transfers between devices, gather_chan(): parts.append(lax.ppermute(x, ('blk', 'chan'), pairs))  3.3 us
  transfers between devices with their start and end apart: 4, of which 2 were waited for; matrix products, arithmetic and copies ran while one was open for 1% of the time, Pallas kernels for 1%

profile of v5, /device:TPU:1, one launch (start us, length us, event | category | flops | bytes accessed | tf_op | source)
XLA Modules:
  0.0 96.3 jit_solution(1599328582995783889)
XLA Ops:
  0.0 0.0 copy-start.3
  0.0 0.0 copy-start.4
  0.0 0.0 copy-start.1
  0.0 0.0 copy-start.2
  0.0 4.5 %project_rows.1 = bf16[32,2,16,512]{3,2,1,0:T(8,128)(2,1)} custom-call(bf16[16,512,128]{2,1,0:T(8,128)(2,1)} %x_ref.1, bf16[2,4,32,128]{3,2,1,0:T(8,128)(2,1)} %bitcast.23, f32[2,128]{1,0:T(2,128)} %gain_ref.5), custom_call_target="tpu_custom_call" | custom-call | tf_op jit(solution)/shard_map/project_rows/pallas_call | solution.py:50
  4.5 0.0 copy-start
  4.5 9.9 %all-to-all-start = ((bf16[32,2,16,512]{3,2,1,0:T(8,128)(2,1)}), bf16[32,2,16,512]{3,2,1,0:T(8,128)(2,1)S(1)}, u32[]{:S(2)}, u32[]{:S(2)}) async-start(bf16[32,2,16,512]{3,2,1,0:T(8,128)(2,1)} %project_rows.1), calls=%async_computation | async-start | bytes 2097152 | tf_op jit(solution)/shard_map/all_to_all | solution.py:240
  14.5 0.0 copy-done.3
  14.5 0.0 copy-done.4
  14.5 0.1 multiply_convert_fusion
  14.6 0.0 copy-done.1
  14.6 0.0 copy-done.2
  14.6 1.0 %collective-permute-start.2 = (bf16[6,32,128]{2,1,0:T(8,128)(2,1)S(1)}, bf16[6,32,128]{2,1,0:T(8,128)(2,1)S(1)}, u32[]{:S(2)}, u32[]{:S(2)}) collective-permute-start(bf16[6,32,128]{2,1,0:T(8,128)(2,1)S(1)} %pad_maximum_fusion.1), channel_id=1, source_target_pairs={{0,1},{1,0},{2,3},{3,2},{4,5},{5,4},{6,7},{7,6},{8,9},{9,8},{10,11... | collective-permute-start | bytes 147464 | tf_op jit(solution)/shard_map/ppermute | solution.py:210
  15.7 2.8 %collective-permute-start.1 = (bf16[6,32,128]{2,1,0:T(8,128)(2,1)S(1)}, bf16[6,32,128]{2,1,0:T(8,128)(2,1)S(1)}, u32[]{:S(2)}, u32[]{:S(2)}) collective-permute-start(bf16[6,32,128]{2,1,0:T(8,128)(2,1)S(1)} %pad_maximum_fusion.1), channel_id=1, source_target_pairs={{0,66},{1,67},{2,64},{3,65},{4,70},{5,71},{6,68},{7,69},{8,74},{9,... | collective-permute-start | bytes 147464 | tf_op jit(solution)/shard_map/ppermute | solution.py:210
  18.5 0.1 collective-permute-start
  18.6 1.1 %constant_dynamic-slice_fusion.x_ref = bf16[16,128,128]{2,1,0:T(8,128)(2,1)S(1)} fusion(bf16[16,512,128]{2,1,0:T(8,128)(2,1)} %x_ref.1, s32[]{:T(128)S(6)} %select_n.51), kind=kLoop, calls=%fused_computation.14 | loop fusion | bytes 1048580 | tf_op jit(solution)/shard_map/dynamic_slice | solution.py:237
  19.7 0.0 copy-done
  19.7 0.7 first_gate.1
  20.4 0.0 collective-permute-done.2
  20.4 0.0 collective-permute-done.1
  20.4 3.3 %collective-permute-done = bf16[6,32,128]{2,1,0:T(8,128)(2,1)S(1)} collective-permute-done((bf16[6,32,128]{2,1,0:T(8,128)(2,1)S(1)}, bf16[6,32,128]{2,1,0:T(8,128)(2,1)S(1)}, u32[]{:S(2)}, u32[]{:S(2)}) %collective-permute-start) | collective-permute-done | bytes 49184 | tf_op jit(solution)/shard_map/ppermute | solution.py:210
  23.8 0.2 copy.7
  23.9 5.4 %all-to-all-done.x_ref = bf16[32,2,16,512]{3,2,1,0:T(8,128)(2,1)S(1)} async-done(((bf16[32,2,16,512]{3,2,1,0:T(8,128)(2,1)}), bf16[32,2,16,512]{3,2,1,0:T(8,128)(2,1)S(1)}, u32[]{:S(2)}, u32[]{:S(2)}) %all-to-all-start) | async-done | bytes 1048608 | tf_op jit(solution)/shard_map/all_to_all | solution.py:240
  29.4 0.7 outgoing_product.1
  30.1 21.9 %all_to_all.20.p_ref = bf16[128,16,128]{2,1,0:T(8,128)(2,1)S(1)} all-to-all(bf16[128,16,128]{2,1,0:T(8,128)(2,1)S(1)} %bitcast.19), channel_id=1, replica_groups=mesh['blk'=32,'chan'=4] {'blk','chan'}, dimensions={0} | all-to-all | bytes 1048576 | tf_op jit(solution)/shard_map/all_to_all | solution.py:243
  52.0 1.7 %middle_step.1 = (bf16[128,2048]{1,0:T(8,128)(2,1)S(1)}, f32[128,2048]{1,0:T(8,128)S(1)}, bf16[128,2,16,128]{3,2,1,0:T(8,128)(2,1)S(1)}) custom-call(bf16[128,16,128]{2,1,0:T(8,128)(2,1)S(1)} %all_to_all.20.p_ref, bf16[128,2048]{1,0:T(8,128)(2,1)S(1)} %get-tuple-element.27.pair_ref, f32[128,2048]{1,0:T(8,128)S(1)} %get-tuple-element.28.gate_ref, ...), custom_call_target="tpu_custom_call" | custom-call | tf_op jit(solution)/shard_map/middle_step/pallas_call | solution.py:171
  53.7 23.1 %all_to_all.21 = bf16[128,2,16,128]{3,2,1,0:T(8,128)(2,1)S(1)} all-to-all(bf16[128,2,16,128]{3,2,1,0:T(8,128)(2,1)S(1)} %get-tuple-element.30), channel_id=1, replica_groups=mesh['blk'=32,'chan'=4] {'blk','chan'}, dimensions={0} | all-to-all | bytes 2097152 | tf_op jit(solution)/shard_map/all_to_all | solution.py:245
  76.7 0.5 incoming_product.1
  77.2 17.7 %all_to_all.22.p_ref = bf16[128,16,128]{2,1,0:T(8,128)(2,1)S(1)} all-to-all(bf16[128,16,128]{2,1,0:T(8,128)(2,1)S(1)} %bitcast.20), channel_id=1, replica_groups=mesh['blk'=32,'chan'=4] {'blk','chan'}, dimensions={0} | all-to-all | bytes 1048576 | tf_op jit(solution)/shard_map/all_to_all | solution.py:248
  95.0 1.3 %last_step.1 = bf16[16,128,128]{2,1,0:T(8,128)(2,1)} custom-call(bf16[128,16,128]{2,1,0:T(8,128)(2,1)S(1)} %all_to_all.22.p_ref, bf16[128,2048]{1,0:T(8,128)(2,1)S(1)} %get-tuple-element.31.mid_ref, f32[128,2048]{1,0:T(8,128)S(1)} %get-tuple-element.32.gate_ref, bf16[6,128,128]{2,1,0:T(8,128)(2,1)S(1)} %bitcast.22), custom_call_target="tpu_custom_call" | custom-call | tf_op jit(solution)/shard_map/last_step/pallas_call | solution.py:194
  (5 shorter events, 0.1 us)
Async XLA Ops:
  0.0 14.5 %copy-start.3 = (bf16[2,32,128]{2,1,0:T(8,128)(2,1)S(1)}, bf16[2,32,128]{2,1,0:T(8,128)(2,1)}, u32[]{:S(2)}) copy-start(bf16[2,32,128]{2,1,0:T(8,128)(2,1)} %param.9) | copy-start | bytes 49156
  0.0 14.5 %copy-start.4 = (f32[2,32]{1,0:T(2,128)S(1)}, f32[2,32]{1,0:T(2,128)}, u32[]{:S(2)}) copy-start(f32[2,32]{1,0:T(2,128)} %param.11) | copy-start | bytes 772
  0.0 14.6 %copy-start.1 = (f32[2,128]{1,0:T(2,128)S(1)}, f32[2,128]{1,0:T(2,128)}, u32[]{:S(2)}) copy-start(f32[2,128]{1,0:T(2,128)} %gain_ref.5) | copy-start | bytes 3076
  0.0 14.6 %copy-start.2 = (bf16[2,4,128,32]{2,3,1,0:T(8,128)(2,1)S(1)}, bf16[2,4,128,32]{2,3,1,0:T(8,128)(2,1)}, u32[]{:S(2)}) copy-start(bf16[2,4,128,32]{2,3,1,0:T(8,128)(2,1)} %param.7) | copy-start | bytes 196612
  4.5 15.2 %copy-start = (bf16[2,128,128]{2,1,0:T(8,128)(2,1)S(1)}, bf16[2,128,128]{2,1,0:T(8,128)(2,1)}, u32[]{:S(2)}) copy-start(bf16[2,128,128]{2,1,0:T(8,128)(2,1)} %gw_ref.1) | copy-start | bytes 196612
  4.5 24.8 %all-to-all-start = ((bf16[32,2,16,512]{3,2,1,0:T(8,128)(2,1)}), bf16[32,2,16,512]{3,2,1,0:T(8,128)(2,1)S(1)}, u32[]{:S(2)}, u32[]{:S(2)}) async-start(bf16[32,2,16,512]{3,2,1,0:T(8,128)(2,1)} %project_rows.1), calls=%async_computation | async-start | bytes 2097152 | tf_op jit(solution)/shard_map/all_to_all | solution.py:240
  14.6 5.7 %collective-permute-start.2 = (bf16[6,32,128]{2,1,0:T(8,128)(2,1)S(1)}, bf16[6,32,128]{2,1,0:T(8,128)(2,1)S(1)}, u32[]{:S(2)}, u32[]{:S(2)}) collective-permute-start(bf16[6,32,128]{2,1,0:T(8,128)(2,1)S(1)} %pad_maximum_fusion.1), channel_id=1, source_target_pairs={{0,1},{1,0},{2,3},{3,2},{4,5},{5,4},{6,7},{7,6},{8,9},{9,8},{10,11... | collective-permute-start | bytes 147464 | tf_op jit(solution)/shard_map/ppermute | solution.py:210
  15.7 4.7 %collective-permute-start.1 = (bf16[6,32,128]{2,1,0:T(8,128)(2,1)S(1)}, bf16[6,32,128]{2,1,0:T(8,128)(2,1)S(1)}, u32[]{:S(2)}, u32[]{:S(2)}) collective-permute-start(bf16[6,32,128]{2,1,0:T(8,128)(2,1)S(1)} %pad_maximum_fusion.1), channel_id=1, source_target_pairs={{0,66},{1,67},{2,64},{3,65},{4,70},{5,71},{6,68},{7,69},{8,74},{9,... | collective-permute-start | bytes 147464 | tf_op jit(solution)/shard_map/ppermute | solution.py:210
  18.5 5.2 %collective-permute-start = (bf16[6,32,128]{2,1,0:T(8,128)(2,1)S(1)}, bf16[6,32,128]{2,1,0:T(8,128)(2,1)S(1)}, u32[]{:S(2)}, u32[]{:S(2)}) collective-permute-start(bf16[6,32,128]{2,1,0:T(8,128)(2,1)S(1)} %pad_maximum_fusion.1), channel_id=1, source_target_pairs={{0,67},{1,66},{2,65},{3,64},{4,71},{5,70},{6,69},{7,68},{8,75},{9,... | collective-permute-start | bytes 147464 | tf_op jit(solution)/shard_map/ppermute | solution.py:210

commit v6 on v5

--- a/solution.py
+++ b/solution.py
@@ -23,6 +23,16 @@
     return lax.dot_general(a, b, (((ca,), (cb,)), ((), ())), preferred_element_type=F32)
 
 
+def center_down(x):
+    ch = x.shape[0]
+    eye = lax.broadcasted_iota(jnp.int32, (ch, ch), 0) == lax.broadcasted_iota(jnp.int32, (ch, ch), 1)
+    center = (jnp.where(eye, 1.0, 0.0) - 1.0 / ch).astype(BF16)
+    centered = dot(center, x, 1, 0)
+    rounded = centered.astype(BF16)
+    var = dot(jnp.full((16, ch), 1.0 / ch, BF16), rounded * rounded, 1, 0)[:8]
+    return centered, var
+
+
 def stacked(x, rows):
     cols = x.shape[1] // rows
     return jnp.swapaxes(jnp.stack([x[:, i * cols : (i + 1) * cols] for i in range(rows)], 0), 0, 1)
@@ -32,10 +42,10 @@
     rows, cols, ch = x_ref.shape
     share = out_ref.shape[0]
     weights = (w_ref[0].reshape(4 * share, ch).astype(F32) * gain_ref[0:1]).astype(BF16)
-    x = jnp.concatenate([x_ref[i].T for i in range(rows)], 1).astype(F32)
-    centered = x - jnp.sum(x, 0, keepdims=True) * (1.0 / ch)
-    var = jnp.sum(centered * centered, 0, keepdims=True) * (1.0 / ch)
-    scale = jnp.broadcast_to(0.5 * lax.rsqrt(var + epsilon), (share, rows * cols))
+    x = jnp.concatenate([x_ref[i].T for i in range(rows)], 1)
+    centered, var = center_down(x)
+    scale = 0.5 * lax.rsqrt(var + epsilon)
+    scale = jnp.concatenate([scale] * (share // scale.shape[0]), 0)
     parts = dot(weights, centered.astype(BF16), 1, 0)
     for s in range(2):
         value = parts[2 * s * share : (2 * s + 1) * share] * scale
@@ -59,10 +69,8 @@
 
 
 def norm_down(x):
-    ch = x.shape[0]
-    centered = x - jnp.sum(x, 0, keepdims=True) * (1.0 / ch)
-    var = jnp.sum(centered * centered, 0, keepdims=True) * (1.0 / ch)
-    return (centered * lax.rsqrt(var + epsilon)).astype(BF16)
+    centered, var = center_down(x)
+    return (centered * lax.rsqrt(var[:1] + epsilon)).astype(BF16)
 
 
 def gate_of(normed, w_ref, gain_ref, s):
@@ -72,8 +80,8 @@
 
 def first_gate_kernel(x_ref, w_ref, gain_ref, turned_ref, gate_ref):
     rows, cols, ch = x_ref.shape
-    turned = jnp.concatenate([x_ref[i].astype(F32).T for i in range(rows)], 1)
-    turned_ref[...] = turned.astype(BF16)
+    turned = jnp.concatenate([x_ref[i].T for i in range(rows)], 1)
+    turned_ref[...] = turned
     gate_ref[...] = gate_of(norm_down(turned), w_ref, gain_ref, 0)
 
 
@@ -95,10 +103,10 @@
     blocks, _, rows, n = x_ref.shape
     tiles, cols = out_ref.shape[1], out_ref.shape[3]
     left = x_ref[:, 0].reshape(blocks * rows, n)
-    per = cols // rows
+    right = x_ref[:, 1].reshape(blocks * rows, n)
+    product = dot(left, right, 1, 1).astype(BF16)
     for q in range(tiles):
-        right = x_ref[q * per : (q + 1) * per, 1].reshape(cols, n)
-        out_ref[:, q] = dot(left, right, 1, 1).reshape(blocks, rows, cols).astype(BF16)
+        out_ref[:, q] = product[:, q * cols : (q + 1) * cols].reshape(blocks, rows, cols)
 
 
 def outgoing(x, tiles):
@@ -138,7 +146,7 @@
     p = p_ref[...].astype(F32)
     mean = jnp.sum(p, 0) * (1.0 / ch)
     square = jnp.sum(p * p, 0) * (1.0 / ch)
-    scale = lax.rsqrt(square - mean * mean + epsilon)
+    scale = lax.rsqrt(jnp.maximum(square - mean * mean, 0.0) + epsilon)
     columns = dot(weights, jnp.ones((ch, cols), BF16), 0, 0)
     by_row = jnp.swapaxes(p_ref[...], 0, 1)
     summed = dot(weights, jnp.concatenate([by_row[i] for i in range(rows)], 1), 0, 0)
@@ -151,13 +159,13 @@
 def middle_kernel(p_ref, pair_ref, gate_ref, whole_ref, gw_ref, gain_ref, mid_ref, gate2_ref, out_ref):
     ch, rows, cols = p_ref.shape
     updates = update_of(p_ref, whole_ref[4])
-    normed = []
+    mids = []
     for i in range(rows):
         lanes = slice(i * cols, (i + 1) * cols)
         mid = (pair_ref[:, lanes].astype(F32) + gate_ref[:, lanes] * updates[i]).astype(BF16)
         mid_ref[:, lanes] = mid
-        normed.append(norm_down(mid.astype(F32)))
-    normed = jnp.concatenate(normed, 1)
+        mids.append(mid)
+    normed = norm_down(jnp.concatenate(mids, 1))
     parts = dot(whole_ref[:4].reshape(4 * ch, ch), normed, 1, 0)
     for s in range(2):
         value = parts[2 * s * ch : (2 * s + 1) * ch]

time: 96.6 us -> 96.3 us (level)
  no operation moved by 1% of the time
where the time goes in v6:
time: 96.3 us; the launch traced here: 96 us
  blocking collectives  62.7 us (65%)
  starting transfers between devices  13.9 us (14%)
  Pallas kernels  9.08 us (9%)
  waiting for transfers between devices  8.7 us (9%)
  local copies, waits for them, and re-layouts  1.25 us (1%)
    all_to_all x2, blocking collectives, on_device(): product = lax.all_to_all(product, everywhere, 0, 0, tiled=True)  39.7 us
    all_to_all x1, blocking collectives, on_device(): halves = lax.all_to_all(halves, everywhere, 0, 0, tiled=True)  23.1 us
    all_to_all x1, starting transfers between devices, on_device(): halves = lax.all_to_all(halves, 'blk', 0, 0, tiled=True)  9.94 us
    all_to_all x1, waiting for transfers between devices, on_device(): halves = lax.all_to_all(halves, 'blk', 0, 0, tiled=True)  5.43 us
    pallas_call x1, Pallas kernels, project(): pl.pallas_call(project_kernel, grid=(width // cols,), in_specs=[pl.BlockS...  4.37 us
    ppermute x3, starting transfers between devices, gather_chan(): parts.append(lax.ppermute(x, ('blk', 'chan'), pairs))  3.97 us
    ppermute x3, waiting for transfers between devices, gather_chan(): parts.append(lax.ppermute(x, ('blk', 'chan'), pairs))  3.27 us
  transfers between devices with their start and end apart: 4, of which 2 were waited for; matrix products, arithmetic and copies ran while one was open for 1% of the time, Pallas kernels for 1%

profile of v6, /device:TPU:1, one launch (start us, length us, event | category | flops | bytes accessed | tf_op | source)
XLA Modules:
  0.0 96.0 jit_solution(15301688722572461884)
XLA Ops:
  0.0 0.0 copy-start.3
  0.0 0.0 copy-start.4
  0.0 0.0 copy-start.1
  0.0 0.0 copy-start.2
  0.0 4.4 %project_rows.1 = bf16[32,2,16,512]{3,2,1,0:T(8,128)(2,1)} custom-call(bf16[16,512,128]{2,1,0:T(8,128)(2,1)} %x_ref.1, bf16[2,4,32,128]{3,2,1,0:T(8,128)(2,1)} %bitcast.23, f32[2,128]{1,0:T(2,128)} %gain_ref.5), custom_call_target="tpu_custom_call" | custom-call | tf_op jit(solution)/shard_map/project_rows/pallas_call | solution.py:60
  4.4 0.0 copy-start
  4.4 9.9 %all-to-all-start = ((bf16[32,2,16,512]{3,2,1,0:T(8,128)(2,1)}), bf16[32,2,16,512]{3,2,1,0:T(8,128)(2,1)S(1)}, u32[]{:S(2)}, u32[]{:S(2)}) async-start(bf16[32,2,16,512]{3,2,1,0:T(8,128)(2,1)} %project_rows.1), calls=%async_computation | async-start | bytes 2097152 | tf_op jit(solution)/shard_map/all_to_all | solution.py:248
  14.3 0.0 copy-done.3
  14.4 0.0 copy-done.4
  14.4 0.1 multiply_convert_fusion
  14.4 0.0 copy-done.1
  14.5 0.0 copy-done.2
  14.5 1.0 %collective-permute-start.2 = (bf16[6,32,128]{2,1,0:T(8,128)(2,1)S(1)}, bf16[6,32,128]{2,1,0:T(8,128)(2,1)S(1)}, u32[]{:S(2)}, u32[]{:S(2)}) collective-permute-start(bf16[6,32,128]{2,1,0:T(8,128)(2,1)S(1)} %pad_maximum_fusion.1), channel_id=1, source_target_pairs={{0,1},{1,0},{2,3},{3,2},{4,5},{5,4},{6,7},{7,6},{8,9},{9,8},{10,11... | collective-permute-start | bytes 147464 | tf_op jit(solution)/shard_map/ppermute | solution.py:218
  15.5 2.8 %collective-permute-start.1 = (bf16[6,32,128]{2,1,0:T(8,128)(2,1)S(1)}, bf16[6,32,128]{2,1,0:T(8,128)(2,1)S(1)}, u32[]{:S(2)}, u32[]{:S(2)}) collective-permute-start(bf16[6,32,128]{2,1,0:T(8,128)(2,1)S(1)} %pad_maximum_fusion.1), channel_id=1, source_target_pairs={{0,66},{1,67},{2,64},{3,65},{4,70},{5,71},{6,68},{7,69},{8,74},{9,... | collective-permute-start | bytes 147464 | tf_op jit(solution)/shard_map/ppermute | solution.py:218
  18.3 0.1 collective-permute-start
  18.5 1.1 %constant_dynamic-slice_fusion.x_ref = bf16[16,128,128]{2,1,0:T(8,128)(2,1)S(1)} fusion(bf16[16,512,128]{2,1,0:T(8,128)(2,1)} %x_ref.1, s32[]{:T(128)S(6)} %select_n.51), kind=kLoop, calls=%fused_computation.14 | loop fusion | bytes 1048580 | tf_op jit(solution)/shard_map/dynamic_slice | solution.py:245
  19.6 0.0 copy-done
  19.6 0.7 first_gate.1
  20.3 0.0 collective-permute-done.2
  20.3 0.0 collective-permute-done.1
  20.3 3.3 %collective-permute-done = bf16[6,32,128]{2,1,0:T(8,128)(2,1)S(1)} collective-permute-done((bf16[6,32,128]{2,1,0:T(8,128)(2,1)S(1)}, bf16[6,32,128]{2,1,0:T(8,128)(2,1)S(1)}, u32[]{:S(2)}, u32[]{:S(2)}) %collective-permute-start) | collective-permute-done | bytes 49184 | tf_op jit(solution)/shard_map/ppermute | solution.py:218
  23.6 0.2 copy.7
  23.8 5.4 %all-to-all-done.x_ref = bf16[32,2,16,512]{3,2,1,0:T(8,128)(2,1)S(1)} async-done(((bf16[32,2,16,512]{3,2,1,0:T(8,128)(2,1)}), bf16[32,2,16,512]{3,2,1,0:T(8,128)(2,1)S(1)}, u32[]{:S(2)}, u32[]{:S(2)}) %all-to-all-start) | async-done | bytes 1048608 | tf_op jit(solution)/shard_map/all_to_all | solution.py:248
  29.2 0.5 outgoing_product.1
  29.7 21.9 %all_to_all.20.p_ref = bf16[128,16,128]{2,1,0:T(8,128)(2,1)S(1)} all-to-all(bf16[128,16,128]{2,1,0:T(8,128)(2,1)S(1)} %bitcast.19), channel_id=1, replica_groups=mesh['blk'=32,'chan'=4] {'blk','chan'}, dimensions={0} | all-to-all | bytes 1048576 | tf_op jit(solution)/shard_map/all_to_all | solution.py:251
  51.6 1.7 %middle_step.1 = (bf16[128,2048]{1,0:T(8,128)(2,1)S(1)}, f32[128,2048]{1,0:T(8,128)S(1)}, bf16[128,2,16,128]{3,2,1,0:T(8,128)(2,1)S(1)}) custom-call(bf16[128,16,128]{2,1,0:T(8,128)(2,1)S(1)} %all_to_all.20.p_ref, bf16[128,2048]{1,0:T(8,128)(2,1)S(1)} %get-tuple-element.27.pair_ref, f32[128,2048]{1,0:T(8,128)S(1)} %get-tuple-element.28.gate_ref, ...), custom_call_target="tpu_custom_call" | custom-call | tf_op jit(solution)/shard_map/middle_step/pallas_call | solution.py:179
  53.4 23.1 %all_to_all.21 = bf16[128,2,16,128]{3,2,1,0:T(8,128)(2,1)S(1)} all-to-all(bf16[128,2,16,128]{3,2,1,0:T(8,128)(2,1)S(1)} %get-tuple-element.30), channel_id=1, replica_groups=mesh['blk'=32,'chan'=4] {'blk','chan'}, dimensions={0} | all-to-all | bytes 2097152 | tf_op jit(solution)/shard_map/all_to_all | solution.py:253
  76.4 0.5 incoming_product.1
  76.9 17.7 %all_to_all.22.p_ref = bf16[128,16,128]{2,1,0:T(8,128)(2,1)S(1)} all-to-all(bf16[128,16,128]{2,1,0:T(8,128)(2,1)S(1)} %bitcast.20), channel_id=1, replica_groups=mesh['blk'=32,'chan'=4] {'blk','chan'}, dimensions={0} | all-to-all | bytes 1048576 | tf_op jit(solution)/shard_map/all_to_all | solution.py:256
  94.6 1.3 %last_step.1 = bf16[16,128,128]{2,1,0:T(8,128)(2,1)} custom-call(bf16[128,16,128]{2,1,0:T(8,128)(2,1)S(1)} %all_to_all.22.p_ref, bf16[128,2048]{1,0:T(8,128)(2,1)S(1)} %get-tuple-element.31.mid_ref, f32[128,2048]{1,0:T(8,128)S(1)} %get-tuple-element.32.gate_ref, bf16[6,128,128]{2,1,0:T(8,128)(2,1)S(1)} %bitcast.22), custom_call_target="tpu_custom_call" | custom-call | tf_op jit(solution)/shard_map/last_step/pallas_call | solution.py:202
  (5 shorter events, 0.1 us)
Async XLA Ops:
  0.0 14.3 %copy-start.3 = (bf16[2,32,128]{2,1,0:T(8,128)(2,1)S(1)}, bf16[2,32,128]{2,1,0:T(8,128)(2,1)}, u32[]{:S(2)}) copy-start(bf16[2,32,128]{2,1,0:T(8,128)(2,1)} %param.9) | copy-start | bytes 49156
  0.0 14.4 %copy-start.4 = (f32[2,32]{1,0:T(2,128)S(1)}, f32[2,32]{1,0:T(2,128)}, u32[]{:S(2)}) copy-start(f32[2,32]{1,0:T(2,128)} %param.11) | copy-start | bytes 772
  0.0 14.4 %copy-start.1 = (f32[2,128]{1,0:T(2,128)S(1)}, f32[2,128]{1,0:T(2,128)}, u32[]{:S(2)}) copy-start(f32[2,128]{1,0:T(2,128)} %gain_ref.5) | copy-start | bytes 3076
  0.0 14.4 %copy-start.2 = (bf16[2,4,128,32]{2,3,1,0:T(8,128)(2,1)S(1)}, bf16[2,4,128,32]{2,3,1,0:T(8,128)(2,1)}, u32[]{:S(2)}) copy-start(bf16[2,4,128,32]{2,3,1,0:T(8,128)(2,1)} %param.7) | copy-start | bytes 196612
  4.4 15.2 %copy-start = (bf16[2,128,128]{2,1,0:T(8,128)(2,1)S(1)}, bf16[2,128,128]{2,1,0:T(8,128)(2,1)}, u32[]{:S(2)}) copy-start(bf16[2,128,128]{2,1,0:T(8,128)(2,1)} %gw_ref.1) | copy-start | bytes 196612
  4.4 24.8 %all-to-all-start = ((bf16[32,2,16,512]{3,2,1,0:T(8,128)(2,1)}), bf16[32,2,16,512]{3,2,1,0:T(8,128)(2,1)S(1)}, u32[]{:S(2)}, u32[]{:S(2)}) async-start(bf16[32,2,16,512]{3,2,1,0:T(8,128)(2,1)} %project_rows.1), calls=%async_computation | async-start | bytes 2097152 | tf_op jit(solution)/shard_map/all_to_all | solution.py:248
  14.5 5.8 %collective-permute-start.2 = (bf16[6,32,128]{2,1,0:T(8,128)(2,1)S(1)}, bf16[6,32,128]{2,1,0:T(8,128)(2,1)S(1)}, u32[]{:S(2)}, u32[]{:S(2)}) collective-permute-start(bf16[6,32,128]{2,1,0:T(8,128)(2,1)S(1)} %pad_maximum_fusion.1), channel_id=1, source_target_pairs={{0,1},{1,0},{2,3},{3,2},{4,5},{5,4},{6,7},{7,6},{8,9},{9,8},{10,11... | collective-permute-start | bytes 147464 | tf_op jit(solution)/shard_map/ppermute | solution.py:218
  15.5 4.7 %collective-permute-start.1 = (bf16[6,32,128]{2,1,0:T(8,128)(2,1)S(1)}, bf16[6,32,128]{2,1,0:T(8,128)(2,1)S(1)}, u32[]{:S(2)}, u32[]{:S(2)}) collective-permute-start(bf16[6,32,128]{2,1,0:T(8,128)(2,1)S(1)} %pad_maximum_fusion.1), channel_id=1, source_target_pairs={{0,66},{1,67},{2,64},{3,65},{4,70},{5,71},{6,68},{7,69},{8,74},{9,... | collective-permute-start | bytes 147464 | tf_op jit(solution)/shard_map/ppermute | solution.py:218
  18.3 5.2 %collective-permute-start = (bf16[6,32,128]{2,1,0:T(8,128)(2,1)S(1)}, bf16[6,32,128]{2,1,0:T(8,128)(2,1)S(1)}, u32[]{:S(2)}, u32[]{:S(2)}) collective-permute-start(bf16[6,32,128]{2,1,0:T(8,128)(2,1)S(1)} %pad_maximum_fusion.1), channel_id=1, source_target_pairs={{0,67},{1,66},{2,65},{3,64},{4,71},{5,70},{6,69},{7,68},{8,75},{9,... | collective-permute-start | bytes 147464 | tf_op jit(solution)/shard_map/ppermute | solution.py:218

commit v7 on v6

--- a/solution.py
+++ b/solution.py
@@ -165,7 +165,10 @@
         mid = (pair_ref[:, lanes].astype(F32) + gate_ref[:, lanes] * updates[i]).astype(BF16)
         mid_ref[:, lanes] = mid
         mids.append(mid)
-    normed = norm_down(jnp.concatenate(mids, 1))
+    mid = jnp.concatenate(mids, 1).astype(F32)
+    centered = mid - jnp.sum(mid, 0, keepdims=True) * (1.0 / ch)
+    var = jnp.sum(centered * centered, 0, keepdims=True) * (1.0 / ch)
+    normed = (centered * lax.rsqrt(var + epsilon)).astype(BF16)
     parts = dot(whole_ref[:4].reshape(4 * ch, ch), normed, 1, 0)
     for s in range(2):
         value = parts[2 * s * ch : (2 * s + 1) * ch]
@@ -188,20 +191,33 @@
     )(p, pair, gate, whole, gate_weight, in_gain)
 
 
-def last_kernel(p_ref, mid_ref, gate_ref, whole_ref, out_ref):
+def last_kernel(p_ref, mid_ref, gate_ref, whole_ref, out_hbm, buffer, sem):
     ch, rows, cols = p_ref.shape
+    parts = sem.shape[0]
+    per = rows // parts
     updates = update_of(p_ref, whole_ref[5])
-    for i in range(rows):
-        lanes = slice(i * cols, (i + 1) * cols)
-        out = mid_ref[:, lanes].astype(F32) + gate_ref[:, lanes] * updates[i]
-        out_ref[i] = out.astype(BF16).T
+    copies = []
+    for g in range(parts):
+        group = slice(g * per, (g + 1) * per)
+        for i in range(g * per, (g + 1) * per):
+            lanes = slice(i * cols, (i + 1) * cols)
+            out = mid_ref[:, lanes].astype(F32) + gate_ref[:, lanes] * updates[i]
+            buffer[i] = out.astype(BF16).T
+        copies.append(pltpu.make_async_copy(buffer.at[group], out_hbm.at[group], sem.at[g]))
+        copies[-1].start()
+    for copy in copies:
+        copy.wait()
 
 
 def last_step(p, mid, gate, whole):
     ch, rows, cols = p.shape
+    out = (rows, cols, mid.shape[0])
     return pl.pallas_call(
         last_kernel,
-        out_shape=jax.ShapeDtypeStruct((rows, cols, mid.shape[0]), BF16),
+        in_specs=[WHOLE] * 4,
+        out_specs=pl.BlockSpec(memory_space=pl.ANY),
+        out_shape=jax.ShapeDtypeStruct(out, BF16),
+        scratch_shapes=[pltpu.VMEM(out, BF16), pltpu.SemaphoreType.DMA((4,))],
         compiler_params=params(32),
         name="last_step",
     )(p, mid, gate, whole)

time: 96.3 us -> 96.2 us (level)
  no operation moved by 1% of the time
where the time goes in v7:
time: 96.2 us; the launch traced here: 95.8 us
  blocking collectives  62.7 us (65%)
  starting transfers between devices  13.9 us (14%)
  Pallas kernels  8.91 us (9%)
  waiting for transfers between devices  8.7 us (9%)
  local copies, waits for them, and re-layouts  1.25 us (1%)
    all_to_all x2, blocking collectives, on_device(): product = lax.all_to_all(product, everywhere, 0, 0, tiled=True)  39.7 us
    all_to_all x1, blocking collectives, on_device(): halves = lax.all_to_all(halves, everywhere, 0, 0, tiled=True)  23.1 us
    all_to_all x1, starting transfers between devices, on_device(): halves = lax.all_to_all(halves, 'blk', 0, 0, tiled=True)  9.94 us
    all_to_all x1, waiting for transfers between devices, on_device(): halves = lax.all_to_all(halves, 'blk', 0, 0, tiled=True)  5.43 us
    pallas_call x1, Pallas kernels, project(): pl.pallas_call(project_kernel, grid=(width // cols,), in_specs=[pl.BlockS...  4.37 us
    ppermute x3, starting transfers between devices, gather_chan(): parts.append(lax.ppermute(x, ('blk', 'chan'), pairs))  3.97 us
    ppermute x3, waiting for transfers between devices, gather_chan(): parts.append(lax.ppermute(x, ('blk', 'chan'), pairs))  3.27 us
  transfers between devices with their start and end apart: 4, of which 2 were waited for; matrix products, arithmetic and copies ran while one was open for 1% of the time, Pallas kernels for 1%

profile of v7, /device:TPU:1, one launch (start us, length us, event | category | flops | bytes accessed | tf_op | source)
XLA Modules:
  0.0 95.8 jit_solution(14182870708237682245)
XLA Ops:
  0.0 0.0 copy-start.3
  0.0 0.0 copy-start.4
  0.0 0.0 copy-start.1
  0.0 0.0 copy-start.2
  0.0 4.4 %project_rows.1 = bf16[32,2,16,512]{3,2,1,0:T(8,128)(2,1)} custom-call(bf16[16,512,128]{2,1,0:T(8,128)(2,1)} %x_ref.1, bf16[2,4,32,128]{3,2,1,0:T(8,128)(2,1)} %bitcast.23, f32[2,128]{1,0:T(2,128)} %gain_ref.5), custom_call_target="tpu_custom_call" | custom-call | tf_op jit(solution)/shard_map/project_rows/pallas_call | solution.py:60
  4.4 0.0 copy-start
  4.4 9.9 %all-to-all-start = ((bf16[32,2,16,512]{3,2,1,0:T(8,128)(2,1)}), bf16[32,2,16,512]{3,2,1,0:T(8,128)(2,1)S(1)}, u32[]{:S(2)}, u32[]{:S(2)}) async-start(bf16[32,2,16,512]{3,2,1,0:T(8,128)(2,1)} %project_rows.1), calls=%async_computation | async-start | bytes 2097152 | tf_op jit(solution)/shard_map/all_to_all | solution.py:264
  14.3 0.0 copy-done.3
  14.4 0.0 copy-done.4
  14.4 0.1 multiply_convert_fusion
  14.4 0.0 copy-done.1
  14.5 0.0 copy-done.2
  14.5 1.0 %collective-permute-start.2 = (bf16[6,32,128]{2,1,0:T(8,128)(2,1)S(1)}, bf16[6,32,128]{2,1,0:T(8,128)(2,1)S(1)}, u32[]{:S(2)}, u32[]{:S(2)}) collective-permute-start(bf16[6,32,128]{2,1,0:T(8,128)(2,1)S(1)} %pad_maximum_fusion.1), channel_id=1, source_target_pairs={{0,1},{1,0},{2,3},{3,2},{4,5},{5,4},{6,7},{7,6},{8,9},{9,8},{10,11... | collective-permute-start | bytes 147464 | tf_op jit(solution)/shard_map/ppermute | solution.py:234
  15.5 2.8 %collective-permute-start.1 = (bf16[6,32,128]{2,1,0:T(8,128)(2,1)S(1)}, bf16[6,32,128]{2,1,0:T(8,128)(2,1)S(1)}, u32[]{:S(2)}, u32[]{:S(2)}) collective-permute-start(bf16[6,32,128]{2,1,0:T(8,128)(2,1)S(1)} %pad_maximum_fusion.1), channel_id=1, source_target_pairs={{0,66},{1,67},{2,64},{3,65},{4,70},{5,71},{6,68},{7,69},{8,74},{9,... | collective-permute-start | bytes 147464 | tf_op jit(solution)/shard_map/ppermute | solution.py:234
  18.3 0.1 collective-permute-start
  18.5 1.1 %constant_dynamic-slice_fusion.x_ref = bf16[16,128,128]{2,1,0:T(8,128)(2,1)S(1)} fusion(bf16[16,512,128]{2,1,0:T(8,128)(2,1)} %x_ref.1, s32[]{:T(128)S(6)} %select_n.51), kind=kLoop, calls=%fused_computation.14 | loop fusion | bytes 1048580 | tf_op jit(solution)/shard_map/dynamic_slice | solution.py:261
  19.6 0.0 copy-done
  19.6 0.7 first_gate.1
  20.3 0.0 collective-permute-done.2
  20.3 0.0 collective-permute-done.1
  20.3 3.3 %collective-permute-done = bf16[6,32,128]{2,1,0:T(8,128)(2,1)S(1)} collective-permute-done((bf16[6,32,128]{2,1,0:T(8,128)(2,1)S(1)}, bf16[6,32,128]{2,1,0:T(8,128)(2,1)S(1)}, u32[]{:S(2)}, u32[]{:S(2)}) %collective-permute-start) | collective-permute-done | bytes 49184 | tf_op jit(solution)/shard_map/ppermute | solution.py:234
  23.6 0.2 copy.7
  23.8 5.4 %all-to-all-done.x_ref = bf16[32,2,16,512]{3,2,1,0:T(8,128)(2,1)S(1)} async-done(((bf16[32,2,16,512]{3,2,1,0:T(8,128)(2,1)}), bf16[32,2,16,512]{3,2,1,0:T(8,128)(2,1)S(1)}, u32[]{:S(2)}, u32[]{:S(2)}) %all-to-all-start) | async-done | bytes 1048608 | tf_op jit(solution)/shard_map/all_to_all | solution.py:264
  29.2 0.5 outgoing_product.1
  29.7 21.9 %all_to_all.20.p_ref = bf16[128,16,128]{2,1,0:T(8,128)(2,1)S(1)} all-to-all(bf16[128,16,128]{2,1,0:T(8,128)(2,1)S(1)} %bitcast.19), channel_id=1, replica_groups=mesh['blk'=32,'chan'=4] {'blk','chan'}, dimensions={0} | all-to-all | bytes 1048576 | tf_op jit(solution)/shard_map/all_to_all | solution.py:267
  51.6 1.7 %middle_step.1 = (bf16[128,2048]{1,0:T(8,128)(2,1)S(1)}, f32[128,2048]{1,0:T(8,128)S(1)}, bf16[128,2,16,128]{3,2,1,0:T(8,128)(2,1)S(1)}) custom-call(bf16[128,16,128]{2,1,0:T(8,128)(2,1)S(1)} %all_to_all.20.p_ref, bf16[128,2048]{1,0:T(8,128)(2,1)S(1)} %get-tuple-element.27.pair_ref, f32[128,2048]{1,0:T(8,128)S(1)} %get-tuple-element.28.gate_ref, ...), custom_call_target="tpu_custom_call" | custom-call | tf_op jit(solution)/shard_map/middle_step/pallas_call | solution.py:182
  53.3 23.1 %all_to_all.21 = bf16[128,2,16,128]{3,2,1,0:T(8,128)(2,1)S(1)} all-to-all(bf16[128,2,16,128]{3,2,1,0:T(8,128)(2,1)S(1)} %get-tuple-element.30), channel_id=1, replica_groups=mesh['blk'=32,'chan'=4] {'blk','chan'}, dimensions={0} | all-to-all | bytes 2097152 | tf_op jit(solution)/shard_map/all_to_all | solution.py:269
  76.4 0.5 incoming_product.1
  76.8 17.7 %all_to_all.22.p_ref = bf16[128,16,128]{2,1,0:T(8,128)(2,1)S(1)} all-to-all(bf16[128,16,128]{2,1,0:T(8,128)(2,1)S(1)} %bitcast.20), channel_id=1, replica_groups=mesh['blk'=32,'chan'=4] {'blk','chan'}, dimensions={0} | all-to-all | bytes 1048576 | tf_op jit(solution)/shard_map/all_to_all | solution.py:272
  94.6 1.2 %last_step.1 = bf16[16,128,128]{2,1,0:T(8,128)(2,1)} custom-call(bf16[128,16,128]{2,1,0:T(8,128)(2,1)S(1)} %all_to_all.22.p_ref, bf16[128,2048]{1,0:T(8,128)(2,1)S(1)} %get-tuple-element.31.mid_ref, f32[128,2048]{1,0:T(8,128)S(1)} %get-tuple-element.32.gate_ref, bf16[6,128,128]{2,1,0:T(8,128)(2,1)S(1)} %bitcast.22), custom_call_target="tpu_custom_call" | custom-call | tf_op jit(solution)/shard_map/last_step/pallas_call | solution.py:215
  (5 shorter events, 0.1 us)
Async XLA Ops:
  0.0 14.3 %copy-start.3 = (bf16[2,32,128]{2,1,0:T(8,128)(2,1)S(1)}, bf16[2,32,128]{2,1,0:T(8,128)(2,1)}, u32[]{:S(2)}) copy-start(bf16[2,32,128]{2,1,0:T(8,128)(2,1)} %param.9) | copy-start | bytes 49156
  0.0 14.4 %copy-start.4 = (f32[2,32]{1,0:T(2,128)S(1)}, f32[2,32]{1,0:T(2,128)}, u32[]{:S(2)}) copy-start(f32[2,32]{1,0:T(2,128)} %param.11) | copy-start | bytes 772
  0.0 14.4 %copy-start.1 = (f32[2,128]{1,0:T(2,128)S(1)}, f32[2,128]{1,0:T(2,128)}, u32[]{:S(2)}) copy-start(f32[2,128]{1,0:T(2,128)} %gain_ref.5) | copy-start | bytes 3076
  0.0 14.4 %copy-start.2 = (bf16[2,4,128,32]{2,3,1,0:T(8,128)(2,1)S(1)}, bf16[2,4,128,32]{2,3,1,0:T(8,128)(2,1)}, u32[]{:S(2)}) copy-start(bf16[2,4,128,32]{2,3,1,0:T(8,128)(2,1)} %param.7) | copy-start | bytes 196612
  4.4 15.2 %copy-start = (bf16[2,128,128]{2,1,0:T(8,128)(2,1)S(1)}, bf16[2,128,128]{2,1,0:T(8,128)(2,1)}, u32[]{:S(2)}) copy-start(bf16[2,128,128]{2,1,0:T(8,128)(2,1)} %gw_ref.1) | copy-start | bytes 196612
  4.4 24.8 %all-to-all-start = ((bf16[32,2,16,512]{3,2,1,0:T(8,128)(2,1)}), bf16[32,2,16,512]{3,2,1,0:T(8,128)(2,1)S(1)}, u32[]{:S(2)}, u32[]{:S(2)}) async-start(bf16[32,2,16,512]{3,2,1,0:T(8,128)(2,1)} %project_rows.1), calls=%async_computation | async-start | bytes 2097152 | tf_op jit(solution)/shard_map/all_to_all | solution.py:264
  14.5 5.8 %collective-permute-start.2 = (bf16[6,32,128]{2,1,0:T(8,128)(2,1)S(1)}, bf16[6,32,128]{2,1,0:T(8,128)(2,1)S(1)}, u32[]{:S(2)}, u32[]{:S(2)}) collective-permute-start(bf16[6,32,128]{2,1,0:T(8,128)(2,1)S(1)} %pad_maximum_fusion.1), channel_id=1, source_target_pairs={{0,1},{1,0},{2,3},{3,2},{4,5},{5,4},{6,7},{7,6},{8,9},{9,8},{10,11... | collective-permute-start | bytes 147464 | tf_op jit(solution)/shard_map/ppermute | solution.py:234
  15.5 4.7 %collective-permute-start.1 = (bf16[6,32,128]{2,1,0:T(8,128)(2,1)S(1)}, bf16[6,32,128]{2,1,0:T(8,128)(2,1)S(1)}, u32[]{:S(2)}, u32[]{:S(2)}) collective-permute-start(bf16[6,32,128]{2,1,0:T(8,128)(2,1)S(1)} %pad_maximum_fusion.1), channel_id=1, source_target_pairs={{0,66},{1,67},{2,64},{3,65},{4,70},{5,71},{6,68},{7,69},{8,74},{9,... | collective-permute-start | bytes 147464 | tf_op jit(solution)/shard_map/ppermute | solution.py:234
  18.3 5.2 %collective-permute-start = (bf16[6,32,128]{2,1,0:T(8,128)(2,1)S(1)}, bf16[6,32,128]{2,1,0:T(8,128)(2,1)S(1)}, u32[]{:S(2)}, u32[]{:S(2)}) collective-permute-start(bf16[6,32,128]{2,1,0:T(8,128)(2,1)S(1)} %pad_maximum_fusion.1), channel_id=1, source_target_pairs={{0,67},{1,66},{2,65},{3,64},{4,71},{5,70},{6,69},{7,68},{8,75},{9,... | collective-permute-start | bytes 147464 | tf_op jit(solution)/shard_map/ppermute | solution.py:234

commit v8 on v7

--- a/solution.py
+++ b/solution.py
@@ -42,14 +42,14 @@
     rows, cols, ch = x_ref.shape
     share = out_ref.shape[0]
     weights = (w_ref[0].reshape(4 * share, ch).astype(F32) * gain_ref[0:1]).astype(BF16)
-    x = jnp.concatenate([x_ref[i].T for i in range(rows)], 1)
-    centered, var = center_down(x)
+    centered, var = center_down(x_ref[...].reshape(rows * cols, ch).T)
+    centered = centered.astype(BF16)
     scale = 0.5 * lax.rsqrt(var + epsilon)
     scale = jnp.concatenate([scale] * (share // scale.shape[0]), 0)
-    parts = dot(weights, centered.astype(BF16), 1, 0)
     for s in range(2):
-        value = parts[2 * s * share : (2 * s + 1) * share] * scale
-        gate = jnp.tanh(parts[(2 * s + 1) * share : (2 * s + 2) * share] * scale)
+        parts = dot(weights[2 * s * share : (2 * s + 2) * share], centered, 1, 0)
+        value = parts[:share] * scale
+        gate = jnp.tanh(parts[share:] * scale)
         out_ref[:, s] = stacked((value + value * gate).astype(BF16), rows)
 
 
@@ -60,7 +60,11 @@
     return pl.pallas_call(
         project_kernel,
         grid=(width // cols,),
-        in_specs=[pl.BlockSpec((rows, cols, ch), lambda t: (0, t, 0)), WHOLE, WHOLE],
+        in_specs=[
+            pl.BlockSpec((rows, cols, ch), lambda t: (0, t, 0)),
+            pl.BlockSpec((1, *w.shape[1:]), lambda t: (0, 0, 0, 0)),
+            WHOLE,
+        ],
         out_specs=pl.BlockSpec((share, 2, rows, cols), lambda t: (0, 0, 0, t)),
         out_shape=jax.ShapeDtypeStruct((share, 2, rows, width), BF16),
         compiler_params=params(60),

time: 96.2 us -> 96 us (level)
  no operation moved by 1% of the time
where the time goes in v8:
time: 96 us; the launch traced here: 95.7 us
  blocking collectives  62.7 us (65%)
  starting transfers between devices  13.9 us (14%)
  Pallas kernels  8.77 us (9%)
  waiting for transfers between devices  8.69 us (9%)
  local copies, waits for them, and re-layouts  1.25 us (1%)
    all_to_all x2, blocking collectives, on_device(): product = lax.all_to_all(product, everywhere, 0, 0, tiled=True)  39.7 us
    all_to_all x1, blocking collectives, on_device(): halves = lax.all_to_all(halves, everywhere, 0, 0, tiled=True)  23.1 us
    all_to_all x1, starting transfers between devices, on_device(): halves = lax.all_to_all(halves, 'blk', 0, 0, tiled=True)  9.94 us
    all_to_all x1, waiting for transfers between devices, on_device(): halves = lax.all_to_all(halves, 'blk', 0, 0, tiled=True)  5.42 us
    pallas_call x1, Pallas kernels, project(): pl.pallas_call(project_kernel, grid=(width // cols,), in_specs=[pl.BlockS...  4.23 us
    ppermute x3, starting transfers between devices, gather_chan(): parts.append(lax.ppermute(x, ('blk', 'chan'), pairs))  3.97 us
    ppermute x3, waiting for transfers between devices, gather_chan(): parts.append(lax.ppermute(x, ('blk', 'chan'), pairs))  3.26 us
  transfers between devices with their start and end apart: 4, of which 2 were waited for; matrix products, arithmetic and copies ran while one was open for 1% of the time, Pallas kernels for 1%

profile of v8, /device:TPU:1, one launch (start us, length us, event | category | flops | bytes accessed | tf_op | source)
XLA Modules:
  0.0 95.7 jit_solution(14570690557743654699)
XLA Ops:
  0.0 0.0 copy-start.3
  0.0 0.0 copy-start.4
  0.0 0.0 copy-start.1
  0.0 0.0 copy-start.2
  0.0 4.2 %project_rows.1 = bf16[32,2,16,512]{3,2,1,0:T(8,128)(2,1)} custom-call(bf16[16,512,128]{2,1,0:T(8,128)(2,1)} %x_ref.1, bf16[2,4,32,128]{3,2,1,0:T(8,128)(2,1)} %bitcast.23, f32[2,128]{1,0:T(2,128)} %gain_ref.5), custom_call_target="tpu_custom_call" | custom-call | tf_op jit(solution)/shard_map/project_rows/pallas_call | solution.py:60
  4.3 0.0 copy-start
  4.3 9.9 %all-to-all-start = ((bf16[32,2,16,512]{3,2,1,0:T(8,128)(2,1)}), bf16[32,2,16,512]{3,2,1,0:T(8,128)(2,1)S(1)}, u32[]{:S(2)}, u32[]{:S(2)}) async-start(bf16[32,2,16,512]{3,2,1,0:T(8,128)(2,1)} %project_rows.1), calls=%async_computation | async-start | bytes 2097152 | tf_op jit(solution)/shard_map/all_to_all | solution.py:268
  14.2 0.0 copy-done.3
  14.2 0.0 copy-done.4
  14.2 0.1 multiply_convert_fusion
  14.3 0.0 copy-done.1
  14.3 0.0 copy-done.2
  14.4 1.0 %collective-permute-start.2 = (bf16[6,32,128]{2,1,0:T(8,128)(2,1)S(1)}, bf16[6,32,128]{2,1,0:T(8,128)(2,1)S(1)}, u32[]{:S(2)}, u32[]{:S(2)}) collective-permute-start(bf16[6,32,128]{2,1,0:T(8,128)(2,1)S(1)} %pad_maximum_fusion.1), channel_id=1, source_target_pairs={{0,1},{1,0},{2,3},{3,2},{4,5},{5,4},{6,7},{7,6},{8,9},{9,8},{10,11... | collective-permute-start | bytes 147464 | tf_op jit(solution)/shard_map/ppermute | solution.py:238
  15.4 2.8 %collective-permute-start.1 = (bf16[6,32,128]{2,1,0:T(8,128)(2,1)S(1)}, bf16[6,32,128]{2,1,0:T(8,128)(2,1)S(1)}, u32[]{:S(2)}, u32[]{:S(2)}) collective-permute-start(bf16[6,32,128]{2,1,0:T(8,128)(2,1)S(1)} %pad_maximum_fusion.1), channel_id=1, source_target_pairs={{0,66},{1,67},{2,64},{3,65},{4,70},{5,71},{6,68},{7,69},{8,74},{9,... | collective-permute-start | bytes 147464 | tf_op jit(solution)/shard_map/ppermute | solution.py:238
  18.2 0.1 collective-permute-start
  18.3 1.1 %constant_dynamic-slice_fusion.x_ref = bf16[16,128,128]{2,1,0:T(8,128)(2,1)S(1)} fusion(bf16[16,512,128]{2,1,0:T(8,128)(2,1)} %x_ref.1, s32[]{:T(128)S(6)} %select_n.51), kind=kLoop, calls=%fused_computation.14 | loop fusion | bytes 1048580 | tf_op jit(solution)/shard_map/dynamic_slice | solution.py:265
  19.4 0.0 copy-done
  19.4 0.7 first_gate.1
  20.1 0.0 collective-permute-done.2
  20.1 0.0 collective-permute-done.1
  20.1 3.3 %collective-permute-done = bf16[6,32,128]{2,1,0:T(8,128)(2,1)S(1)} collective-permute-done((bf16[6,32,128]{2,1,0:T(8,128)(2,1)S(1)}, bf16[6,32,128]{2,1,0:T(8,128)(2,1)S(1)}, u32[]{:S(2)}, u32[]{:S(2)}) %collective-permute-start) | collective-permute-done | bytes 49184 | tf_op jit(solution)/shard_map/ppermute | solution.py:238
  23.5 0.2 copy.7
  23.6 5.4 %all-to-all-done.x_ref = bf16[32,2,16,512]{3,2,1,0:T(8,128)(2,1)S(1)} async-done(((bf16[32,2,16,512]{3,2,1,0:T(8,128)(2,1)}), bf16[32,2,16,512]{3,2,1,0:T(8,128)(2,1)S(1)}, u32[]{:S(2)}, u32[]{:S(2)}) %all-to-all-start) | async-done | bytes 1048608 | tf_op jit(solution)/shard_map/all_to_all | solution.py:268
  29.1 0.5 outgoing_product.1
  29.5 21.9 %all_to_all.20.p_ref = bf16[128,16,128]{2,1,0:T(8,128)(2,1)S(1)} all-to-all(bf16[128,16,128]{2,1,0:T(8,128)(2,1)S(1)} %bitcast.19), channel_id=1, replica_groups=mesh['blk'=32,'chan'=4] {'blk','chan'}, dimensions={0} | all-to-all | bytes 1048576 | tf_op jit(solution)/shard_map/all_to_all | solution.py:271
  51.5 1.7 %middle_step.1 = (bf16[128,2048]{1,0:T(8,128)(2,1)S(1)}, f32[128,2048]{1,0:T(8,128)S(1)}, bf16[128,2,16,128]{3,2,1,0:T(8,128)(2,1)S(1)}) custom-call(bf16[128,16,128]{2,1,0:T(8,128)(2,1)S(1)} %all_to_all.20.p_ref, bf16[128,2048]{1,0:T(8,128)(2,1)S(1)} %get-tuple-element.27.pair_ref, f32[128,2048]{1,0:T(8,128)S(1)} %get-tuple-element.28.gate_ref, ...), custom_call_target="tpu_custom_call" | custom-call | tf_op jit(solution)/shard_map/middle_step/pallas_call | solution.py:186
  53.2 23.1 %all_to_all.21 = bf16[128,2,16,128]{3,2,1,0:T(8,128)(2,1)S(1)} all-to-all(bf16[128,2,16,128]{3,2,1,0:T(8,128)(2,1)S(1)} %get-tuple-element.30), channel_id=1, replica_groups=mesh['blk'=32,'chan'=4] {'blk','chan'}, dimensions={0} | all-to-all | bytes 2097152 | tf_op jit(solution)/shard_map/all_to_all | solution.py:273
  76.2 0.5 incoming_product.1
  76.7 17.7 %all_to_all.22.p_ref = bf16[128,16,128]{2,1,0:T(8,128)(2,1)S(1)} all-to-all(bf16[128,16,128]{2,1,0:T(8,128)(2,1)S(1)} %bitcast.20), channel_id=1, replica_groups=mesh['blk'=32,'chan'=4] {'blk','chan'}, dimensions={0} | all-to-all | bytes 1048576 | tf_op jit(solution)/shard_map/all_to_all | solution.py:276
  94.4 1.2 %last_step.1 = bf16[16,128,128]{2,1,0:T(8,128)(2,1)} custom-call(bf16[128,16,128]{2,1,0:T(8,128)(2,1)S(1)} %all_to_all.22.p_ref, bf16[128,2048]{1,0:T(8,128)(2,1)S(1)} %get-tuple-element.31.mid_ref, f32[128,2048]{1,0:T(8,128)S(1)} %get-tuple-element.32.gate_ref, bf16[6,128,128]{2,1,0:T(8,128)(2,1)S(1)} %bitcast.22), custom_call_target="tpu_custom_call" | custom-call | tf_op jit(solution)/shard_map/last_step/pallas_call | solution.py:219
  (5 shorter events, 0.1 us)
Async XLA Ops:
  0.0 14.2 %copy-start.3 = (bf16[2,32,128]{2,1,0:T(8,128)(2,1)S(1)}, bf16[2,32,128]{2,1,0:T(8,128)(2,1)}, u32[]{:S(2)}) copy-start(bf16[2,32,128]{2,1,0:T(8,128)(2,1)} %param.9) | copy-start | bytes 49156
  0.0 14.2 %copy-start.4 = (f32[2,32]{1,0:T(2,128)S(1)}, f32[2,32]{1,0:T(2,128)}, u32[]{:S(2)}) copy-start(f32[2,32]{1,0:T(2,128)} %param.11) | copy-start | bytes 772
  0.0 14.3 %copy-start.1 = (f32[2,128]{1,0:T(2,128)S(1)}, f32[2,128]{1,0:T(2,128)}, u32[]{:S(2)}) copy-start(f32[2,128]{1,0:T(2,128)} %gain_ref.5) | copy-start | bytes 3076
  0.0 14.3 %copy-start.2 = (bf16[2,4,128,32]{2,3,1,0:T(8,128)(2,1)S(1)}, bf16[2,4,128,32]{2,3,1,0:T(8,128)(2,1)}, u32[]{:S(2)}) copy-start(bf16[2,4,128,32]{2,3,1,0:T(8,128)(2,1)} %param.7) | copy-start | bytes 196612
  4.3 15.2 %copy-start = (bf16[2,128,128]{2,1,0:T(8,128)(2,1)S(1)}, bf16[2,128,128]{2,1,0:T(8,128)(2,1)}, u32[]{:S(2)}) copy-start(bf16[2,128,128]{2,1,0:T(8,128)(2,1)} %gw_ref.1) | copy-start | bytes 196612
  4.3 24.8 %all-to-all-start = ((bf16[32,2,16,512]{3,2,1,0:T(8,128)(2,1)}), bf16[32,2,16,512]{3,2,1,0:T(8,128)(2,1)S(1)}, u32[]{:S(2)}, u32[]{:S(2)}) async-start(bf16[32,2,16,512]{3,2,1,0:T(8,128)(2,1)} %project_rows.1), calls=%async_computation | async-start | bytes 2097152 | tf_op jit(solution)/shard_map/all_to_all | solution.py:268
  14.4 5.8 %collective-permute-start.2 = (bf16[6,32,128]{2,1,0:T(8,128)(2,1)S(1)}, bf16[6,32,128]{2,1,0:T(8,128)(2,1)S(1)}, u32[]{:S(2)}, u32[]{:S(2)}) collective-permute-start(bf16[6,32,128]{2,1,0:T(8,128)(2,1)S(1)} %pad_maximum_fusion.1), channel_id=1, source_target_pairs={{0,1},{1,0},{2,3},{3,2},{4,5},{5,4},{6,7},{7,6},{8,9},{9,8},{10,11... | collective-permute-start | bytes 147464 | tf_op jit(solution)/shard_map/ppermute | solution.py:238
  15.4 4.7 %collective-permute-start.1 = (bf16[6,32,128]{2,1,0:T(8,128)(2,1)S(1)}, bf16[6,32,128]{2,1,0:T(8,128)(2,1)S(1)}, u32[]{:S(2)}, u32[]{:S(2)}) collective-permute-start(bf16[6,32,128]{2,1,0:T(8,128)(2,1)S(1)} %pad_maximum_fusion.1), channel_id=1, source_target_pairs={{0,66},{1,67},{2,64},{3,65},{4,70},{5,71},{6,68},{7,69},{8,74},{9,... | collective-permute-start | bytes 147464 | tf_op jit(solution)/shard_map/ppermute | solution.py:238
  18.2 5.2 %collective-permute-start = (bf16[6,32,128]{2,1,0:T(8,128)(2,1)S(1)}, bf16[6,32,128]{2,1,0:T(8,128)(2,1)S(1)}, u32[]{:S(2)}, u32[]{:S(2)}) collective-permute-start(bf16[6,32,128]{2,1,0:T(8,128)(2,1)S(1)} %pad_maximum_fusion.1), channel_id=1, source_target_pairs={{0,67},{1,66},{2,65},{3,64},{4,71},{5,70},{6,69},{7,68},{8,75},{9,... | collective-permute-start | bytes 147464 | tf_op jit(solution)/shard_map/ppermute | solution.py:238

commit v9 on v8

--- a/solution.py
+++ b/solution.py
@@ -125,14 +125,12 @@
 
 def incoming_kernel(x_ref, out_ref):
     blocks, tiles, _, rows, cols = x_ref.shape
-    per = cols // rows
-    rights = [x_ref[:, q, 1].reshape(blocks * rows, cols) for q in range(tiles)]
-    right = jnp.concatenate(rights, axis=1)
-    for p in range(tiles):
-        left = x_ref[:, p, 0].reshape(blocks * rows, cols)
-        product = dot(left, right, 0, 0).astype(BF16)
-        for q in range(tiles):
-            out_ref[p * per : (p + 1) * per, q] = product[:, q * cols : (q + 1) * cols].reshape(per, rows, cols)
+    left, right = (
+        jnp.concatenate([x_ref[:, q, s].reshape(blocks * rows, cols) for q in range(tiles)], 1) for s in range(2)
+    )
+    product = dot(left, right, 0, 0).astype(BF16)
+    for q in range(tiles):
+        out_ref[:, q] = product[:, q * cols : (q + 1) * cols].reshape(blocks, rows, cols)
 
 
 def incoming(x):

time: 96 us -> 96 us (level)
  no operation moved by 1% of the time
where the time goes in v9:
time: 96 us; the launch traced here: 95.7 us
  blocking collectives  62.7 us (65%)
  starting transfers between devices  13.9 us (14%)
  Pallas kernels  8.76 us (9%)
  waiting for transfers between devices  8.69 us (9%)
  local copies, waits for them, and re-layouts  1.25 us (1%)
    all_to_all x2, blocking collectives, on_device(): product = lax.all_to_all(product, everywhere, 0, 0, tiled=True)  39.7 us
    all_to_all x1, blocking collectives, on_device(): halves = lax.all_to_all(halves, everywhere, 0, 0, tiled=True)  23.1 us
    all_to_all x1, starting transfers between devices, on_device(): halves = lax.all_to_all(halves, 'blk', 0, 0, tiled=True)  9.94 us
    all_to_all x1, waiting for transfers between devices, on_device(): halves = lax.all_to_all(halves, 'blk', 0, 0, tiled=True)  5.42 us
    pallas_call x1, Pallas kernels, project(): pl.pallas_call(project_kernel, grid=(width // cols,), in_specs=[pl.BlockS...  4.23 us
    ppermute x3, starting transfers between devices, gather_chan(): parts.append(lax.ppermute(x, ('blk', 'chan'), pairs))  3.97 us
    ppermute x3, waiting for transfers between devices, gather_chan(): parts.append(lax.ppermute(x, ('blk', 'chan'), pairs))  3.26 us
  transfers between devices with their start and end apart: 4, of which 2 were waited for; matrix products, arithmetic and copies ran while one was open for 1% of the time, Pallas kernels for 1%

profile of v9, /device:TPU:1, one launch (start us, length us, event | category | flops | bytes accessed | tf_op | source)
XLA Modules:
  0.0 95.7 jit_solution(7362696183579650865)
XLA Ops:
  0.0 0.0 copy-start.3
  0.0 0.0 copy-start.4
  0.0 0.0 copy-start.1
  0.0 0.0 copy-start.2
  0.0 4.2 %project_rows.1 = bf16[32,2,16,512]{3,2,1,0:T(8,128)(2,1)} custom-call(bf16[16,512,128]{2,1,0:T(8,128)(2,1)} %x_ref.1, bf16[2,4,32,128]{3,2,1,0:T(8,128)(2,1)} %bitcast.23, f32[2,128]{1,0:T(2,128)} %gain_ref.5), custom_call_target="tpu_custom_call" | custom-call | tf_op jit(solution)/shard_map/project_rows/pallas_call | solution.py:60
  4.3 0.0 copy-start
  4.3 9.9 %all-to-all-start = ((bf16[32,2,16,512]{3,2,1,0:T(8,128)(2,1)}), bf16[32,2,16,512]{3,2,1,0:T(8,128)(2,1)S(1)}, u32[]{:S(2)}, u32[]{:S(2)}) async-start(bf16[32,2,16,512]{3,2,1,0:T(8,128)(2,1)} %project_rows.1), calls=%async_computation | async-start | bytes 2097152 | tf_op jit(solution)/shard_map/all_to_all | solution.py:266
  14.2 0.0 copy-done.3
  14.2 0.0 copy-done.4
  14.2 0.1 multiply_convert_fusion
  14.3 0.0 copy-done.1
  14.3 0.0 copy-done.2
  14.4 1.0 %collective-permute-start.2 = (bf16[6,32,128]{2,1,0:T(8,128)(2,1)S(1)}, bf16[6,32,128]{2,1,0:T(8,128)(2,1)S(1)}, u32[]{:S(2)}, u32[]{:S(2)}) collective-permute-start(bf16[6,32,128]{2,1,0:T(8,128)(2,1)S(1)} %pad_maximum_fusion.1), channel_id=1, source_target_pairs={{0,1},{1,0},{2,3},{3,2},{4,5},{5,4},{6,7},{7,6},{8,9},{9,8},{10,11... | collective-permute-start | bytes 147464 | tf_op jit(solution)/shard_map/ppermute | solution.py:236
  15.4 2.8 %collective-permute-start.1 = (bf16[6,32,128]{2,1,0:T(8,128)(2,1)S(1)}, bf16[6,32,128]{2,1,0:T(8,128)(2,1)S(1)}, u32[]{:S(2)}, u32[]{:S(2)}) collective-permute-start(bf16[6,32,128]{2,1,0:T(8,128)(2,1)S(1)} %pad_maximum_fusion.1), channel_id=1, source_target_pairs={{0,66},{1,67},{2,64},{3,65},{4,70},{5,71},{6,68},{7,69},{8,74},{9,... | collective-permute-start | bytes 147464 | tf_op jit(solution)/shard_map/ppermute | solution.py:236
  18.2 0.1 collective-permute-start
  18.3 1.1 %constant_dynamic-slice_fusion.x_ref = bf16[16,128,128]{2,1,0:T(8,128)(2,1)S(1)} fusion(bf16[16,512,128]{2,1,0:T(8,128)(2,1)} %x_ref.1, s32[]{:T(128)S(6)} %select_n.51), kind=kLoop, calls=%fused_computation.14 | loop fusion | bytes 1048580 | tf_op jit(solution)/shard_map/dynamic_slice | solution.py:263
  19.4 0.0 copy-done
  19.4 0.7 first_gate.1
  20.1 0.0 collective-permute-done.2
  20.1 0.0 collective-permute-done.1
  20.1 3.3 %collective-permute-done = bf16[6,32,128]{2,1,0:T(8,128)(2,1)S(1)} collective-permute-done((bf16[6,32,128]{2,1,0:T(8,128)(2,1)S(1)}, bf16[6,32,128]{2,1,0:T(8,128)(2,1)S(1)}, u32[]{:S(2)}, u32[]{:S(2)}) %collective-permute-start) | collective-permute-done | bytes 49184 | tf_op jit(solution)/shard_map/ppermute | solution.py:236
  23.5 0.2 copy.7
  23.6 5.4 %all-to-all-done.x_ref = bf16[32,2,16,512]{3,2,1,0:T(8,128)(2,1)S(1)} async-done(((bf16[32,2,16,512]{3,2,1,0:T(8,128)(2,1)}), bf16[32,2,16,512]{3,2,1,0:T(8,128)(2,1)S(1)}, u32[]{:S(2)}, u32[]{:S(2)}) %all-to-all-start) | async-done | bytes 1048608 | tf_op jit(solution)/shard_map/all_to_all | solution.py:266
  29.1 0.5 outgoing_product.1
  29.5 21.9 %all_to_all.20.p_ref = bf16[128,16,128]{2,1,0:T(8,128)(2,1)S(1)} all-to-all(bf16[128,16,128]{2,1,0:T(8,128)(2,1)S(1)} %bitcast.19), channel_id=1, replica_groups=mesh['blk'=32,'chan'=4] {'blk','chan'}, dimensions={0} | all-to-all | bytes 1048576 | tf_op jit(solution)/shard_map/all_to_all | solution.py:269
  51.5 1.7 %middle_step.1 = (bf16[128,2048]{1,0:T(8,128)(2,1)S(1)}, f32[128,2048]{1,0:T(8,128)S(1)}, bf16[128,2,16,128]{3,2,1,0:T(8,128)(2,1)S(1)}) custom-call(bf16[128,16,128]{2,1,0:T(8,128)(2,1)S(1)} %all_to_all.20.p_ref, bf16[128,2048]{1,0:T(8,128)(2,1)S(1)} %get-tuple-element.27.pair_ref, f32[128,2048]{1,0:T(8,128)S(1)} %get-tuple-element.28.gate_ref, ...), custom_call_target="tpu_custom_call" | custom-call | tf_op jit(solution)/shard_map/middle_step/pallas_call | solution.py:184
  53.2 23.1 %all_to_all.21 = bf16[128,2,16,128]{3,2,1,0:T(8,128)(2,1)S(1)} all-to-all(bf16[128,2,16,128]{3,2,1,0:T(8,128)(2,1)S(1)} %get-tuple-element.30), channel_id=1, replica_groups=mesh['blk'=32,'chan'=4] {'blk','chan'}, dimensions={0} | all-to-all | bytes 2097152 | tf_op jit(solution)/shard_map/all_to_all | solution.py:271
  76.2 0.5 incoming_product.1
  76.7 17.7 %all_to_all.22.p_ref = bf16[128,16,128]{2,1,0:T(8,128)(2,1)S(1)} all-to-all(bf16[128,16,128]{2,1,0:T(8,128)(2,1)S(1)} %bitcast.20), channel_id=1, replica_groups=mesh['blk'=32,'chan'=4] {'blk','chan'}, dimensions={0} | all-to-all | bytes 1048576 | tf_op jit(solution)/shard_map/all_to_all | solution.py:274
  94.4 1.2 %last_step.1 = bf16[16,128,128]{2,1,0:T(8,128)(2,1)} custom-call(bf16[128,16,128]{2,1,0:T(8,128)(2,1)S(1)} %all_to_all.22.p_ref, bf16[128,2048]{1,0:T(8,128)(2,1)S(1)} %get-tuple-element.31.mid_ref, f32[128,2048]{1,0:T(8,128)S(1)} %get-tuple-element.32.gate_ref, bf16[6,128,128]{2,1,0:T(8,128)(2,1)S(1)} %bitcast.22), custom_call_target="tpu_custom_call" | custom-call | tf_op jit(solution)/shard_map/last_step/pallas_call | solution.py:217
  (5 shorter events, 0.1 us)
Async XLA Ops:
  0.0 14.2 %copy-start.3 = (bf16[2,32,128]{2,1,0:T(8,128)(2,1)S(1)}, bf16[2,32,128]{2,1,0:T(8,128)(2,1)}, u32[]{:S(2)}) copy-start(bf16[2,32,128]{2,1,0:T(8,128)(2,1)} %param.9) | copy-start | bytes 49156
  0.0 14.2 %copy-start.4 = (f32[2,32]{1,0:T(2,128)S(1)}, f32[2,32]{1,0:T(2,128)}, u32[]{:S(2)}) copy-start(f32[2,32]{1,0:T(2,128)} %param.11) | copy-start | bytes 772
  0.0 14.3 %copy-start.1 = (f32[2,128]{1,0:T(2,128)S(1)}, f32[2,128]{1,0:T(2,128)}, u32[]{:S(2)}) copy-start(f32[2,128]{1,0:T(2,128)} %gain_ref.5) | copy-start | bytes 3076
  0.0 14.3 %copy-start.2 = (bf16[2,4,128,32]{2,3,1,0:T(8,128)(2,1)S(1)}, bf16[2,4,128,32]{2,3,1,0:T(8,128)(2,1)}, u32[]{:S(2)}) copy-start(bf16[2,4,128,32]{2,3,1,0:T(8,128)(2,1)} %param.7) | copy-start | bytes 196612
  4.3 15.2 %copy-start = (bf16[2,128,128]{2,1,0:T(8,128)(2,1)S(1)}, bf16[2,128,128]{2,1,0:T(8,128)(2,1)}, u32[]{:S(2)}) copy-start(bf16[2,128,128]{2,1,0:T(8,128)(2,1)} %gw_ref.1) | copy-start | bytes 196612
  4.3 24.8 %all-to-all-start = ((bf16[32,2,16,512]{3,2,1,0:T(8,128)(2,1)}), bf16[32,2,16,512]{3,2,1,0:T(8,128)(2,1)S(1)}, u32[]{:S(2)}, u32[]{:S(2)}) async-start(bf16[32,2,16,512]{3,2,1,0:T(8,128)(2,1)} %project_rows.1), calls=%async_computation | async-start | bytes 2097152 | tf_op jit(solution)/shard_map/all_to_all | solution.py:266
  14.4 5.8 %collective-permute-start.2 = (bf16[6,32,128]{2,1,0:T(8,128)(2,1)S(1)}, bf16[6,32,128]{2,1,0:T(8,128)(2,1)S(1)}, u32[]{:S(2)}, u32[]{:S(2)}) collective-permute-start(bf16[6,32,128]{2,1,0:T(8,128)(2,1)S(1)} %pad_maximum_fusion.1), channel_id=1, source_target_pairs={{0,1},{1,0},{2,3},{3,2},{4,5},{5,4},{6,7},{7,6},{8,9},{9,8},{10,11... | collective-permute-start | bytes 147464 | tf_op jit(solution)/shard_map/ppermute | solution.py:236
  15.4 4.7 %collective-permute-start.1 = (bf16[6,32,128]{2,1,0:T(8,128)(2,1)S(1)}, bf16[6,32,128]{2,1,0:T(8,128)(2,1)S(1)}, u32[]{:S(2)}, u32[]{:S(2)}) collective-permute-start(bf16[6,32,128]{2,1,0:T(8,128)(2,1)S(1)} %pad_maximum_fusion.1), channel_id=1, source_target_pairs={{0,66},{1,67},{2,64},{3,65},{4,70},{5,71},{6,68},{7,69},{8,74},{9,... | collective-permute-start | bytes 147464 | tf_op jit(solution)/shard_map/ppermute | solution.py:236
  18.2 5.2 %collective-permute-start = (bf16[6,32,128]{2,1,0:T(8,128)(2,1)S(1)}, bf16[6,32,128]{2,1,0:T(8,128)(2,1)S(1)}, u32[]{:S(2)}, u32[]{:S(2)}) collective-permute-start(bf16[6,32,128]{2,1,0:T(8,128)(2,1)S(1)} %pad_maximum_fusion.1), channel_id=1, source_target_pairs={{0,67},{1,66},{2,65},{3,64},{4,71},{5,70},{6,69},{7,68},{8,75},{9,... | collective-permute-start | bytes 147464 | tf_op jit(solution)/shard_map/ppermute | solution.py:236

commit v10 on v9

--- a/solution.py
+++ b/solution.py
@@ -201,10 +201,10 @@
     copies = []
     for g in range(parts):
         group = slice(g * per, (g + 1) * per)
-        for i in range(g * per, (g + 1) * per):
-            lanes = slice(i * cols, (i + 1) * cols)
-            out = mid_ref[:, lanes].astype(F32) + gate_ref[:, lanes] * updates[i]
-            buffer[i] = out.astype(BF16).T
+        lanes = slice(g * per * cols, (g + 1) * per * cols)
+        update = jnp.concatenate(updates[group], 1)
+        out = mid_ref[:, lanes].astype(F32) + gate_ref[:, lanes] * update
+        buffer[group] = out.astype(BF16).T.reshape(per, cols, out.shape[0])
         copies.append(pltpu.make_async_copy(buffer.at[group], out_hbm.at[group], sem.at[g]))
         copies[-1].start()
     for copy in copies:

time: 96 us -> 96 us (level)
  no operation moved by 1% of the time
where the time goes in v10:
time: 96 us; the launch traced here: 95.7 us
  blocking collectives  62.7 us (65%)
  starting transfers between devices  13.9 us (14%)
  Pallas kernels  8.76 us (9%)
  waiting for transfers between devices  8.69 us (9%)
  local copies, waits for them, and re-layouts  1.25 us (1%)
    all_to_all x2, blocking collectives, on_device(): product = lax.all_to_all(product, everywhere, 0, 0, tiled=True)  39.7 us
    all_to_all x1, blocking collectives, on_device(): halves = lax.all_to_all(halves, everywhere, 0, 0, tiled=True)  23.1 us
    all_to_all x1, starting transfers between devices, on_device(): halves = lax.all_to_all(halves, 'blk', 0, 0, tiled=True)  9.94 us
    all_to_all x1, waiting for transfers between devices, on_device(): halves = lax.all_to_all(halves, 'blk', 0, 0, tiled=True)  5.42 us
    pallas_call x1, Pallas kernels, project(): pl.pallas_call(project_kernel, grid=(width // cols,), in_specs=[pl.BlockS...  4.23 us
    ppermute x3, starting transfers between devices, gather_chan(): parts.append(lax.ppermute(x, ('blk', 'chan'), pairs))  3.97 us
    ppermute x3, waiting for transfers between devices, gather_chan(): parts.append(lax.ppermute(x, ('blk', 'chan'), pairs))  3.26 us
  transfers between devices with their start and end apart: 4, of which 2 were waited for; matrix products, arithmetic and copies ran while one was open for 1% of the time, Pallas kernels for 1%

profile of v10, /device:TPU:1, one launch (start us, length us, event | category | flops | bytes accessed | tf_op | source)
XLA Modules:
  0.0 95.7 jit_solution(5045619062399894786)
XLA Ops:
  0.0 0.0 copy-start.3
  0.0 0.0 copy-start.4
  0.0 0.0 copy-start.1
  0.0 0.0 copy-start.2
  0.0 4.2 %project_rows.1 = bf16[32,2,16,512]{3,2,1,0:T(8,128)(2,1)} custom-call(bf16[16,512,128]{2,1,0:T(8,128)(2,1)} %x_ref.1, bf16[2,4,32,128]{3,2,1,0:T(8,128)(2,1)} %bitcast.23, f32[2,128]{1,0:T(2,128)} %gain_ref.5), custom_call_target="tpu_custom_call" | custom-call | tf_op jit(solution)/shard_map/project_rows/pallas_call | solution.py:60
  4.3 0.0 copy-start
  4.3 9.9 %all-to-all-start = ((bf16[32,2,16,512]{3,2,1,0:T(8,128)(2,1)}), bf16[32,2,16,512]{3,2,1,0:T(8,128)(2,1)S(1)}, u32[]{:S(2)}, u32[]{:S(2)}) async-start(bf16[32,2,16,512]{3,2,1,0:T(8,128)(2,1)} %project_rows.1), calls=%async_computation | async-start | bytes 2097152 | tf_op jit(solution)/shard_map/all_to_all | solution.py:266
  14.2 0.0 copy-done.3
  14.2 0.0 copy-done.4
  14.2 0.1 multiply_convert_fusion
  14.3 0.0 copy-done.1
  14.3 0.0 copy-done.2
  14.4 1.0 %collective-permute-start.2 = (bf16[6,32,128]{2,1,0:T(8,128)(2,1)S(1)}, bf16[6,32,128]{2,1,0:T(8,128)(2,1)S(1)}, u32[]{:S(2)}, u32[]{:S(2)}) collective-permute-start(bf16[6,32,128]{2,1,0:T(8,128)(2,1)S(1)} %pad_maximum_fusion.1), channel_id=1, source_target_pairs={{0,1},{1,0},{2,3},{3,2},{4,5},{5,4},{6,7},{7,6},{8,9},{9,8},{10,11... | collective-permute-start | bytes 147464 | tf_op jit(solution)/shard_map/ppermute | solution.py:236
  15.4 2.8 %collective-permute-start.1 = (bf16[6,32,128]{2,1,0:T(8,128)(2,1)S(1)}, bf16[6,32,128]{2,1,0:T(8,128)(2,1)S(1)}, u32[]{:S(2)}, u32[]{:S(2)}) collective-permute-start(bf16[6,32,128]{2,1,0:T(8,128)(2,1)S(1)} %pad_maximum_fusion.1), channel_id=1, source_target_pairs={{0,66},{1,67},{2,64},{3,65},{4,70},{5,71},{6,68},{7,69},{8,74},{9,... | collective-permute-start | bytes 147464 | tf_op jit(solution)/shard_map/ppermute | solution.py:236
  18.2 0.1 collective-permute-start
  18.3 1.1 %constant_dynamic-slice_fusion.x_ref = bf16[16,128,128]{2,1,0:T(8,128)(2,1)S(1)} fusion(bf16[16,512,128]{2,1,0:T(8,128)(2,1)} %x_ref.1, s32[]{:T(128)S(6)} %select_n.51), kind=kLoop, calls=%fused_computation.14 | loop fusion | bytes 1048580 | tf_op jit(solution)/shard_map/dynamic_slice | solution.py:263
  19.4 0.0 copy-done
  19.4 0.7 first_gate.1
  20.1 0.0 collective-permute-done.2
  20.1 0.0 collective-permute-done.1
  20.1 3.3 %collective-permute-done = bf16[6,32,128]{2,1,0:T(8,128)(2,1)S(1)} collective-permute-done((bf16[6,32,128]{2,1,0:T(8,128)(2,1)S(1)}, bf16[6,32,128]{2,1,0:T(8,128)(2,1)S(1)}, u32[]{:S(2)}, u32[]{:S(2)}) %collective-permute-start) | collective-permute-done | bytes 49184 | tf_op jit(solution)/shard_map/ppermute | solution.py:236
  23.5 0.2 copy.7
  23.6 5.4 %all-to-all-done.x_ref = bf16[32,2,16,512]{3,2,1,0:T(8,128)(2,1)S(1)} async-done(((bf16[32,2,16,512]{3,2,1,0:T(8,128)(2,1)}), bf16[32,2,16,512]{3,2,1,0:T(8,128)(2,1)S(1)}, u32[]{:S(2)}, u32[]{:S(2)}) %all-to-all-start) | async-done | bytes 1048608 | tf_op jit(solution)/shard_map/all_to_all | solution.py:266
  29.1 0.5 outgoing_product.1
  29.5 21.9 %all_to_all.20.p_ref = bf16[128,16,128]{2,1,0:T(8,128)(2,1)S(1)} all-to-all(bf16[128,16,128]{2,1,0:T(8,128)(2,1)S(1)} %bitcast.19), channel_id=1, replica_groups=mesh['blk'=32,'chan'=4] {'blk','chan'}, dimensions={0} | all-to-all | bytes 1048576 | tf_op jit(solution)/shard_map/all_to_all | solution.py:269
  51.5 1.7 %middle_step.1 = (bf16[128,2048]{1,0:T(8,128)(2,1)S(1)}, f32[128,2048]{1,0:T(8,128)S(1)}, bf16[128,2,16,128]{3,2,1,0:T(8,128)(2,1)S(1)}) custom-call(bf16[128,16,128]{2,1,0:T(8,128)(2,1)S(1)} %all_to_all.20.p_ref, bf16[128,2048]{1,0:T(8,128)(2,1)S(1)} %get-tuple-element.27.pair_ref, f32[128,2048]{1,0:T(8,128)S(1)} %get-tuple-element.28.gate_ref, ...), custom_call_target="tpu_custom_call" | custom-call | tf_op jit(solution)/shard_map/middle_step/pallas_call | solution.py:184
  53.2 23.1 %all_to_all.21 = bf16[128,2,16,128]{3,2,1,0:T(8,128)(2,1)S(1)} all-to-all(bf16[128,2,16,128]{3,2,1,0:T(8,128)(2,1)S(1)} %get-tuple-element.30), channel_id=1, replica_groups=mesh['blk'=32,'chan'=4] {'blk','chan'}, dimensions={0} | all-to-all | bytes 2097152 | tf_op jit(solution)/shard_map/all_to_all | solution.py:271
  76.2 0.5 incoming_product.1
  76.7 17.7 %all_to_all.22.p_ref = bf16[128,16,128]{2,1,0:T(8,128)(2,1)S(1)} all-to-all(bf16[128,16,128]{2,1,0:T(8,128)(2,1)S(1)} %bitcast.20), channel_id=1, replica_groups=mesh['blk'=32,'chan'=4] {'blk','chan'}, dimensions={0} | all-to-all | bytes 1048576 | tf_op jit(solution)/shard_map/all_to_all | solution.py:274
  94.4 1.2 %last_step.1 = bf16[16,128,128]{2,1,0:T(8,128)(2,1)} custom-call(bf16[128,16,128]{2,1,0:T(8,128)(2,1)S(1)} %all_to_all.22.p_ref, bf16[128,2048]{1,0:T(8,128)(2,1)S(1)} %get-tuple-element.31.mid_ref, f32[128,2048]{1,0:T(8,128)S(1)} %get-tuple-element.32.gate_ref, bf16[6,128,128]{2,1,0:T(8,128)(2,1)S(1)} %bitcast.22), custom_call_target="tpu_custom_call" | custom-call | tf_op jit(solution)/shard_map/last_step/pallas_call | solution.py:217
  (5 shorter events, 0.1 us)
Async XLA Ops:
  0.0 14.2 %copy-start.3 = (bf16[2,32,128]{2,1,0:T(8,128)(2,1)S(1)}, bf16[2,32,128]{2,1,0:T(8,128)(2,1)}, u32[]{:S(2)}) copy-start(bf16[2,32,128]{2,1,0:T(8,128)(2,1)} %param.9) | copy-start | bytes 49156
  0.0 14.2 %copy-start.4 = (f32[2,32]{1,0:T(2,128)S(1)}, f32[2,32]{1,0:T(2,128)}, u32[]{:S(2)}) copy-start(f32[2,32]{1,0:T(2,128)} %param.11) | copy-start | bytes 772
  0.0 14.3 %copy-start.1 = (f32[2,128]{1,0:T(2,128)S(1)}, f32[2,128]{1,0:T(2,128)}, u32[]{:S(2)}) copy-start(f32[2,128]{1,0:T(2,128)} %gain_ref.5) | copy-start | bytes 3076
  0.0 14.3 %copy-start.2 = (bf16[2,4,128,32]{2,3,1,0:T(8,128)(2,1)S(1)}, bf16[2,4,128,32]{2,3,1,0:T(8,128)(2,1)}, u32[]{:S(2)}) copy-start(bf16[2,4,128,32]{2,3,1,0:T(8,128)(2,1)} %param.7) | copy-start | bytes 196612
  4.3 15.2 %copy-start = (bf16[2,128,128]{2,1,0:T(8,128)(2,1)S(1)}, bf16[2,128,128]{2,1,0:T(8,128)(2,1)}, u32[]{:S(2)}) copy-start(bf16[2,128,128]{2,1,0:T(8,128)(2,1)} %gw_ref.1) | copy-start | bytes 196612
  4.3 24.8 %all-to-all-start = ((bf16[32,2,16,512]{3,2,1,0:T(8,128)(2,1)}), bf16[32,2,16,512]{3,2,1,0:T(8,128)(2,1)S(1)}, u32[]{:S(2)}, u32[]{:S(2)}) async-start(bf16[32,2,16,512]{3,2,1,0:T(8,128)(2,1)} %project_rows.1), calls=%async_computation | async-start | bytes 2097152 | tf_op jit(solution)/shard_map/all_to_all | solution.py:266
  14.4 5.8 %collective-permute-start.2 = (bf16[6,32,128]{2,1,0:T(8,128)(2,1)S(1)}, bf16[6,32,128]{2,1,0:T(8,128)(2,1)S(1)}, u32[]{:S(2)}, u32[]{:S(2)}) collective-permute-start(bf16[6,32,128]{2,1,0:T(8,128)(2,1)S(1)} %pad_maximum_fusion.1), channel_id=1, source_target_pairs={{0,1},{1,0},{2,3},{3,2},{4,5},{5,4},{6,7},{7,6},{8,9},{9,8},{10,11... | collective-permute-start | bytes 147464 | tf_op jit(solution)/shard_map/ppermute | solution.py:236
  15.4 4.7 %collective-permute-start.1 = (bf16[6,32,128]{2,1,0:T(8,128)(2,1)S(1)}, bf16[6,32,128]{2,1,0:T(8,128)(2,1)S(1)}, u32[]{:S(2)}, u32[]{:S(2)}) collective-permute-start(bf16[6,32,128]{2,1,0:T(8,128)(2,1)S(1)} %pad_maximum_fusion.1), channel_id=1, source_target_pairs={{0,66},{1,67},{2,64},{3,65},{4,70},{5,71},{6,68},{7,69},{8,74},{9,... | collective-permute-start | bytes 147464 | tf_op jit(solution)/shard_map/ppermute | solution.py:236
  18.2 5.2 %collective-permute-start = (bf16[6,32,128]{2,1,0:T(8,128)(2,1)S(1)}, bf16[6,32,128]{2,1,0:T(8,128)(2,1)S(1)}, u32[]{:S(2)}, u32[]{:S(2)}) collective-permute-start(bf16[6,32,128]{2,1,0:T(8,128)(2,1)S(1)} %pad_maximum_fusion.1), channel_id=1, source_target_pairs={{0,67},{1,66},{2,65},{3,64},{4,71},{5,70},{6,69},{7,68},{8,75},{9,... | collective-permute-start | bytes 147464 | tf_op jit(solution)/shard_map/ppermute | solution.py:236

commit v11 on v9

--- a/solution.py
+++ b/solution.py
@@ -176,7 +176,7 @@
         value = parts[2 * s * ch : (2 * s + 1) * ch]
         gate = jnp.tanh(parts[(2 * s + 1) * ch : (2 * s + 2) * ch])
         out_ref[:, s] = stacked((value + value * gate).astype(BF16), rows)
-    gate2_ref[...] = gate_of(normed, gw_ref, gain_ref, 1)
+    gate2_ref[...] = gate_of(normed, gw_ref, gain_ref, 1).astype(BF16)
 
 
 def middle_step(p, pair, gate, whole, gate_weight, in_gain):
@@ -185,7 +185,7 @@
         middle_kernel,
         out_shape=(
             jax.ShapeDtypeStruct(pair.shape, BF16),
-            jax.ShapeDtypeStruct(pair.shape, F32),
+            jax.ShapeDtypeStruct(pair.shape, BF16),
             jax.ShapeDtypeStruct((ch, 2, rows, cols), BF16),
         ),
         compiler_params=params(32),
@@ -203,7 +203,7 @@
         group = slice(g * per, (g + 1) * per)
         for i in range(g * per, (g + 1) * per):
             lanes = slice(i * cols, (i + 1) * cols)
-            out = mid_ref[:, lanes].astype(F32) + gate_ref[:, lanes] * updates[i]
+            out = mid_ref[:, lanes].astype(F32) + gate_ref[:, lanes].astype(F32) * updates[i]
             buffer[i] = out.astype(BF16).T
         copies.append(pltpu.make_async_copy(buffer.at[group], out_hbm.at[group], sem.at[g]))
         copies[-1].start()

time: 96 us -> 96.1 us (level)
  no operation moved by 1% of the time
where the time goes in v11:
time: 96.1 us; the launch traced here: 95.7 us
  blocking collectives  62.7 us (65%)
  starting transfers between devices  13.9 us (14%)
  Pallas kernels  8.79 us (9%)
  waiting for transfers between devices  8.69 us (9%)
  local copies, waits for them, and re-layouts  1.25 us (1%)
    all_to_all x2, blocking collectives, on_device(): product = lax.all_to_all(product, everywhere, 0, 0, tiled=True)  39.7 us
    all_to_all x1, blocking collectives, on_device(): halves = lax.all_to_all(halves, everywhere, 0, 0, tiled=True)  23.1 us
    all_to_all x1, starting transfers between devices, on_device(): halves = lax.all_to_all(halves, 'blk', 0, 0, tiled=True)  9.94 us
    all_to_all x1, waiting for transfers between devices, on_device(): halves = lax.all_to_all(halves, 'blk', 0, 0, tiled=True)  5.42 us
    pallas_call x1, Pallas kernels, project(): pl.pallas_call(project_kernel, grid=(width // cols,), in_specs=[pl.BlockS...  4.23 us
    ppermute x3, starting transfers between devices, gather_chan(): parts.append(lax.ppermute(x, ('blk', 'chan'), pairs))  3.97 us
    ppermute x3, waiting for transfers between devices, gather_chan(): parts.append(lax.ppermute(x, ('blk', 'chan'), pairs))  3.26 us
  transfers between devices with their start and end apart: 4, of which 2 were waited for; matrix products, arithmetic and copies ran while one was open for 1% of the time, Pallas kernels for 1%

profile of v11, /device:TPU:1, one launch (start us, length us, event | category | flops | bytes accessed | tf_op | source)
XLA Modules:
  0.0 95.7 jit_solution(7909472040568000431)
XLA Ops:
  0.0 0.0 copy-start.3
  0.0 0.0 copy-start.4
  0.0 0.0 copy-start.1
  0.0 0.0 copy-start.2
  0.0 4.2 %project_rows.1 = bf16[32,2,16,512]{3,2,1,0:T(8,128)(2,1)} custom-call(bf16[16,512,128]{2,1,0:T(8,128)(2,1)} %x_ref.1, bf16[2,4,32,128]{3,2,1,0:T(8,128)(2,1)} %bitcast.23, f32[2,128]{1,0:T(2,128)} %gain_ref.5), custom_call_target="tpu_custom_call" | custom-call | tf_op jit(solution)/shard_map/project_rows/pallas_call | solution.py:60
  4.3 0.0 copy-start
  4.3 9.9 %all-to-all-start = ((bf16[32,2,16,512]{3,2,1,0:T(8,128)(2,1)}), bf16[32,2,16,512]{3,2,1,0:T(8,128)(2,1)S(1)}, u32[]{:S(2)}, u32[]{:S(2)}) async-start(bf16[32,2,16,512]{3,2,1,0:T(8,128)(2,1)} %project_rows.1), calls=%async_computation | async-start | bytes 2097152 | tf_op jit(solution)/shard_map/all_to_all | solution.py:266
  14.2 0.0 copy-done.3
  14.2 0.0 copy-done.4
  14.2 0.1 multiply_convert_fusion
  14.3 0.0 copy-done.1
  14.3 0.0 copy-done.2
  14.4 1.0 %collective-permute-start.2 = (bf16[6,32,128]{2,1,0:T(8,128)(2,1)S(1)}, bf16[6,32,128]{2,1,0:T(8,128)(2,1)S(1)}, u32[]{:S(2)}, u32[]{:S(2)}) collective-permute-start(bf16[6,32,128]{2,1,0:T(8,128)(2,1)S(1)} %pad_maximum_fusion.1), channel_id=1, source_target_pairs={{0,1},{1,0},{2,3},{3,2},{4,5},{5,4},{6,7},{7,6},{8,9},{9,8},{10,11... | collective-permute-start | bytes 147464 | tf_op jit(solution)/shard_map/ppermute | solution.py:236
  15.4 2.8 %collective-permute-start.1 = (bf16[6,32,128]{2,1,0:T(8,128)(2,1)S(1)}, bf16[6,32,128]{2,1,0:T(8,128)(2,1)S(1)}, u32[]{:S(2)}, u32[]{:S(2)}) collective-permute-start(bf16[6,32,128]{2,1,0:T(8,128)(2,1)S(1)} %pad_maximum_fusion.1), channel_id=1, source_target_pairs={{0,66},{1,67},{2,64},{3,65},{4,70},{5,71},{6,68},{7,69},{8,74},{9,... | collective-permute-start | bytes 147464 | tf_op jit(solution)/shard_map/ppermute | solution.py:236
  18.2 0.1 collective-permute-start
  18.3 1.1 %constant_dynamic-slice_fusion.x_ref = bf16[16,128,128]{2,1,0:T(8,128)(2,1)S(1)} fusion(bf16[16,512,128]{2,1,0:T(8,128)(2,1)} %x_ref.1, s32[]{:T(128)S(6)} %select_n.51), kind=kLoop, calls=%fused_computation.14 | loop fusion | bytes 1048580 | tf_op jit(solution)/shard_map/dynamic_slice | solution.py:263
  19.4 0.0 copy-done
  19.4 0.7 first_gate.1
  20.1 0.0 collective-permute-done.2
  20.1 0.0 collective-permute-done.1
  20.1 3.3 %collective-permute-done = bf16[6,32,128]{2,1,0:T(8,128)(2,1)S(1)} collective-permute-done((bf16[6,32,128]{2,1,0:T(8,128)(2,1)S(1)}, bf16[6,32,128]{2,1,0:T(8,128)(2,1)S(1)}, u32[]{:S(2)}, u32[]{:S(2)}) %collective-permute-start) | collective-permute-done | bytes 49184 | tf_op jit(solution)/shard_map/ppermute | solution.py:236
  23.5 0.2 copy.7
  23.6 5.4 %all-to-all-done.x_ref = bf16[32,2,16,512]{3,2,1,0:T(8,128)(2,1)S(1)} async-done(((bf16[32,2,16,512]{3,2,1,0:T(8,128)(2,1)}), bf16[32,2,16,512]{3,2,1,0:T(8,128)(2,1)S(1)}, u32[]{:S(2)}, u32[]{:S(2)}) %all-to-all-start) | async-done | bytes 1048608 | tf_op jit(solution)/shard_map/all_to_all | solution.py:266
  29.1 0.5 outgoing_product.1
  29.5 21.9 %all_to_all.20.p_ref = bf16[128,16,128]{2,1,0:T(8,128)(2,1)S(1)} all-to-all(bf16[128,16,128]{2,1,0:T(8,128)(2,1)S(1)} %bitcast.19), channel_id=1, replica_groups=mesh['blk'=32,'chan'=4] {'blk','chan'}, dimensions={0} | all-to-all | bytes 1048576 | tf_op jit(solution)/shard_map/all_to_all | solution.py:269
  51.5 1.7 %middle_step.1 = (bf16[128,2048]{1,0:T(8,128)(2,1)S(1)}, bf16[128,2048]{1,0:T(8,128)(2,1)S(1)}, bf16[128,2,16,128]{3,2,1,0:T(8,128)(2,1)S(1)}) custom-call(bf16[128,16,128]{2,1,0:T(8,128)(2,1)S(1)} %all_to_all.20.p_ref, bf16[128,2048]{1,0:T(8,128)(2,1)S(1)} %get-tuple-element.27.pair_ref, f32[128,2048]{1,0:T(8,128)S(1)} %get-tuple-element.28.gate_ref, ...), custom_call_target="tpu_custom_call" | custom-call | tf_op jit(solution)/shard_map/middle_step/pallas_call | solution.py:184
  53.2 23.1 %all_to_all.21 = bf16[128,2,16,128]{3,2,1,0:T(8,128)(2,1)S(1)} all-to-all(bf16[128,2,16,128]{3,2,1,0:T(8,128)(2,1)S(1)} %get-tuple-element.30), channel_id=1, replica_groups=mesh['blk'=32,'chan'=4] {'blk','chan'}, dimensions={0} | all-to-all | bytes 2097152 | tf_op jit(solution)/shard_map/all_to_all | solution.py:271
  76.2 0.5 incoming_product.1
  76.7 17.7 %all_to_all.22.p_ref = bf16[128,16,128]{2,1,0:T(8,128)(2,1)S(1)} all-to-all(bf16[128,16,128]{2,1,0:T(8,128)(2,1)S(1)} %bitcast.20), channel_id=1, replica_groups=mesh['blk'=32,'chan'=4] {'blk','chan'}, dimensions={0} | all-to-all | bytes 1048576 | tf_op jit(solution)/shard_map/all_to_all | solution.py:274
  94.4 1.3 %last_step.1 = bf16[16,128,128]{2,1,0:T(8,128)(2,1)} custom-call(bf16[128,16,128]{2,1,0:T(8,128)(2,1)S(1)} %all_to_all.22.p_ref, bf16[128,2048]{1,0:T(8,128)(2,1)S(1)} %get-tuple-element.31.mid_ref, bf16[128,2048]{1,0:T(8,128)(2,1)S(1)} %get-tuple-element.32.gate_ref, bf16[6,128,128]{2,1,0:T(8,128)(2,1)S(1)} %bitcast.22), custom_call_target="tpu_custom_call" | custom-call | tf_op jit(solution)/shard_map/last_step/pallas_call | solution.py:217
  (5 shorter events, 0.1 us)
Async XLA Ops:
  0.0 14.2 %copy-start.3 = (bf16[2,32,128]{2,1,0:T(8,128)(2,1)S(1)}, bf16[2,32,128]{2,1,0:T(8,128)(2,1)}, u32[]{:S(2)}) copy-start(bf16[2,32,128]{2,1,0:T(8,128)(2,1)} %param.9) | copy-start | bytes 49156
  0.0 14.2 %copy-start.4 = (f32[2,32]{1,0:T(2,128)S(1)}, f32[2,32]{1,0:T(2,128)}, u32[]{:S(2)}) copy-start(f32[2,32]{1,0:T(2,128)} %param.11) | copy-start | bytes 772
  0.0 14.3 %copy-start.1 = (f32[2,128]{1,0:T(2,128)S(1)}, f32[2,128]{1,0:T(2,128)}, u32[]{:S(2)}) copy-start(f32[2,128]{1,0:T(2,128)} %gain_ref.5) | copy-start | bytes 3076
  0.0 14.3 %copy-start.2 = (bf16[2,4,128,32]{2,3,1,0:T(8,128)(2,1)S(1)}, bf16[2,4,128,32]{2,3,1,0:T(8,128)(2,1)}, u32[]{:S(2)}) copy-start(bf16[2,4,128,32]{2,3,1,0:T(8,128)(2,1)} %param.7) | copy-start | bytes 196612
  4.3 15.2 %copy-start = (bf16[2,128,128]{2,1,0:T(8,128)(2,1)S(1)}, bf16[2,128,128]{2,1,0:T(8,128)(2,1)}, u32[]{:S(2)}) copy-start(bf16[2,128,128]{2,1,0:T(8,128)(2,1)} %gw_ref.1) | copy-start | bytes 196612
  4.3 24.8 %all-to-all-start = ((bf16[32,2,16,512]{3,2,1,0:T(8,128)(2,1)}), bf16[32,2,16,512]{3,2,1,0:T(8,128)(2,1)S(1)}, u32[]{:S(2)}, u32[]{:S(2)}) async-start(bf16[32,2,16,512]{3,2,1,0:T(8,128)(2,1)} %project_rows.1), calls=%async_computation | async-start | bytes 2097152 | tf_op jit(solution)/shard_map/all_to_all | solution.py:266
  14.4 5.8 %collective-permute-start.2 = (bf16[6,32,128]{2,1,0:T(8,128)(2,1)S(1)}, bf16[6,32,128]{2,1,0:T(8,128)(2,1)S(1)}, u32[]{:S(2)}, u32[]{:S(2)}) collective-permute-start(bf16[6,32,128]{2,1,0:T(8,128)(2,1)S(1)} %pad_maximum_fusion.1), channel_id=1, source_target_pairs={{0,1},{1,0},{2,3},{3,2},{4,5},{5,4},{6,7},{7,6},{8,9},{9,8},{10,11... | collective-permute-start | bytes 147464 | tf_op jit(solution)/shard_map/ppermute | solution.py:236
  15.4 4.7 %collective-permute-start.1 = (bf16[6,32,128]{2,1,0:T(8,128)(2,1)S(1)}, bf16[6,32,128]{2,1,0:T(8,128)(2,1)S(1)}, u32[]{:S(2)}, u32[]{:S(2)}) collective-permute-start(bf16[6,32,128]{2,1,0:T(8,128)(2,1)S(1)} %pad_maximum_fusion.1), channel_id=1, source_target_pairs={{0,66},{1,67},{2,64},{3,65},{4,70},{5,71},{6,68},{7,69},{8,74},{9,... | collective-permute-start | bytes 147464 | tf_op jit(solution)/shard_map/ppermute | solution.py:236
  18.2 5.2 %collective-permute-start = (bf16[6,32,128]{2,1,0:T(8,128)(2,1)S(1)}, bf16[6,32,128]{2,1,0:T(8,128)(2,1)S(1)}, u32[]{:S(2)}, u32[]{:S(2)}) collective-permute-start(bf16[6,32,128]{2,1,0:T(8,128)(2,1)S(1)} %pad_maximum_fusion.1), channel_id=1, source_target_pairs={{0,67},{1,66},{2,65},{3,64},{4,71},{5,70},{6,69},{7,68},{8,75},{9,... | collective-permute-start | bytes 147464 | tf_op jit(solution)/shard_map/ppermute | solution.py:236
